TPU v7x, 32 devices: a whole 2x2x4 slice. The times are simulated.
32 devices in a mesh: prow: 8 (over z, x), pcol: 2 (over y), zgrid: 2 (over core).
Axes of the slice: x: 2, y: 2, z: 4, core: 2. Of those that a mesh axis runs over, the one named last changes fastest.
Arguments:
- blocks: bfloat16 [8, 2, 2, 3, 40, 128, 128], P('prow', 'pcol', 'zgrid'), may hold values from -0.078125 to 0.078125
- sources: int32 [8, 2, 2, 3, 40], P('prow', 'pcol', 'zgrid'), may hold values from 0 to 1, as said below
- targets: int32 [8, 2, 2, 3, 40], P('prow', 'pcol', 'zgrid'), may hold values from 0 to 23, as said below
- counts: int32 [8, 2, 2, 3], P('prow', 'pcol', 'zgrid'), may hold values from 1 to 40, as said below
- given_sub: bfloat16 [8, 2, 2, 2, 128, 128], P('prow', 'pcol', 'zgrid'), may hold values from -6 to 6
- given_top: bfloat16 [8, 2, 2, 128, 128], P('prow', 'pcol'), may hold values from -6 to 6
- inverse_sub: bfloat16 [8, 2, 2, 2, 128, 128], P('prow', 'pcol', 'zgrid'), as said below
- inverse_top: bfloat16 [8, 2, 2, 128, 128], P('prow', 'pcol'), as said below
Outputs:
- solved_sub: bfloat16 [8, 2, 2, 2, 128, 128], P('prow', 'pcol', 'zgrid')
- solved_top: bfloat16 [8, 2, 2, 128, 128], P('prow', 'pcol')
Inputs may be any that keep to these rules, and one draw needn't show every extreme that they name: `sources`: column of the source supernode of a slot. `targets`: a slot of source level l aims at a level t = value // 8 + 1 above l and the row value % 8. `counts`: on some device of each source level all 40 slots are live. `inverse_sub`: unit lower triangular. `inverse_top`: unit lower triangular.
All inputs are finite; a program needn't handle non-finite values.
Results may differ from a plain program's by a relative error of at most 0.023.
Values may be sent and summed in bfloat16 or wider, within the bound.
No kernel may reach another device: no remote copies, remote signals or barrier semaphores. Data moves between devices by JAX's collectives and lax.ppermute only.
A program may use at most 64 MiB of HBM per device.

v0:
```python
import functools

import jax
import jax.numpy as jnp
from jax import lax
from jax.experimental import pallas as pl
from jax.experimental.pallas import tpu as pltpu
from jax.sharding import PartitionSpec as P

slot_group = 8
batch = 4
field = 10
field_mask = (1 << field) - 1
pairs = ((0, 1), (0, 2), (0, 3), (1, 2), (1, 3), (2, 3), (2, 3))
count_row = len(pairs)
params = pltpu.CompilerParams(vmem_limit_bytes=24 * 1024 * 1024)
vmem = pl.BlockSpec(memory_space=pltpu.VMEM)
smem = pl.BlockSpec(memory_space=pltpu.SMEM)
hbm = pl.BlockSpec(memory_space=pltpu.HBM)
anywhere = pl.BlockSpec(memory_space=pl.ANY)


def sibling_values(value, layers):
    cols = lax.axis_size("pcol")
    depth = lax.axis_size("zgrid")
    found = []
    for k in range(cols):
        if k == 0 and layers == 0:
            found.append(value)
            continue
        moves = []
        for c in range(cols):
            for z in range(depth):
                target = ((c - k) % cols) * depth + (z - layers) % depth
                moves.append((c * depth + z, target))
        found.append(lax.ppermute(value, ("pcol", "zgrid"), moves))
    return found


def from_other_core(value):
    return lax.ppermute(value, "zgrid", [(0, 1), (1, 0)])


def in_hbm(value):
    return pltpu.with_memory_space_constraint(value, pltpu.HBM)


def plan_kernel(row_count, cols, sources_in, targets_in, counts_in, blocks, plan, staged, *scratch):
    sources, targets, counts, semaphores = scratch
    loads = [
        pltpu.make_async_copy(sources_in, sources, semaphores.at[0]),
        pltpu.make_async_copy(targets_in, targets, semaphores.at[1]),
        pltpu.make_async_copy(counts_in, counts, semaphores.at[2]),
    ]
    for load in loads:
        load.start()
    stage = pltpu.make_async_copy(blocks.at[0], staged, semaphores.at[3])
    stage.start()
    for load in loads:
        load.wait()
    me = lax.axis_index("pcol")
    spare = row_count << field
    for level in range(3):
        first_list = pairs.index((level, level + 1))
        steps = 3 - level
        lists = max(steps, 2)

        def one_slot(slot, found):
            target = targets[level, 0, slot]
            higher = [(target >= (level + j) * row_count).astype(jnp.int32) for j in range(1, steps)]
            step = sum(higher) if higher else jnp.int32(0)
            row = target - (level + step) * row_count
            column = sources[level, 0, slot] - me
            column = jnp.where(column < 0, column + cols, column)
            kind = step if steps > 1 else (column > 0).astype(jnp.int32)
            place = found[lists - 1]
            for j in range(lists - 1):
                place = jnp.where(kind == j, found[j], place)
            plan[first_list + kind, place] = (slot << (2 * field)) + (row << field) + column
            return tuple(found[j] + (kind == j).astype(jnp.int32) for j in range(lists))

        found = lax.fori_loop(0, counts[level], one_slot, (jnp.int32(0),) * lists)
        for j in range(lists):
            plan[count_row, first_list + j] = found[j]
            for extra in range(slot_group):
                plan[first_list + j, found[j] + extra] = spare
    stage.wait()


def make_plan(row_count, cols, sources, targets, counts, blocks):
    width = -(-(sources.shape[-1] + slot_group) // 128) * 128
    return pl.pallas_call(
        functools.partial(plan_kernel, row_count, cols),
        out_shape=[
            jax.ShapeDtypeStruct((8, width), jnp.int32),
            pltpu.VMEM(blocks.shape[1:], blocks.dtype),
        ],
        in_specs=[hbm] * 4,
        out_specs=[smem, vmem],
        scratch_shapes=[
            pltpu.SMEM(sources.shape, jnp.int32),
            pltpu.SMEM(targets.shape, jnp.int32),
            pltpu.SMEM(counts.shape, jnp.int32),
            pltpu.SemaphoreType.DMA((4,)),
        ],
        compiler_params=params,
    )(in_hbm(sources), in_hbm(targets), in_hbm(counts), blocks)


def exchange_order(row_count):
    return [(row + row_count // 2) % row_count for row in range(row_count)]


def fetched_levels(lists, resident):
    needed = dict.fromkeys((layer, pairs[pair][0]) for pair, layer, _ in lists)
    return [key for key in needed if key not in resident]


def update_kernel(config, *refs):
    lists, layer_count, groups_of_solutions, cols, row_count, resident, stages, carries = config
    refs = list(refs)
    plans_in = [refs.pop(0) for _ in range(layer_count)]
    blocks = [refs.pop(0) for _ in range(layer_count)]
    solutions = [refs.pop(0) for _ in range(groups_of_solutions * cols)]
    places = {key: refs.pop(0) for key in resident}
    total_in = refs.pop(0) if carries else None
    out = refs.pop(0)
    next_ref = refs.pop(0) if stages else None
    chosen, total, plans, plan_semaphores, semaphores = refs[:5]
    fetched = fetched_levels(lists, resident + ((stages,) if stages else ()))

    plan_loads = [
        pltpu.make_async_copy(plans_in[n], plans.at[n], plan_semaphores.at[n])
        for n in range(layer_count)
    ]
    loads = {
        key: pltpu.make_async_copy(blocks[key[0]].at[key[1]], refs[5].at[k], semaphores.at[k])
        for k, key in enumerate(fetched)
    }
    for load in plan_loads + list(loads.values()):
        load.start()
    places.update({key: refs[5].at[k] for k, key in enumerate(fetched)})
    if stages:
        places[stages] = next_ref
        loads[stages] = pltpu.make_async_copy(
            blocks[stages[0]].at[stages[1]], next_ref, semaphores.at[len(fetched)]
        )
        loads[stages].start()

    for j, solution_ref in enumerate(solutions):
        chosen[j] = solution_ref[...]
    if carries:
        total[:row_count] = total_in[...]
    else:
        total[...] = jnp.zeros_like(total)
    for load in plan_loads:
        load.wait()

    for pair, layer, j in lists:
        key = (layer, pairs[pair][0])
        if key in loads:
            loads.pop(key).wait()
        pieces = places[key]

        def one_group(g, unused):
            for first in range(0, slot_group, batch):
                entries = [plans[layer, pair, g * slot_group + first + s] for s in range(batch)]
                products = [
                    jnp.dot(
                        pieces[lax.shift_right_logical(entry, 2 * field)],
                        chosen[j * cols + (entry & field_mask)],
                        preferred_element_type=jnp.float32,
                    )
                    for entry in entries
                ]
                for entry, product in zip(entries, products):
                    total[lax.shift_right_logical(entry, field) & field_mask] += product
            return unused

        live = plans[layer, count_row, pair]
        lax.fori_loop(0, (live + slot_group - 1) // slot_group, one_group, 0)

    if out.dtype == jnp.bfloat16:
        for k, row in enumerate(exchange_order(row_count)):
            out[k] = total[row].astype(jnp.bfloat16)
    else:
        out[...] = total[:row_count]
    for load in loads.values():
        load.wait()


def update(
    lists, plans, blocks, solution_groups, total_in, row_count, sends, resident, stages
):
    cols = len(solution_groups[0])
    width, sides = solution_groups[0][0].shape
    solutions = [part for group in solution_groups for part in group]
    operands = plans + blocks + solutions
    specs = [anywhere] * len(plans) + [hbm] * len(blocks) + [vmem] * len(solutions)
    for extra in list(resident.values()) + [total_in]:
        if extra is not None:
            operands.append(extra)
            specs.append(vmem)
    fetched = fetched_levels(lists, tuple(resident) + ((stages,) if stages else ()))
    shape = (row_count, width, sides)
    outs = [pltpu.VMEM(shape, jnp.bfloat16) if sends else jax.ShapeDtypeStruct(shape, jnp.float32)]
    if stages:
        outs.append(pltpu.VMEM(blocks[0].shape[1:], blocks[0].dtype))
    config = (
        lists, len(plans), len(solution_groups), cols, row_count, tuple(resident), stages,
        total_in is not None,
    )
    scratch = [
        pltpu.VMEM((len(solutions), width, sides), jnp.bfloat16),
        pltpu.VMEM((row_count + 1, width, sides), jnp.float32),
        pltpu.SMEM((len(plans),) + plans[0].shape, jnp.int32),
        pltpu.SemaphoreType.DMA((len(plans),)),
        pltpu.SemaphoreType.DMA((len(fetched) + 1,)),
    ]
    if fetched:
        scratch.append(pltpu.VMEM((len(fetched),) + blocks[0].shape[1:], jnp.bfloat16))
    found = pl.pallas_call(
        functools.partial(update_kernel, config),
        out_shape=outs,
        in_specs=specs,
        out_specs=[vmem] * len(outs),
        scratch_shapes=scratch,
        compiler_params=params,
    )(*operands)
    return found if stages else found[0]


def solve_block(inverse, residual):
    return jnp.dot(inverse, residual, preferred_element_type=jnp.float32).astype(jnp.bfloat16)


def reduced_solve(received, given, inverse):
    incoming = jnp.sum(received.astype(jnp.float32), axis=0)
    residual = (given.astype(jnp.float32) - incoming).astype(jnp.bfloat16)
    return solve_block(inverse, residual)


def exchange(send):
    order = exchange_order(lax.axis_size("prow"))
    return lax.all_to_all(send, "prow", 0, 0, tiled=True, axis_index_groups=[order])


def local(blocks, sources, targets, counts, given_sub, given_top, inverse_sub, inverse_top):
    row_count = lax.axis_size("prow")
    cols = lax.axis_size("pcol")
    levels, capacity = sources.shape[3:]
    block_set = blocks[0, 0, 0]
    right_sub = given_sub[0, 0, 0]
    factor_sub = inverse_sub[0, 0, 0]
    right_top = given_top[0, 0]
    factor_top = inverse_top[0, 0]

    level_zero = solve_block(factor_sub[0], right_sub[0])
    zero_own = sibling_values(level_zero, 0)
    block_own = in_hbm(block_set)
    block_sent, level_zero = lax.optimization_barrier((block_set, level_zero))
    plan, staged = make_plan(
        row_count, cols,
        sources.reshape(levels, 1, capacity), targets.reshape(levels, 1, capacity),
        counts.reshape(levels), block_own,
    )
    both = [block_own, in_hbm(from_other_core(block_sent))]

    send = update(
        [(0, 0, 0)], [plan], both[:1], [zero_own], None, row_count, True, {(0, 0): staged}, None
    )
    send, zero_sent, plan_sent = lax.optimization_barrier((send, level_zero, plan))
    received = exchange(send)
    zero_other = sibling_values(zero_sent, 1)
    plans = [plan, from_other_core(plan_sent)]
    second, staged = update(
        [(1, 0, 0), (1, 1, 1)], plans, both, [zero_own, zero_other], None, row_count, False,
        {}, (0, 1),
    )
    received, second, staged = lax.optimization_barrier((received, second, staged))
    level_one = reduced_solve(received, right_sub[1], factor_sub[1])
    one_own = sibling_values(level_one, 0)
    one_other = sibling_values(level_one, 1)

    send = update(
        [(3, 0, 0), (3, 1, 1)], plans, both, [one_own, one_other], second, row_count, True,
        {(0, 1): staged}, None,
    )
    received = exchange(send)
    third, staged = update(
        [(2, 0, 0), (2, 1, 1), (4, 0, 2), (4, 1, 3)], plans, both,
        [zero_own, zero_other, one_own, one_other], None, row_count, False, {}, (0, 2),
    )
    received, third, staged = lax.optimization_barrier((received, third, staged))
    level_two = reduced_solve(received, right_top[0], factor_top[0])
    two_own = sibling_values(level_two, 0)

    resident = {(0, 2): staged}
    third, resident[(1, 2)] = update(
        [(5, 0, 0), (5, 1, 0)], plans, both, [[level_two] * cols], third, row_count, False, resident,
        (1, 2),
    )
    send = update(
        [(6, 0, 0), (6, 1, 0)], plans, both, [two_own], third, row_count, True, resident, None
    )
    send, level_zero, level_one = lax.optimization_barrier((send, level_zero, level_one))
    level_three = reduced_solve(exchange(send), right_top[1], factor_top[1])
    solved_sub = jnp.stack([level_zero, level_one])[None, None, None]
    solved_top = jnp.stack([level_two, level_three])[None, None]
    return (solved_sub, solved_top)


def solution(mesh):
    in_specs = (
        P("prow", "pcol", "zgrid", None, None, None, None),
        P("prow", "pcol", "zgrid", None, None),
        P("prow", "pcol", "zgrid", None, None),
        P("prow", "pcol", "zgrid", None),
        P("prow", "pcol", "zgrid", None, None, None),
        P("prow", "pcol", None, None, None),
        P("prow", "pcol", "zgrid", None, None, None),
        P("prow", "pcol", None, None, None),
    )
    out_specs = (P("prow", "pcol", "zgrid", None, None, None), P("prow", "pcol", None, None, None))
    return jax.shard_map(local, mesh=mesh, in_specs=in_specs, out_specs=out_specs, check_vma=False)
```

profile of v0, /device:TPU:0, one launch (start us, length us, event | category | flops | bytes accessed | tf_op | source)
XLA Modules:
  0.0 58.9 jit_solution(2090745773888927414)
XLA Ops:
  0.6 0.9 %convolution_convert_fusion.3.refs_2_.refs_4_ = bf16[128,128]{1,0:T(8,128)(2,1)S(1)} fusion(bf16[1,1,1,2,128,128]{5,4,3,2,1,0:T(8,128)(2,1)} %param.12, bf16[1,1,1,2,128,128]{5,4,3,2,1,0:T(8,128)(2,1)} %param.14), kind=kOutput, calls=%fused_computation.3 | convolution fusion | flops 4210688 | bytes 98304 | tf_op jit(solution)/shard_map/dot_general | solution.py:234
  2.0 2.6 %collective-permute-start = (bf16[128,128]{1,0:T(8,128)(2,1)S(1)}, bf16[128,128]{1,0:T(8,128)(2,1)S(1)}, u32[]{:S(2)}, u32[]{:S(2)}) collective-permute-start(bf16[128,128]{1,0:T(8,128)(2,1)S(1)} %convolution_convert_fusion.3.refs_2_.refs_4_), channel_id=1, source_target_pairs={{0,2},{1,3},{2,0},{3,1},{4,6},{5,7},{6,4},{7,5},{8,10},{9,11},{10,... | collective-permute-start | bytes 98312 | tf_op jit(solution)/shard_map/ppermute | solution.py:36
  4.6 2.1 %shard_map.95 = (s32[8,128]{1,0:T(8,128)S(1)}, bf16[40,128,128]{2,1,0:T(8,128)(2,1)S(1)}) custom-call(s32[3,1,40]{2,1,0:T(1,128)} %bitcast.79, s32[3,1,40]{2,1,0:T(1,128)} %bitcast.80, s32[3]{0:T(128)} %bitcast.81, bf16[3,40,128,128]{3,2,1,0:T(8,128)(2,1)} %bitcast.72), custom_call_target="tpu_custom_call" | custom-call | tf_op jit(solution)/shard_map/pallas_call | solution.py:92
  6.7 1.6 %shard_map.96 = bf16[8,128,128]{2,1,0:T(8,128)(2,1)} custom-call(s32[8,128]{1,0:T(8,128)S(1)} %get-tuple-element.27.refs_0_, bf16[3,40,128,128]{3,2,1,0:T(8,128)(2,1)} %bitcast.73, bf16[128,128]{1,0:T(8,128)(2,1)S(1)} %convolution_convert_fusion.3.refs_2_.refs_4_, bf16[128,128]{1,0:T(8,128)(2,1)S(1)} %collective-permute-done.refs_3_.refs_5_, ...), custom_call_target="tpu_custom_call" | custom-call | tf_op jit(solution)/shard_map/pallas_call | solution.py:222
  8.3 6.9 %all-to-all-start = ((bf16[8,128,128]{2,1,0:T(8,128)(2,1)}), bf16[8,128,128]{2,1,0:T(8,128)(2,1)S(1)}, u32[]{:S(2)}, u32[]{:S(2)}) async-start(bf16[8,128,128]{2,1,0:T(8,128)(2,1)} %shard_map.96), calls=%async_computation | async-start | bytes 524288 | tf_op jit(solution)/shard_map/all_to_all | solution.py:245
  15.2 1.4 %collective-permute-start.3 = (bf16[128,128]{1,0:T(8,128)(2,1)S(1)}, bf16[128,128]{1,0:T(8,128)(2,1)S(1)}, u32[]{:S(2)}, u32[]{:S(2)}) collective-permute-start(bf16[128,128]{1,0:T(8,128)(2,1)S(1)} %convolution_convert_fusion.3.refs_2_.refs_4_), channel_id=1, source_target_pairs={{0,1},{1,0},{2,3},{3,2},{4,5},{5,4},{6,7},{7,6},{8,9},{9,8},{10,11... | collective-permute-start | bytes 98312 | tf_op jit(solution)/shard_map/ppermute | solution.py:36
  16.6 1.2 %collective-permute-done.1.refs_1_ = s32[8,128]{1,0:T(8,128)S(1)} collective-permute-done((s32[8,128]{1,0:T(8,128)S(1)}, s32[8,128]{1,0:T(8,128)S(1)}, u32[]{:S(2)}, u32[]{:S(2)}) %collective-permute-start.1) | collective-permute-done | bytes 4128 | tf_op jit(solution)/shard_map/ppermute | solution.py:41
  17.8 1.1 %collective-permute-done.4.refs_7_ = bf16[128,128]{1,0:T(8,128)(2,1)S(1)} collective-permute-done((bf16[128,128]{1,0:T(8,128)(2,1)S(1)}, bf16[128,128]{1,0:T(8,128)(2,1)S(1)}, u32[]{:S(2)}, u32[]{:S(2)}) %collective-permute-start.4) | collective-permute-done | bytes 32800 | tf_op jit(solution)/shard_map/ppermute | solution.py:36
  18.8 2.2 %shard_map.97 = (f32[8,128,128]{2,1,0:T(8,128)S(1)}, bf16[40,128,128]{2,1,0:T(8,128)(2,1)S(1)}) custom-call(s32[8,128]{1,0:T(8,128)S(1)} %get-tuple-element.27.refs_0_, s32[8,128]{1,0:T(8,128)S(1)} %collective-permute-done.1.refs_1_, bf16[3,40,128,128]{3,2,1,0:T(8,128)(2,1)} %bitcast.74, bf16[3,40,128,128]{3,2,1,0:T(8,128)(2,1)} %collective-permute-done.2.refs_3_, ...), custom_call_target="tpu_custom_call" | custom-call | tf_op jit(solution)/shard_map/pallas_call | solution.py:222
  21.0 1.2 %all-to-all-done = bf16[8,128,128]{2,1,0:T(8,128)(2,1)S(1)} async-done(((bf16[8,128,128]{2,1,0:T(8,128)(2,1)}), bf16[8,128,128]{2,1,0:T(8,128)(2,1)S(1)}, u32[]{:S(2)}, u32[]{:S(2)}) %all-to-all-start) | async-done | bytes 262176 | tf_op jit(solution)/shard_map/all_to_all | solution.py:245
  23.1 1.5 %collective-permute-start.5 = (bf16[128,128]{1,0:T(8,128)(2,1)S(1)}, bf16[128,128]{1,0:T(8,128)(2,1)S(1)}, u32[]{:S(2)}, u32[]{:S(2)}) collective-permute-start(bf16[128,128]{1,0:T(8,128)(2,1)S(1)} %fusion.refs_4_.refs_8_), channel_id=1, source_target_pairs={{0,2},{1,3},{2,0},{3,1},{4,6},{5,7},{6,4},{7,5},{8,10},{9,11},{10,... | collective-permute-start | bytes 98312 | tf_op jit(solution)/shard_map/ppermute | solution.py:36
  24.6 1.2 %collective-permute-done.7.refs_7_.refs_11_ = bf16[128,128]{1,0:T(8,128)(2,1)S(1)} collective-permute-done((bf16[128,128]{1,0:T(8,128)(2,1)S(1)}, bf16[128,128]{1,0:T(8,128)(2,1)S(1)}, u32[]{:S(2)}, u32[]{:S(2)}) %collective-permute-start.7) | collective-permute-done | bytes 32800 | tf_op jit(solution)/shard_map/ppermute | solution.py:36
  25.8 1.2 %collective-permute-done.5.refs_5_.refs_9_ = bf16[128,128]{1,0:T(8,128)(2,1)S(1)} collective-permute-done((bf16[128,128]{1,0:T(8,128)(2,1)S(1)}, bf16[128,128]{1,0:T(8,128)(2,1)S(1)}, u32[]{:S(2)}, u32[]{:S(2)}) %collective-permute-start.5) | collective-permute-done | bytes 32800 | tf_op jit(solution)/shard_map/ppermute | solution.py:36
  27.0 2.3 %shard_map.98 = bf16[8,128,128]{2,1,0:T(8,128)(2,1)} custom-call(s32[8,128]{1,0:T(8,128)S(1)} %get-tuple-element.27.refs_0_, s32[8,128]{1,0:T(8,128)S(1)} %collective-permute-done.1.refs_1_, bf16[3,40,128,128]{3,2,1,0:T(8,128)(2,1)} %bitcast.75, bf16[3,40,128,128]{3,2,1,0:T(8,128)(2,1)} %collective-permute-done.2.refs_3_, ...), custom_call_target="tpu_custom_call" | custom-call | tf_op jit(solution)/shard_map/pallas_call | solution.py:222
  29.3 5.3 %all-to-all-start.1 = ((bf16[8,128,128]{2,1,0:T(8,128)(2,1)}), bf16[8,128,128]{2,1,0:T(8,128)(2,1)S(1)}, u32[]{:S(2)}, u32[]{:S(2)}) async-start(bf16[8,128,128]{2,1,0:T(8,128)(2,1)} %shard_map.98), calls=%async_computation.1 | async-start | bytes 524288 | tf_op jit(solution)/shard_map/all_to_all | solution.py:245
  34.6 3.0 %shard_map.99 = (f32[8,128,128]{2,1,0:T(8,128)S(1)}, bf16[40,128,128]{2,1,0:T(8,128)(2,1)S(1)}) custom-call(s32[8,128]{1,0:T(8,128)S(1)} %get-tuple-element.27.refs_0_, s32[8,128]{1,0:T(8,128)S(1)} %collective-permute-done.1.refs_1_, bf16[3,40,128,128]{3,2,1,0:T(8,128)(2,1)} %bitcast.76, bf16[3,40,128,128]{3,2,1,0:T(8,128)(2,1)} %collective-permute-done.2.refs_3_, ...), custom_call_target="tpu_custom_call" | custom-call | tf_op jit(solution)/shard_map/pallas_call | solution.py:222
  37.6 3.0 %all-to-all-done.1 = bf16[8,128,128]{2,1,0:T(8,128)(2,1)S(1)} async-done(((bf16[8,128,128]{2,1,0:T(8,128)(2,1)}), bf16[8,128,128]{2,1,0:T(8,128)(2,1)S(1)}, u32[]{:S(2)}, u32[]{:S(2)}) %all-to-all-start.1) | async-done | bytes 262176 | tf_op jit(solution)/shard_map/all_to_all | solution.py:245
  40.8 1.9 %collective-permute-start.8 = (bf16[128,128]{1,0:T(8,128)(2,1)S(1)}, bf16[128,128]{1,0:T(8,128)(2,1)S(1)}, u32[]{:S(2)}, u32[]{:S(2)}) collective-permute-start(bf16[128,128]{1,0:T(8,128)(2,1)S(1)} %bitcast.65), channel_id=1, source_target_pairs={{0,2},{1,3},{2,0},{3,1},{4,6},{5,7},{6,4},{7,5},{8,10},{9,11},{10,... | collective-permute-start | bytes 98312 | tf_op jit(solution)/shard_map/ppermute | solution.py:36
  42.7 1.9 %shard_map.100 = (f32[8,128,128]{2,1,0:T(8,128)S(1)}, bf16[40,128,128]{2,1,0:T(8,128)(2,1)S(1)}) custom-call(s32[8,128]{1,0:T(8,128)S(1)} %get-tuple-element.27.refs_0_, s32[8,128]{1,0:T(8,128)S(1)} %collective-permute-done.1.refs_1_, bf16[3,40,128,128]{3,2,1,0:T(8,128)(2,1)} %bitcast.77, bf16[3,40,128,128]{3,2,1,0:T(8,128)(2,1)} %collective-permute-done.2.refs_3_, ...), custom_call_target="tpu_custom_call" | custom-call | tf_op jit(solution)/shard_map/pallas_call | solution.py:222
  44.7 2.1 %shard_map.101 = bf16[8,128,128]{2,1,0:T(8,128)(2,1)} custom-call(s32[8,128]{1,0:T(8,128)S(1)} %get-tuple-element.27.refs_0_, s32[8,128]{1,0:T(8,128)S(1)} %collective-permute-done.1.refs_1_, bf16[3,40,128,128]{3,2,1,0:T(8,128)(2,1)} %bitcast.78, bf16[3,40,128,128]{3,2,1,0:T(8,128)(2,1)} %collective-permute-done.2.refs_3_, bf16[128,128]{1,0:T(8,128)(2,1)S(1)} %bitcast.68, ...), custom_call_target="tpu_custom_call" | custom-call | tf_op jit(solution)/shard_map/pallas_call | solution.py:222
  46.9 5.3 %all-to-all-start.2 = ((bf16[8,128,128]{2,1,0:T(8,128)(2,1)}), bf16[8,128,128]{2,1,0:T(8,128)(2,1)S(1)}, u32[]{:S(2)}, u32[]{:S(2)}) async-start(bf16[8,128,128]{2,1,0:T(8,128)(2,1)} %shard_map.101), calls=%async_computation.2 | async-start | bytes 524288 | tf_op jit(solution)/shard_map/all_to_all | solution.py:245
  52.2 0.6 %maximum_bitcast_fusion = bf16[1,1,1,2,128,128]{5,4,3,2,1,0:T(8,128)(2,1)} fusion(bf16[1,128,128]{2,1,0:T(8,128)(2,1)S(1)} %bitcast.70, bf16[1,128,128]{2,1,0:T(8,128)(2,1)S(1)} %bitcast.64), kind=kLoop, calls=%fused_computation.9 | loop fusion | flops 32768 | bytes 131072 | tf_op jit(solution)/shard_map/broadcast_in_dim | solution.py:308
  52.8 5.2 %all-to-all-done.2 = bf16[8,128,128]{2,1,0:T(8,128)(2,1)S(1)} async-done(((bf16[8,128,128]{2,1,0:T(8,128)(2,1)}), bf16[8,128,128]{2,1,0:T(8,128)(2,1)S(1)}, u32[]{:S(2)}, u32[]{:S(2)}) %all-to-all-start.2) | async-done | bytes 262176 | tf_op jit(solution)/shard_map/all_to_all | solution.py:245
  58.2 0.6 %maximum_bitcast_fusion.1 = bf16[1,1,2,128,128]{4,3,2,1,0:T(8,128)(2,1)} fusion(bf16[1,128,128]{2,1,0:T(8,128)(2,1)S(1)} %fusion.1, bf16[1,128,128]{2,1,0:T(8,128)(2,1)S(1)} %bitcast.69), kind=kLoop, calls=%fused_computation.10 | loop fusion | flops 32768 | bytes 131072 | tf_op jit(solution)/shard_map/broadcast_in_dim | solution.py:309
  (24 shorter events, 1.8 us)
Async XLA Ops:
  1.5 17.3 %collective-permute-start.2 = (bf16[3,40,128,128]{3,2,1,0:T(8,128)(2,1)}, bf16[3,40,128,128]{3,2,1,0:T(8,128)(2,1)}, u32[]{:S(2)}, u32[]{:S(2)}) collective-permute-start(bf16[3,40,128,128]{3,2,1,0:T(8,128)(2,1)} %bitcast.71), channel_id=1, source_target_pairs={{0,1},{1,0},{2,3},{3,2},{4,5},{5,4},{6,7},{7,6},{8,9},{9,8},{10,11... | collective-permute-start | bytes 11796488 | tf_op jit(solution)/shard_map/ppermute | solution.py:41
  2.0 4.7 %collective-permute-start = (bf16[128,128]{1,0:T(8,128)(2,1)S(1)}, bf16[128,128]{1,0:T(8,128)(2,1)S(1)}, u32[]{:S(2)}, u32[]{:S(2)}) collective-permute-start(bf16[128,128]{1,0:T(8,128)(2,1)S(1)} %convolution_convert_fusion.3.refs_2_.refs_4_), channel_id=1, source_target_pairs={{0,2},{1,3},{2,0},{3,1},{4,6},{5,7},{6,4},{7,5},{8,10},{9,11},{10,... | collective-permute-start | bytes 98312 | tf_op jit(solution)/shard_map/ppermute | solution.py:36
  8.3 14.0 %all-to-all-start = ((bf16[8,128,128]{2,1,0:T(8,128)(2,1)}), bf16[8,128,128]{2,1,0:T(8,128)(2,1)S(1)}, u32[]{:S(2)}, u32[]{:S(2)}) async-start(bf16[8,128,128]{2,1,0:T(8,128)(2,1)} %shard_map.96), calls=%async_computation | async-start | bytes 524288 | tf_op jit(solution)/shard_map/all_to_all | solution.py:245
  15.2 7.1 %copy-start = (bf16[1,1,1,2,128,128]{5,4,3,2,1,0:T(8,128)(2,1)S(1)}, bf16[1,1,1,2,128,128]{5,4,3,2,1,0:T(8,128)(2,1)}, u32[]{:S(2)}) copy-start(bf16[1,1,1,2,128,128]{5,4,3,2,1,0:T(8,128)(2,1)} %param.12) | copy-start | bytes 196612
  15.2 7.1 %copy-start.1 = (bf16[1,1,1,2,128,128]{5,4,3,2,1,0:T(8,128)(2,1)S(1)}, bf16[1,1,1,2,128,128]{5,4,3,2,1,0:T(8,128)(2,1)}, u32[]{:S(2)}) copy-start(bf16[1,1,1,2,128,128]{5,4,3,2,1,0:T(8,128)(2,1)} %param.14) | copy-start | bytes 196612
  15.2 3.7 %collective-permute-start.4 = (bf16[128,128]{1,0:T(8,128)(2,1)S(1)}, bf16[128,128]{1,0:T(8,128)(2,1)S(1)}, u32[]{:S(2)}, u32[]{:S(2)}) collective-permute-start(bf16[128,128]{1,0:T(8,128)(2,1)S(1)} %convolution_convert_fusion.3.refs_2_.refs_4_), channel_id=1, source_target_pairs={{0,3},{1,2},{2,1},{3,0},{4,7},{5,6},{6,5},{7,4},{8,11},{9,10},{10,... | collective-permute-start | bytes 98312 | tf_op jit(solution)/shard_map/ppermute | solution.py:36
  15.2 3.7 %collective-permute-start.3 = (bf16[128,128]{1,0:T(8,128)(2,1)S(1)}, bf16[128,128]{1,0:T(8,128)(2,1)S(1)}, u32[]{:S(2)}, u32[]{:S(2)}) collective-permute-start(bf16[128,128]{1,0:T(8,128)(2,1)S(1)} %convolution_convert_fusion.3.refs_2_.refs_4_), channel_id=1, source_target_pairs={{0,1},{1,0},{2,3},{3,2},{4,5},{5,4},{6,7},{7,6},{8,9},{9,8},{10,11... | collective-permute-start | bytes 98312 | tf_op jit(solution)/shard_map/ppermute | solution.py:36
  16.6 1.2 %collective-permute-start.1 = (s32[8,128]{1,0:T(8,128)S(1)}, s32[8,128]{1,0:T(8,128)S(1)}, u32[]{:S(2)}, u32[]{:S(2)}) collective-permute-start(s32[8,128]{1,0:T(8,128)S(1)} %get-tuple-element.27.refs_0_), channel_id=1, source_target_pairs={{0,1},{1,0},{2,3},{3,2},{4,5},{5,4},{6,7},{7,6},{8,9},{9,8},{10,11... | collective-permute-start | bytes 12296 | tf_op jit(solution)/shard_map/ppermute | solution.py:41
  22.4 3.4 %collective-permute-start.7 = (bf16[128,128]{1,0:T(8,128)(2,1)S(1)}, bf16[128,128]{1,0:T(8,128)(2,1)S(1)}, u32[]{:S(2)}, u32[]{:S(2)}) collective-permute-start(bf16[128,128]{1,0:T(8,128)(2,1)S(1)} %fusion.refs_4_.refs_8_), channel_id=1, source_target_pairs={{0,3},{1,2},{2,1},{3,0},{4,7},{5,6},{6,5},{7,4},{8,11},{9,10},{10,... | collective-permute-start | bytes 98312 | tf_op jit(solution)/shard_map/ppermute | solution.py:36
  22.5 3.3 %collective-permute-start.6 = (bf16[128,128]{1,0:T(8,128)(2,1)S(1)}, bf16[128,128]{1,0:T(8,128)(2,1)S(1)}, u32[]{:S(2)}, u32[]{:S(2)}) collective-permute-start(bf16[128,128]{1,0:T(8,128)(2,1)S(1)} %fusion.refs_4_.refs_8_), channel_id=1, source_target_pairs={{0,1},{1,0},{2,3},{3,2},{4,5},{5,4},{6,7},{7,6},{8,9},{9,8},{10,11... | collective-permute-start | bytes 98312 | tf_op jit(solution)/shard_map/ppermute | solution.py:36
  23.1 3.9 %collective-permute-start.5 = (bf16[128,128]{1,0:T(8,128)(2,1)S(1)}, bf16[128,128]{1,0:T(8,128)(2,1)S(1)}, u32[]{:S(2)}, u32[]{:S(2)}) collective-permute-start(bf16[128,128]{1,0:T(8,128)(2,1)S(1)} %fusion.refs_4_.refs_8_), channel_id=1, source_target_pairs={{0,2},{1,3},{2,0},{3,1},{4,6},{5,7},{6,4},{7,5},{8,10},{9,11},{10,... | collective-permute-start | bytes 98312 | tf_op jit(solution)/shard_map/ppermute | solution.py:36
  29.3 11.3 %all-to-all-start.1 = ((bf16[8,128,128]{2,1,0:T(8,128)(2,1)}), bf16[8,128,128]{2,1,0:T(8,128)(2,1)S(1)}, u32[]{:S(2)}, u32[]{:S(2)}) async-start(bf16[8,128,128]{2,1,0:T(8,128)(2,1)} %shard_map.98), calls=%async_computation.1 | async-start | bytes 524288 | tf_op jit(solution)/shard_map/all_to_all | solution.py:245
  34.6 6.0 %copy-start.2 = (bf16[1,1,2,128,128]{4,3,2,1,0:T(8,128)(2,1)S(1)}, bf16[1,1,2,128,128]{4,3,2,1,0:T(8,128)(2,1)}, u32[]{:S(2)}) copy-start(bf16[1,1,2,128,128]{4,3,2,1,0:T(8,128)(2,1)} %param.15) | copy-start | bytes 196612
  34.6 6.0 %copy-start.3 = (bf16[1,1,2,128,128]{4,3,2,1,0:T(8,128)(2,1)S(1)}, bf16[1,1,2,128,128]{4,3,2,1,0:T(8,128)(2,1)}, u32[]{:S(2)}) copy-start(bf16[1,1,2,128,128]{4,3,2,1,0:T(8,128)(2,1)} %param.13) | copy-start | bytes 196612
  40.8 3.9 %collective-permute-start.8 = (bf16[128,128]{1,0:T(8,128)(2,1)S(1)}, bf16[128,128]{1,0:T(8,128)(2,1)S(1)}, u32[]{:S(2)}, u32[]{:S(2)}) collective-permute-start(bf16[128,128]{1,0:T(8,128)(2,1)S(1)} %bitcast.65), channel_id=1, source_target_pairs={{0,2},{1,3},{2,0},{3,1},{4,6},{5,7},{6,4},{7,5},{8,10},{9,11},{10,... | collective-permute-start | bytes 98312 | tf_op jit(solution)/shard_map/ppermute | solution.py:36
  46.9 11.2 %all-to-all-start.2 = ((bf16[8,128,128]{2,1,0:T(8,128)(2,1)}), bf16[8,128,128]{2,1,0:T(8,128)(2,1)S(1)}, u32[]{:S(2)}, u32[]{:S(2)}) async-start(bf16[8,128,128]{2,1,0:T(8,128)(2,1)} %shard_map.101), calls=%async_computation.2 | async-start | bytes 524288 | tf_op jit(solution)/shard_map/all_to_all | solution.py:245
where the time goes:
time: 59.5 us; the launch traced here: 58.9 us
  starting transfers between devices  26 us (44%)
  Pallas kernels  15.1 us (25%)
  waiting for transfers between devices  14.2 us (24%)
  other arithmetic  1.4 us (2%)
  matrix products  1.3 us (2%)
  between operations  0.76 us (1%)
    all_to_all x3, starting transfers between devices, exchange(): lax.all_to_all(send, 'prow', 0, 0, tiled=True, axis_index_groups=[order])  17.5 us
    pallas_call x6, Pallas kernels, update(): pl.pallas_call(functools.partial(update_kernel, config), out_shape=outs,...  13 us
    all_to_all x3, waiting for transfers between devices, exchange(): lax.all_to_all(send, 'prow', 0, 0, tiled=True, axis_index_groups=[order])  9.43 us
    ppermute x7, starting transfers between devices, sibling_values(): found.append(lax.ppermute(value, ('pcol', 'zgrid'), moves))  8.06 us
    ppermute x7, waiting for transfers between devices, sibling_values(): found.append(lax.ppermute(value, ('pcol', 'zgrid'), moves))  3.64 us
    pallas_call x1, Pallas kernels, make_plan(): pl.pallas_call(functools.partial(plan_kernel, row_count, cols), out_shape...  2.08 us
    dot_general x4, matrix products, solve_block(): jnp.dot(inverse, residual, preferred_element_type=jnp.float32)  1.3 us
  transfers between devices with their start and end apart: 12, of which 8 were waited for; matrix products, arithmetic and copies ran while one was open for 1% of the time, Pallas kernels for 18%

commit v1 on v0

--- a/solution.py
+++ b/solution.py
@@ -45,7 +45,7 @@
     return pltpu.with_memory_space_constraint(value, pltpu.HBM)
 
 
-def plan_kernel(row_count, cols, sources_in, targets_in, counts_in, blocks, plan, staged, *scratch):
+def plan_kernel(row_count, cols, sources_in, targets_in, counts_in, blocks, plan, kept, staged, *scratch):
     sources, targets, counts, semaphores = scratch
     loads = [
         pltpu.make_async_copy(sources_in, sources, semaphores.at[0]),
@@ -76,14 +76,18 @@
             place = found[lists - 1]
             for j in range(lists - 1):
                 place = jnp.where(kind == j, found[j], place)
-            plan[first_list + kind, place] = (slot << (2 * field)) + (row << field) + column
+            entry = (slot << (2 * field)) + (row << field) + column
+            plan[first_list + kind, place] = entry
+            kept[first_list + kind, place] = entry
             return tuple(found[j] + (kind == j).astype(jnp.int32) for j in range(lists))
 
         found = lax.fori_loop(0, counts[level], one_slot, (jnp.int32(0),) * lists)
         for j in range(lists):
             plan[count_row, first_list + j] = found[j]
+            kept[count_row, first_list + j] = found[j]
             for extra in range(slot_group):
                 plan[first_list + j, found[j] + extra] = spare
+                kept[first_list + j, found[j] + extra] = spare
     stage.wait()
 
 
@@ -93,10 +97,11 @@
         functools.partial(plan_kernel, row_count, cols),
         out_shape=[
             jax.ShapeDtypeStruct((8, width), jnp.int32),
+            pltpu.SMEM((8, width), jnp.int32),
             pltpu.VMEM(blocks.shape[1:], blocks.dtype),
         ],
         in_specs=[hbm] * 4,
-        out_specs=[smem, vmem],
+        out_specs=[smem, smem, vmem],
         scratch_shapes=[
             pltpu.SMEM(sources.shape, jnp.int32),
             pltpu.SMEM(targets.shape, jnp.int32),
@@ -117,7 +122,7 @@
 
 
 def update_kernel(config, *refs):
-    lists, layer_count, groups_of_solutions, cols, row_count, resident, stages, carries = config
+    lists, layer_count, groups_of_solutions, cols, row_count, resident, stages, carries, keeps_plan = config
     refs = list(refs)
     plans_in = [refs.pop(0) for _ in range(layer_count)]
     blocks = [refs.pop(0) for _ in range(layer_count)]
@@ -126,20 +131,22 @@
     total_in = refs.pop(0) if carries else None
     out = refs.pop(0)
     next_ref = refs.pop(0) if stages else None
-    chosen, total, plans, plan_semaphores, semaphores = refs[:5]
+    plans = list(plans_in)
+    if keeps_plan:
+        plans[1] = refs.pop(0)
+    chosen, total, plan_semaphore, semaphores = refs[:4]
     fetched = fetched_levels(lists, resident + ((stages,) if stages else ()))
 
-    plan_loads = [
-        pltpu.make_async_copy(plans_in[n], plans.at[n], plan_semaphores.at[n])
-        for n in range(layer_count)
-    ]
+    plan_loads = []
+    if keeps_plan:
+        plan_loads.append(pltpu.make_async_copy(plans_in[1], plans[1], plan_semaphore))
     loads = {
-        key: pltpu.make_async_copy(blocks[key[0]].at[key[1]], refs[5].at[k], semaphores.at[k])
+        key: pltpu.make_async_copy(blocks[key[0]].at[key[1]], refs[4].at[k], semaphores.at[k])
         for k, key in enumerate(fetched)
     }
     for load in plan_loads + list(loads.values()):
         load.start()
-    places.update({key: refs[5].at[k] for k, key in enumerate(fetched)})
+    places.update({key: refs[4].at[k] for k, key in enumerate(fetched)})
     if stages:
         places[stages] = next_ref
         loads[stages] = pltpu.make_async_copy(
@@ -164,7 +171,7 @@
 
         def one_group(g, unused):
             for first in range(0, slot_group, batch):
-                entries = [plans[layer, pair, g * slot_group + first + s] for s in range(batch)]
+                entries = [plans[layer][pair, g * slot_group + first + s] for s in range(batch)]
                 products = [
                     jnp.dot(
                         pieces[lax.shift_right_logical(entry, 2 * field)],
@@ -177,7 +184,7 @@
                     total[lax.shift_right_logical(entry, field) & field_mask] += product
             return unused
 
-        live = plans[layer, count_row, pair]
+        live = plans[layer][count_row, pair]
         lax.fori_loop(0, (live + slot_group - 1) // slot_group, one_group, 0)
 
     if out.dtype == jnp.bfloat16:
@@ -190,13 +197,13 @@
 
 
 def update(
-    lists, plans, blocks, solution_groups, total_in, row_count, sends, resident, stages
+    lists, plans, blocks, solution_groups, total_in, row_count, sends, resident, stages, keeps_plan=False
 ):
     cols = len(solution_groups[0])
     width, sides = solution_groups[0][0].shape
     solutions = [part for group in solution_groups for part in group]
     operands = plans + blocks + solutions
-    specs = [anywhere] * len(plans) + [hbm] * len(blocks) + [vmem] * len(solutions)
+    specs = [smem] * len(plans) + [hbm] * len(blocks) + [vmem] * len(solutions)
     for extra in list(resident.values()) + [total_in]:
         if extra is not None:
             operands.append(extra)
@@ -206,15 +213,19 @@
     outs = [pltpu.VMEM(shape, jnp.bfloat16) if sends else jax.ShapeDtypeStruct(shape, jnp.float32)]
     if stages:
         outs.append(pltpu.VMEM(blocks[0].shape[1:], blocks[0].dtype))
+    places = [vmem] * len(outs)
+    if keeps_plan:
+        specs[1] = anywhere
+        outs.append(pltpu.SMEM(plans[1].shape, jnp.int32))
+        places.append(smem)
     config = (
         lists, len(plans), len(solution_groups), cols, row_count, tuple(resident), stages,
-        total_in is not None,
+        total_in is not None, keeps_plan,
     )
     scratch = [
         pltpu.VMEM((len(solutions), width, sides), jnp.bfloat16),
         pltpu.VMEM((row_count + 1, width, sides), jnp.float32),
-        pltpu.SMEM((len(plans),) + plans[0].shape, jnp.int32),
-        pltpu.SemaphoreType.DMA((len(plans),)),
+        pltpu.SemaphoreType.DMA,
         pltpu.SemaphoreType.DMA((len(fetched) + 1,)),
     ]
     if fetched:
@@ -223,11 +234,11 @@
         functools.partial(update_kernel, config),
         out_shape=outs,
         in_specs=specs,
-        out_specs=[vmem] * len(outs),
+        out_specs=places,
         scratch_shapes=scratch,
         compiler_params=params,
     )(*operands)
-    return found if stages else found[0]
+    return found if len(outs) > 1 else found[0]
 
 
 def solve_block(inverse, residual):
@@ -259,7 +270,7 @@
     zero_own = sibling_values(level_zero, 0)
     block_own = in_hbm(block_set)
     block_sent, level_zero = lax.optimization_barrier((block_set, level_zero))
-    plan, staged = make_plan(
+    plan, own_plan, staged = make_plan(
         row_count, cols,
         sources.reshape(levels, 1, capacity), targets.reshape(levels, 1, capacity),
         counts.reshape(levels), block_own,
@@ -267,15 +278,15 @@
     both = [block_own, in_hbm(from_other_core(block_sent))]
 
     send = update(
-        [(0, 0, 0)], [plan], both[:1], [zero_own], None, row_count, True, {(0, 0): staged}, None
+        [(0, 0, 0)], [own_plan], both[:1], [zero_own], None, row_count, True, {(0, 0): staged}, None
     )
     send, zero_sent, plan_sent = lax.optimization_barrier((send, level_zero, plan))
     received = exchange(send)
     zero_other = sibling_values(zero_sent, 1)
-    plans = [plan, from_other_core(plan_sent)]
-    second, staged = update(
+    plans = [own_plan, from_other_core(plan_sent)]
+    second, staged, plans[1] = update(
         [(1, 0, 0), (1, 1, 1)], plans, both, [zero_own, zero_other], None, row_count, False,
-        {}, (0, 1),
+        {}, (0, 1), True,
     )
     received, second, staged = lax.optimization_barrier((received, second, staged))
     level_one = reduced_solve(received, right_sub[1], factor_sub[1])

time: 59.5 us -> 58.5 us (0.983)
  Pallas kernels: 15.1 us -> 13.4 us
  waiting for transfers between devices: 14.2 us -> 15.1 us
    pallas_call x6, Pallas kernels: 13 us -> 11.1 us  [update(): pl.pallas_call(functools.partial(update_kernel, config), out_shape=outs,...]
    ppermute x7, waiting for transfers between devices: 3.64 us -> 4.33 us  [sibling_values(): found.append(lax.ppermute(value, ('pcol', 'zgrid'), moves))]
    ppermute x7, starting transfers between devices: 8.06 us -> 7.4 us  [sibling_values(): found.append(lax.ppermute(value, ('pcol', 'zgrid'), moves))]
  transfers between devices with their start and end apart: 12 -> 12, of which waited for: 8 -> 8; matrix products, arithmetic and copies ran while one was open for 1% -> 1% of each run, Pallas kernels for 18% -> 17%
where the time goes in v1:
time: 58.5 us; the launch traced here: 57.7 us
  starting transfers between devices  25.7 us (44%)
  waiting for transfers between devices  15.1 us (26%)
  Pallas kernels  13.4 us (23%)
  other arithmetic  1.4 us (2%)
  matrix products  1.3 us (2%)
  between operations  0.76 us (1%)
    all_to_all x3, starting transfers between devices, exchange(): lax.all_to_all(send, 'prow', 0, 0, tiled=True, axis_index_groups=[order])  17.8 us
    pallas_call x6, Pallas kernels, update(): pl.pallas_call(functools.partial(update_kernel, config), out_shape=outs,...  11.1 us
    all_to_all x3, waiting for transfers between devices, exchange(): lax.all_to_all(send, 'prow', 0, 0, tiled=True, axis_index_groups=[order])  9.61 us
    ppermute x7, starting transfers between devices, sibling_values(): found.append(lax.ppermute(value, ('pcol', 'zgrid'), moves))  7.4 us
    ppermute x7, waiting for transfers between devices, sibling_values(): found.append(lax.ppermute(value, ('pcol', 'zgrid'), moves))  4.33 us
    pallas_call x1, Pallas kernels, make_plan(): pl.pallas_call(functools.partial(plan_kernel, row_count, cols), out_shape...  2.35 us
    dot_general x4, matrix products, solve_block(): jnp.dot(inverse, residual, preferred_element_type=jnp.float32)  1.3 us
  transfers between devices with their start and end apart: 12, of which 8 were waited for; matrix products, arithmetic and copies ran while one was open for 1% of the time, Pallas kernels for 17%

profile of v1, /device:TPU:0, one launch (start us, length us, event | category | flops | bytes accessed | tf_op | source)
XLA Modules:
  0.0 57.7 jit_solution(10835621150635798915)
XLA Ops:
  0.6 0.9 %convolution_convert_fusion.3.refs_2_.refs_4_ = bf16[128,128]{1,0:T(8,128)(2,1)S(1)} fusion(bf16[1,1,1,2,128,128]{5,4,3,2,1,0:T(8,128)(2,1)} %param.12, bf16[1,1,1,2,128,128]{5,4,3,2,1,0:T(8,128)(2,1)} %param.14), kind=kOutput, calls=%fused_computation.3 | convolution fusion | flops 4210688 | bytes 98304 | tf_op jit(solution)/shard_map/dot_general | solution.py:245
  2.0 2.6 %collective-permute-start = (bf16[128,128]{1,0:T(8,128)(2,1)S(1)}, bf16[128,128]{1,0:T(8,128)(2,1)S(1)}, u32[]{:S(2)}, u32[]{:S(2)}) collective-permute-start(bf16[128,128]{1,0:T(8,128)(2,1)S(1)} %convolution_convert_fusion.3.refs_2_.refs_4_), channel_id=1, source_target_pairs={{0,2},{1,3},{2,0},{3,1},{4,6},{5,7},{6,4},{7,5},{8,10},{9,11},{10,... | collective-permute-start | bytes 98312 | tf_op jit(solution)/shard_map/ppermute | solution.py:36
  4.6 2.3 %shard_map.95 = (s32[8,128]{1,0:T(8,128)S(1)}, s32[8,128]{1,0:T(8,128)S(4)}, bf16[40,128,128]{2,1,0:T(8,128)(2,1)S(1)}) custom-call(s32[3,1,40]{2,1,0:T(1,128)} %bitcast.79, s32[3,1,40]{2,1,0:T(1,128)} %bitcast.80, s32[3]{0:T(128)} %bitcast.81, bf16[3,40,128,128]{3,2,1,0:T(8,128)(2,1)} %bitcast.72), custom_call_target="tpu_custom_call" | custom-call | tf_op jit(solution)/shard_map/pallas_call | solution.py:96
  7.0 1.0 %shard_map.96 = bf16[8,128,128]{2,1,0:T(8,128)(2,1)} custom-call(s32[8,128]{1,0:T(8,128)S(4)} %get-tuple-element.26.refs_0_, bf16[3,40,128,128]{3,2,1,0:T(8,128)(2,1)} %bitcast.73, bf16[128,128]{1,0:T(8,128)(2,1)S(1)} %convolution_convert_fusion.3.refs_2_.refs_4_, bf16[128,128]{1,0:T(8,128)(2,1)S(1)} %collective-permute-done.refs_3_.refs_5_, ...), custom_call_target="tpu_custom_call" | custom-call | tf_op jit(solution)/shard_map/pallas_call | solution.py:233
  8.0 7.0 %all-to-all-start = ((bf16[8,128,128]{2,1,0:T(8,128)(2,1)}), bf16[8,128,128]{2,1,0:T(8,128)(2,1)S(1)}, u32[]{:S(2)}, u32[]{:S(2)}) async-start(bf16[8,128,128]{2,1,0:T(8,128)(2,1)} %shard_map.96), calls=%async_computation | async-start | bytes 524288 | tf_op jit(solution)/shard_map/all_to_all | solution.py:256
  15.0 1.0 %collective-permute-start.3 = (bf16[128,128]{1,0:T(8,128)(2,1)S(1)}, bf16[128,128]{1,0:T(8,128)(2,1)S(1)}, u32[]{:S(2)}, u32[]{:S(2)}) collective-permute-start(bf16[128,128]{1,0:T(8,128)(2,1)S(1)} %convolution_convert_fusion.3.refs_2_.refs_4_), channel_id=1, source_target_pairs={{0,1},{1,0},{2,3},{3,2},{4,5},{5,4},{6,7},{7,6},{8,9},{9,8},{10,11... | collective-permute-start | bytes 98312 | tf_op jit(solution)/shard_map/ppermute | solution.py:36
  16.0 1.2 %collective-permute-done.1.refs_1_ = s32[8,128]{1,0:T(8,128)S(1)} collective-permute-done((s32[8,128]{1,0:T(8,128)S(1)}, s32[8,128]{1,0:T(8,128)S(1)}, u32[]{:S(2)}, u32[]{:S(2)}) %collective-permute-start.1) | collective-permute-done | bytes 4128 | tf_op jit(solution)/shard_map/ppermute | solution.py:41
  17.2 1.2 %collective-permute-done.4.refs_7_ = bf16[128,128]{1,0:T(8,128)(2,1)S(1)} collective-permute-done((bf16[128,128]{1,0:T(8,128)(2,1)S(1)}, bf16[128,128]{1,0:T(8,128)(2,1)S(1)}, u32[]{:S(2)}, u32[]{:S(2)}) %collective-permute-start.4) | collective-permute-done | bytes 32800 | tf_op jit(solution)/shard_map/ppermute | solution.py:36
  18.4 2.1 %shard_map.97 = (f32[8,128,128]{2,1,0:T(8,128)S(1)}, bf16[40,128,128]{2,1,0:T(8,128)(2,1)S(1)}, s32[8,128]{1,0:T(8,128)S(4)}) custom-call(s32[8,128]{1,0:T(8,128)S(4)} %get-tuple-element.26.refs_0_, s32[8,128]{1,0:T(8,128)S(1)} %collective-permute-done.1.refs_1_, bf16[3,40,128,128]{3,2,1,0:T(8,128)(2,1)} %bitcast.74, ...), custom_call_target="tpu_custom_call" | custom-call | tf_op jit(solution)/shard_map/pallas_call | solution.py:233
  20.5 1.0 %all-to-all-done = bf16[8,128,128]{2,1,0:T(8,128)(2,1)S(1)} async-done(((bf16[8,128,128]{2,1,0:T(8,128)(2,1)}), bf16[8,128,128]{2,1,0:T(8,128)(2,1)S(1)}, u32[]{:S(2)}, u32[]{:S(2)}) %all-to-all-start) | async-done | bytes 262176 | tf_op jit(solution)/shard_map/all_to_all | solution.py:256
  22.2 1.7 %collective-permute-start.5 = (bf16[128,128]{1,0:T(8,128)(2,1)S(1)}, bf16[128,128]{1,0:T(8,128)(2,1)S(1)}, u32[]{:S(2)}, u32[]{:S(2)}) collective-permute-start(bf16[128,128]{1,0:T(8,128)(2,1)S(1)} %fusion.refs_4_.refs_8_), channel_id=1, source_target_pairs={{0,2},{1,3},{2,0},{3,1},{4,6},{5,7},{6,4},{7,5},{8,10},{9,11},{10,... | collective-permute-start | bytes 98312 | tf_op jit(solution)/shard_map/ppermute | solution.py:36
  23.9 1.2 %collective-permute-done.7.refs_7_.refs_11_ = bf16[128,128]{1,0:T(8,128)(2,1)S(1)} collective-permute-done((bf16[128,128]{1,0:T(8,128)(2,1)S(1)}, bf16[128,128]{1,0:T(8,128)(2,1)S(1)}, u32[]{:S(2)}, u32[]{:S(2)}) %collective-permute-start.7) | collective-permute-done | bytes 32800 | tf_op jit(solution)/shard_map/ppermute | solution.py:36
  25.1 1.1 %collective-permute-done.5.refs_5_.refs_9_ = bf16[128,128]{1,0:T(8,128)(2,1)S(1)} collective-permute-done((bf16[128,128]{1,0:T(8,128)(2,1)S(1)}, bf16[128,128]{1,0:T(8,128)(2,1)S(1)}, u32[]{:S(2)}, u32[]{:S(2)}) %collective-permute-start.5) | collective-permute-done | bytes 32800 | tf_op jit(solution)/shard_map/ppermute | solution.py:36
  26.2 2.3 %shard_map.98 = bf16[8,128,128]{2,1,0:T(8,128)(2,1)} custom-call(s32[8,128]{1,0:T(8,128)S(4)} %get-tuple-element.26.refs_0_, s32[8,128]{1,0:T(8,128)S(4)} %get-tuple-element.33.refs_1_, bf16[3,40,128,128]{3,2,1,0:T(8,128)(2,1)} %bitcast.75, bf16[3,40,128,128]{3,2,1,0:T(8,128)(2,1)} %collective-permute-done.2.refs_3_, ...), custom_call_target="tpu_custom_call" | custom-call | tf_op jit(solution)/shard_map/pallas_call | solution.py:233
  28.5 5.3 %all-to-all-start.1 = ((bf16[8,128,128]{2,1,0:T(8,128)(2,1)}), bf16[8,128,128]{2,1,0:T(8,128)(2,1)S(1)}, u32[]{:S(2)}, u32[]{:S(2)}) async-start(bf16[8,128,128]{2,1,0:T(8,128)(2,1)} %shard_map.98), calls=%async_computation.1 | async-start | bytes 524288 | tf_op jit(solution)/shard_map/all_to_all | solution.py:256
  33.8 3.0 %shard_map.99 = (f32[8,128,128]{2,1,0:T(8,128)S(1)}, bf16[40,128,128]{2,1,0:T(8,128)(2,1)S(1)}) custom-call(s32[8,128]{1,0:T(8,128)S(4)} %get-tuple-element.26.refs_0_, s32[8,128]{1,0:T(8,128)S(4)} %get-tuple-element.33.refs_1_, bf16[3,40,128,128]{3,2,1,0:T(8,128)(2,1)} %bitcast.76, bf16[3,40,128,128]{3,2,1,0:T(8,128)(2,1)} %collective-permute-done.2.refs_3_, ...), custom_call_target="tpu_custom_call" | custom-call | tf_op jit(solution)/shard_map/pallas_call | solution.py:233
  36.8 3.4 %all-to-all-done.1 = bf16[8,128,128]{2,1,0:T(8,128)(2,1)S(1)} async-done(((bf16[8,128,128]{2,1,0:T(8,128)(2,1)}), bf16[8,128,128]{2,1,0:T(8,128)(2,1)S(1)}, u32[]{:S(2)}, u32[]{:S(2)}) %all-to-all-start.1) | async-done | bytes 262176 | tf_op jit(solution)/shard_map/all_to_all | solution.py:256
  40.3 1.6 %collective-permute-start.8 = (bf16[128,128]{1,0:T(8,128)(2,1)S(1)}, bf16[128,128]{1,0:T(8,128)(2,1)S(1)}, u32[]{:S(2)}, u32[]{:S(2)}) collective-permute-start(bf16[128,128]{1,0:T(8,128)(2,1)S(1)} %bitcast.65), channel_id=1, source_target_pairs={{0,2},{1,3},{2,0},{3,1},{4,6},{5,7},{6,4},{7,5},{8,10},{9,11},{10,... | collective-permute-start | bytes 98312 | tf_op jit(solution)/shard_map/ppermute | solution.py:36
  42.0 1.4 %shard_map.100 = (f32[8,128,128]{2,1,0:T(8,128)S(1)}, bf16[40,128,128]{2,1,0:T(8,128)(2,1)S(1)}) custom-call(s32[8,128]{1,0:T(8,128)S(4)} %get-tuple-element.26.refs_0_, s32[8,128]{1,0:T(8,128)S(4)} %get-tuple-element.33.refs_1_, bf16[3,40,128,128]{3,2,1,0:T(8,128)(2,1)} %bitcast.77, bf16[3,40,128,128]{3,2,1,0:T(8,128)(2,1)} %collective-permute-done.2.refs_3_, ...), custom_call_target="tpu_custom_call" | custom-call | tf_op jit(solution)/shard_map/pallas_call | solution.py:233
  43.4 0.9 %collective-permute-done.8.refs_5_ = bf16[128,128]{1,0:T(8,128)(2,1)S(1)} collective-permute-done((bf16[128,128]{1,0:T(8,128)(2,1)S(1)}, bf16[128,128]{1,0:T(8,128)(2,1)S(1)}, u32[]{:S(2)}, u32[]{:S(2)}) %collective-permute-start.8) | collective-permute-done | bytes 32800 | tf_op jit(solution)/shard_map/ppermute | solution.py:36
  44.3 1.3 %shard_map.101 = bf16[8,128,128]{2,1,0:T(8,128)(2,1)} custom-call(s32[8,128]{1,0:T(8,128)S(4)} %get-tuple-element.26.refs_0_, s32[8,128]{1,0:T(8,128)S(4)} %get-tuple-element.33.refs_1_, bf16[3,40,128,128]{3,2,1,0:T(8,128)(2,1)} %bitcast.78, bf16[3,40,128,128]{3,2,1,0:T(8,128)(2,1)} %collective-permute-done.2.refs_3_, bf16[128,128]{1,0:T(8,128)(2,1)S(1)} %bitcast.68, ...), custom_call_target="tpu_custom_call" | custom-call | tf_op jit(solution)/shard_map/pallas_call | solution.py:233
  45.5 5.5 %all-to-all-start.2 = ((bf16[8,128,128]{2,1,0:T(8,128)(2,1)}), bf16[8,128,128]{2,1,0:T(8,128)(2,1)S(1)}, u32[]{:S(2)}, u32[]{:S(2)}) async-start(bf16[8,128,128]{2,1,0:T(8,128)(2,1)} %shard_map.101), calls=%async_computation.2 | async-start | bytes 524288 | tf_op jit(solution)/shard_map/all_to_all | solution.py:256
  51.7 5.2 %all-to-all-done.2 = bf16[8,128,128]{2,1,0:T(8,128)(2,1)S(1)} async-done(((bf16[8,128,128]{2,1,0:T(8,128)(2,1)}), bf16[8,128,128]{2,1,0:T(8,128)(2,1)S(1)}, u32[]{:S(2)}, u32[]{:S(2)}) %all-to-all-start.2) | async-done | bytes 262176 | tf_op jit(solution)/shard_map/all_to_all | solution.py:256
  57.1 0.6 %maximum_bitcast_fusion.1 = bf16[1,1,2,128,128]{4,3,2,1,0:T(8,128)(2,1)} fusion(bf16[1,128,128]{2,1,0:T(8,128)(2,1)S(1)} %fusion.1, bf16[1,128,128]{2,1,0:T(8,128)(2,1)S(1)} %bitcast.69), kind=kLoop, calls=%fused_computation.10 | loop fusion | flops 32768 | bytes 131072 | tf_op jit(solution)/shard_map/broadcast_in_dim | solution.py:320
  (24 shorter events, 2.1 us)
Async XLA Ops:
  1.5 16.8 %collective-permute-start.2 = (bf16[3,40,128,128]{3,2,1,0:T(8,128)(2,1)}, bf16[3,40,128,128]{3,2,1,0:T(8,128)(2,1)}, u32[]{:S(2)}, u32[]{:S(2)}) collective-permute-start(bf16[3,40,128,128]{3,2,1,0:T(8,128)(2,1)} %bitcast.71), channel_id=1, source_target_pairs={{0,1},{1,0},{2,3},{3,2},{4,5},{5,4},{6,7},{7,6},{8,9},{9,8},{10,11... | collective-permute-start | bytes 11796488 | tf_op jit(solution)/shard_map/ppermute | solution.py:41
  2.0 5.0 %collective-permute-start = (bf16[128,128]{1,0:T(8,128)(2,1)S(1)}, bf16[128,128]{1,0:T(8,128)(2,1)S(1)}, u32[]{:S(2)}, u32[]{:S(2)}) collective-permute-start(bf16[128,128]{1,0:T(8,128)(2,1)S(1)} %convolution_convert_fusion.3.refs_2_.refs_4_), channel_id=1, source_target_pairs={{0,2},{1,3},{2,0},{3,1},{4,6},{5,7},{6,4},{7,5},{8,10},{9,11},{10,... | collective-permute-start | bytes 98312 | tf_op jit(solution)/shard_map/ppermute | solution.py:36
  8.0 13.6 %all-to-all-start = ((bf16[8,128,128]{2,1,0:T(8,128)(2,1)}), bf16[8,128,128]{2,1,0:T(8,128)(2,1)S(1)}, u32[]{:S(2)}, u32[]{:S(2)}) async-start(bf16[8,128,128]{2,1,0:T(8,128)(2,1)} %shard_map.96), calls=%async_computation | async-start | bytes 524288 | tf_op jit(solution)/shard_map/all_to_all | solution.py:256
  15.0 6.6 %copy-start = (bf16[1,1,1,2,128,128]{5,4,3,2,1,0:T(8,128)(2,1)S(1)}, bf16[1,1,1,2,128,128]{5,4,3,2,1,0:T(8,128)(2,1)}, u32[]{:S(2)}) copy-start(bf16[1,1,1,2,128,128]{5,4,3,2,1,0:T(8,128)(2,1)} %param.12) | copy-start | bytes 196612
  15.0 6.6 %copy-start.1 = (bf16[1,1,1,2,128,128]{5,4,3,2,1,0:T(8,128)(2,1)S(1)}, bf16[1,1,1,2,128,128]{5,4,3,2,1,0:T(8,128)(2,1)}, u32[]{:S(2)}) copy-start(bf16[1,1,1,2,128,128]{5,4,3,2,1,0:T(8,128)(2,1)} %param.14) | copy-start | bytes 196612
  15.0 3.3 %collective-permute-start.4 = (bf16[128,128]{1,0:T(8,128)(2,1)S(1)}, bf16[128,128]{1,0:T(8,128)(2,1)S(1)}, u32[]{:S(2)}, u32[]{:S(2)}) collective-permute-start(bf16[128,128]{1,0:T(8,128)(2,1)S(1)} %convolution_convert_fusion.3.refs_2_.refs_4_), channel_id=1, source_target_pairs={{0,3},{1,2},{2,1},{3,0},{4,7},{5,6},{6,5},{7,4},{8,11},{9,10},{10,... | collective-permute-start | bytes 98312 | tf_op jit(solution)/shard_map/ppermute | solution.py:36
  15.0 3.3 %collective-permute-start.3 = (bf16[128,128]{1,0:T(8,128)(2,1)S(1)}, bf16[128,128]{1,0:T(8,128)(2,1)S(1)}, u32[]{:S(2)}, u32[]{:S(2)}) collective-permute-start(bf16[128,128]{1,0:T(8,128)(2,1)S(1)} %convolution_convert_fusion.3.refs_2_.refs_4_), channel_id=1, source_target_pairs={{0,1},{1,0},{2,3},{3,2},{4,5},{5,4},{6,7},{7,6},{8,9},{9,8},{10,11... | collective-permute-start | bytes 98312 | tf_op jit(solution)/shard_map/ppermute | solution.py:36
  16.0 1.2 %collective-permute-start.1 = (s32[8,128]{1,0:T(8,128)S(1)}, s32[8,128]{1,0:T(8,128)S(1)}, u32[]{:S(2)}, u32[]{:S(2)}) collective-permute-start(s32[8,128]{1,0:T(8,128)S(1)} %get-tuple-element.30), channel_id=1, source_target_pairs={{0,1},{1,0},{2,3},{3,2},{4,5},{5,4},{6,7},{7,6},{8,9},{9,8},{10,11... | collective-permute-start | bytes 12296 | tf_op jit(solution)/shard_map/ppermute | solution.py:41
  21.7 3.4 %collective-permute-start.7 = (bf16[128,128]{1,0:T(8,128)(2,1)S(1)}, bf16[128,128]{1,0:T(8,128)(2,1)S(1)}, u32[]{:S(2)}, u32[]{:S(2)}) collective-permute-start(bf16[128,128]{1,0:T(8,128)(2,1)S(1)} %fusion.refs_4_.refs_8_), channel_id=1, source_target_pairs={{0,3},{1,2},{2,1},{3,0},{4,7},{5,6},{6,5},{7,4},{8,11},{9,10},{10,... | collective-permute-start | bytes 98312 | tf_op jit(solution)/shard_map/ppermute | solution.py:36
  21.8 3.3 %collective-permute-start.6 = (bf16[128,128]{1,0:T(8,128)(2,1)S(1)}, bf16[128,128]{1,0:T(8,128)(2,1)S(1)}, u32[]{:S(2)}, u32[]{:S(2)}) collective-permute-start(bf16[128,128]{1,0:T(8,128)(2,1)S(1)} %fusion.refs_4_.refs_8_), channel_id=1, source_target_pairs={{0,1},{1,0},{2,3},{3,2},{4,5},{5,4},{6,7},{7,6},{8,9},{9,8},{10,11... | collective-permute-start | bytes 98312 | tf_op jit(solution)/shard_map/ppermute | solution.py:36
  22.2 3.9 %collective-permute-start.5 = (bf16[128,128]{1,0:T(8,128)(2,1)S(1)}, bf16[128,128]{1,0:T(8,128)(2,1)S(1)}, u32[]{:S(2)}, u32[]{:S(2)}) collective-permute-start(bf16[128,128]{1,0:T(8,128)(2,1)S(1)} %fusion.refs_4_.refs_8_), channel_id=1, source_target_pairs={{0,2},{1,3},{2,0},{3,1},{4,6},{5,7},{6,4},{7,5},{8,10},{9,11},{10,... | collective-permute-start | bytes 98312 | tf_op jit(solution)/shard_map/ppermute | solution.py:36
  28.5 11.7 %all-to-all-start.1 = ((bf16[8,128,128]{2,1,0:T(8,128)(2,1)}), bf16[8,128,128]{2,1,0:T(8,128)(2,1)S(1)}, u32[]{:S(2)}, u32[]{:S(2)}) async-start(bf16[8,128,128]{2,1,0:T(8,128)(2,1)} %shard_map.98), calls=%async_computation.1 | async-start | bytes 524288 | tf_op jit(solution)/shard_map/all_to_all | solution.py:256
  33.8 6.4 %copy-start.2 = (bf16[1,1,2,128,128]{4,3,2,1,0:T(8,128)(2,1)S(1)}, bf16[1,1,2,128,128]{4,3,2,1,0:T(8,128)(2,1)}, u32[]{:S(2)}) copy-start(bf16[1,1,2,128,128]{4,3,2,1,0:T(8,128)(2,1)} %param.15) | copy-start | bytes 196612
  33.8 6.4 %copy-start.3 = (bf16[1,1,2,128,128]{4,3,2,1,0:T(8,128)(2,1)S(1)}, bf16[1,1,2,128,128]{4,3,2,1,0:T(8,128)(2,1)}, u32[]{:S(2)}) copy-start(bf16[1,1,2,128,128]{4,3,2,1,0:T(8,128)(2,1)} %param.13) | copy-start | bytes 196612
  40.3 3.9 %collective-permute-start.8 = (bf16[128,128]{1,0:T(8,128)(2,1)S(1)}, bf16[128,128]{1,0:T(8,128)(2,1)S(1)}, u32[]{:S(2)}, u32[]{:S(2)}) collective-permute-start(bf16[128,128]{1,0:T(8,128)(2,1)S(1)} %bitcast.65), channel_id=1, source_target_pairs={{0,2},{1,3},{2,0},{3,1},{4,6},{5,7},{6,4},{7,5},{8,10},{9,11},{10,... | collective-permute-start | bytes 98312 | tf_op jit(solution)/shard_map/ppermute | solution.py:36
  45.5 11.4 %all-to-all-start.2 = ((bf16[8,128,128]{2,1,0:T(8,128)(2,1)}), bf16[8,128,128]{2,1,0:T(8,128)(2,1)S(1)}, u32[]{:S(2)}, u32[]{:S(2)}) async-start(bf16[8,128,128]{2,1,0:T(8,128)(2,1)} %shard_map.101), calls=%async_computation.2 | async-start | bytes 524288 | tf_op jit(solution)/shard_map/all_to_all | solution.py:256

commit v2 on v1

--- a/solution.py
+++ b/solution.py
@@ -11,8 +11,7 @@
 batch = 4
 field = 10
 field_mask = (1 << field) - 1
-pairs = ((0, 1), (0, 2), (0, 3), (1, 2), (1, 3), (2, 3), (2, 3))
-count_row = len(pairs)
+pairs = ((0, 1), (0, 2), (0, 3), (1, 2), (1, 2), (1, 3), (2, 3), (2, 3))
 params = pltpu.CompilerParams(vmem_limit_bytes=24 * 1024 * 1024)
 vmem = pl.BlockSpec(memory_space=pltpu.VMEM)
 smem = pl.BlockSpec(memory_space=pltpu.SMEM)
@@ -24,7 +23,7 @@
     cols = lax.axis_size("pcol")
     depth = lax.axis_size("zgrid")
     found = []
-    for k in range(cols):
+    for k in reversed(range(cols)):
         if k == 0 and layers == 0:
             found.append(value)
             continue
@@ -34,7 +33,7 @@
                 target = ((c - k) % cols) * depth + (z - layers) % depth
                 moves.append((c * depth + z, target))
         found.append(lax.ppermute(value, ("pcol", "zgrid"), moves))
-    return found
+    return found[::-1]
 
 
 def from_other_core(value):
@@ -60,19 +59,22 @@
         load.wait()
     me = lax.axis_index("pcol")
     spare = row_count << field
+    width = plan.shape[1]
     for level in range(3):
         first_list = pairs.index((level, level + 1))
         steps = 3 - level
-        lists = max(steps, 2)
+        lists = sum(pair[0] == level for pair in pairs)
 
         def one_slot(slot, found):
             target = targets[level, 0, slot]
             higher = [(target >= (level + j) * row_count).astype(jnp.int32) for j in range(1, steps)]
-            step = sum(higher) if higher else jnp.int32(0)
+            step = sum(higher, jnp.int32(0))
             row = target - (level + step) * row_count
             column = sources[level, 0, slot] - me
             column = jnp.where(column < 0, column + cols, column)
-            kind = step if steps > 1 else (column > 0).astype(jnp.int32)
+            kind = step
+            if lists > steps:
+                kind = step + ((step > 0) | (column > 0)).astype(jnp.int32)
             place = found[lists - 1]
             for j in range(lists - 1):
                 place = jnp.where(kind == j, found[j], place)
@@ -83,8 +85,8 @@
 
         found = lax.fori_loop(0, counts[level], one_slot, (jnp.int32(0),) * lists)
         for j in range(lists):
-            plan[count_row, first_list + j] = found[j]
-            kept[count_row, first_list + j] = found[j]
+            plan[first_list + j, width - 1] = found[j]
+            kept[first_list + j, width - 1] = found[j]
             for extra in range(slot_group):
                 plan[first_list + j, found[j] + extra] = spare
                 kept[first_list + j, found[j] + extra] = spare
@@ -92,12 +94,12 @@
 
 
 def make_plan(row_count, cols, sources, targets, counts, blocks):
-    width = -(-(sources.shape[-1] + slot_group) // 128) * 128
+    width = -(-(sources.shape[-1] + slot_group + 1) // 128) * 128
     return pl.pallas_call(
         functools.partial(plan_kernel, row_count, cols),
         out_shape=[
-            jax.ShapeDtypeStruct((8, width), jnp.int32),
-            pltpu.SMEM((8, width), jnp.int32),
+            jax.ShapeDtypeStruct((len(pairs), width), jnp.int32),
+            pltpu.SMEM((len(pairs), width), jnp.int32),
             pltpu.VMEM(blocks.shape[1:], blocks.dtype),
         ],
         in_specs=[hbm] * 4,
@@ -184,7 +186,7 @@
                     total[lax.shift_right_logical(entry, field) & field_mask] += product
             return unused
 
-        live = plans[layer][count_row, pair]
+        live = plans[layer][pair, plans[layer].shape[1] - 1]
         lax.fori_loop(0, (live + slot_group - 1) // slot_group, one_group, 0)
 
     if out.dtype == jnp.bfloat16:
@@ -293,13 +295,18 @@
     one_own = sibling_values(level_one, 0)
     one_other = sibling_values(level_one, 1)
 
+    resident = {(0, 1): staged}
+    second, resident[(1, 1)] = update(
+        [(3, 0, 0)], plans, both, [[level_one] * cols], second, row_count, False, resident, (1, 1)
+    )
     send = update(
-        [(3, 0, 0), (3, 1, 1)], plans, both, [one_own, one_other], second, row_count, True,
-        {(0, 1): staged}, None,
-    )
+        [(4, 0, 0), (3, 1, 1), (4, 1, 1)], plans, both, [one_own, one_other], second, row_count,
+        True, resident, None,
+    )
+    send, one_own, one_other = lax.optimization_barrier((send, one_own, one_other))
     received = exchange(send)
     third, staged = update(
-        [(2, 0, 0), (2, 1, 1), (4, 0, 2), (4, 1, 3)], plans, both,
+        [(2, 0, 0), (2, 1, 1), (5, 0, 2), (5, 1, 3)], plans, both,
         [zero_own, zero_other, one_own, one_other], None, row_count, False, {}, (0, 2),
     )
     received, third, staged = lax.optimization_barrier((received, third, staged))
@@ -308,11 +315,11 @@
 
     resident = {(0, 2): staged}
     third, resident[(1, 2)] = update(
-        [(5, 0, 0), (5, 1, 0)], plans, both, [[level_two] * cols], third, row_count, False, resident,
+        [(6, 0, 0), (6, 1, 0)], plans, both, [[level_two] * cols], third, row_count, False, resident,
         (1, 2),
     )
     send = update(
-        [(6, 0, 0), (6, 1, 0)], plans, both, [two_own], third, row_count, True, resident, None
+        [(7, 0, 0), (7, 1, 0)], plans, both, [two_own], third, row_count, True, resident, None
     )
     send, level_zero, level_one = lax.optimization_barrier((send, level_zero, level_one))
     level_three = reduced_solve(exchange(send), right_top[1], factor_top[1])

time: 58.5 us -> 58.5 us (level)
  Pallas kernels: 13.4 us -> 15 us
  starting transfers between devices: 25.7 us -> 24.5 us
    pallas_call x6 -> x7, Pallas kernels: 11.1 us -> 12 us  [update(): pl.pallas_call(functools.partial(update_kernel, config), out_shape=outs,...]
    ppermute x7, waiting for transfers between devices: 4.33 us -> 3.39 us  [sibling_values(): found.append(lax.ppermute(value, ('pcol', 'zgrid'), moves))]
    ppermute x7, starting transfers between devices: 7.4 us -> 6.71 us  [sibling_values(): found.append(lax.ppermute(value, ('pcol', 'zgrid'), moves))]
    all_to_all x3, starting transfers between devices: 17.8 us -> 17.2 us  [exchange(): lax.all_to_all(send, 'prow', 0, 0, tiled=True, axis_index_groups=[order])]
    pallas_call x1, Pallas kernels: 2.35 us -> 2.96 us  [make_plan(): pl.pallas_call(functools.partial(plan_kernel, row_count, cols), out_shape...]
  transfers between devices with their start and end apart: 12 -> 12, of which waited for: 8 -> 8; matrix products, arithmetic and copies ran while one was open for 1% -> 1% of each run, Pallas kernels for 17% -> 21%
where the time goes in v2:
time: 58.5 us; the launch traced here: 57.6 us
  starting transfers between devices  24.5 us (42%)
  Pallas kernels  15 us (26%)
  waiting for transfers between devices  14.7 us (25%)
  other arithmetic  1.4 us (2%)
  matrix products  1.3 us (2%)
  between operations  0.76 us (1%)
    all_to_all x3, starting transfers between devices, exchange(): lax.all_to_all(send, 'prow', 0, 0, tiled=True, axis_index_groups=[order])  17.2 us
    pallas_call x7, Pallas kernels, update(): pl.pallas_call(functools.partial(update_kernel, config), out_shape=outs,...  12 us
    all_to_all x3, waiting for transfers between devices, exchange(): lax.all_to_all(send, 'prow', 0, 0, tiled=True, axis_index_groups=[order])  10.2 us
    ppermute x7, starting transfers between devices, sibling_values(): found.append(lax.ppermute(value, ('pcol', 'zgrid'), moves))  6.71 us
    ppermute x7, waiting for transfers between devices, sibling_values(): found.append(lax.ppermute(value, ('pcol', 'zgrid'), moves))  3.39 us
    pallas_call x1, Pallas kernels, make_plan(): pl.pallas_call(functools.partial(plan_kernel, row_count, cols), out_shape...  2.96 us
    dot_general x4, matrix products, solve_block(): jnp.dot(inverse, residual, preferred_element_type=jnp.float32)  1.3 us
  transfers between devices with their start and end apart: 12, of which 8 were waited for; matrix products, arithmetic and copies ran while one was open for 1% of the time, Pallas kernels for 21%

profile of v2, /device:TPU:0, one launch (start us, length us, event | category | flops | bytes accessed | tf_op | source)
XLA Modules:
  0.0 57.6 jit_solution(2841151884053726626)
XLA Ops:
  0.6 0.9 %convolution_convert_fusion.3.refs_2_.refs_4_ = bf16[128,128]{1,0:T(8,128)(2,1)S(1)} fusion(bf16[1,1,1,2,128,128]{5,4,3,2,1,0:T(8,128)(2,1)} %param.12, bf16[1,1,1,2,128,128]{5,4,3,2,1,0:T(8,128)(2,1)} %param.14), kind=kOutput, calls=%fused_computation.3 | convolution fusion | flops 4210688 | bytes 98304 | tf_op jit(solution)/shard_map/dot_general | solution.py:247
  2.0 2.6 %collective-permute-start = (bf16[128,128]{1,0:T(8,128)(2,1)S(1)}, bf16[128,128]{1,0:T(8,128)(2,1)S(1)}, u32[]{:S(2)}, u32[]{:S(2)}) collective-permute-start(bf16[128,128]{1,0:T(8,128)(2,1)S(1)} %convolution_convert_fusion.3.refs_2_.refs_4_), channel_id=1, source_target_pairs={{0,2},{1,3},{2,0},{3,1},{4,6},{5,7},{6,4},{7,5},{8,10},{9,11},{10,... | collective-permute-start | bytes 98312 | tf_op jit(solution)/shard_map/ppermute | solution.py:35
  4.6 3.0 %shard_map.95 = (s32[8,128]{1,0:T(8,128)S(1)}, s32[8,128]{1,0:T(8,128)S(4)}, bf16[40,128,128]{2,1,0:T(8,128)(2,1)S(1)}) custom-call(s32[3,1,40]{2,1,0:T(1,128)} %bitcast.80, s32[3,1,40]{2,1,0:T(1,128)} %bitcast.81, s32[3]{0:T(128)} %bitcast.82, bf16[3,40,128,128]{3,2,1,0:T(8,128)(2,1)} %bitcast.72), custom_call_target="tpu_custom_call" | custom-call | tf_op jit(solution)/shard_map/pallas_call | solution.py:98
  7.6 1.3 %shard_map.96 = bf16[8,128,128]{2,1,0:T(8,128)(2,1)} custom-call(s32[8,128]{1,0:T(8,128)S(4)} %get-tuple-element.33.refs_0_, bf16[3,40,128,128]{3,2,1,0:T(8,128)(2,1)} %bitcast.73, bf16[128,128]{1,0:T(8,128)(2,1)S(1)} %convolution_convert_fusion.3.refs_2_.refs_4_, bf16[128,128]{1,0:T(8,128)(2,1)S(1)} %collective-permute-done.refs_3_.refs_5_, ...), custom_call_target="tpu_custom_call" | custom-call | tf_op jit(solution)/shard_map/pallas_call | solution.py:235
  8.8 6.4 %all-to-all-start = ((bf16[8,128,128]{2,1,0:T(8,128)(2,1)}), bf16[8,128,128]{2,1,0:T(8,128)(2,1)S(1)}, u32[]{:S(2)}, u32[]{:S(2)}) async-start(bf16[8,128,128]{2,1,0:T(8,128)(2,1)} %shard_map.96), calls=%async_computation | async-start | bytes 524288 | tf_op jit(solution)/shard_map/all_to_all | solution.py:258
  15.2 0.8 %collective-permute-start.4 = (bf16[128,128]{1,0:T(8,128)(2,1)S(1)}, bf16[128,128]{1,0:T(8,128)(2,1)S(1)}, u32[]{:S(2)}, u32[]{:S(2)}) collective-permute-start(bf16[128,128]{1,0:T(8,128)(2,1)S(1)} %convolution_convert_fusion.3.refs_2_.refs_4_), channel_id=1, source_target_pairs={{0,3},{1,2},{2,1},{3,0},{4,7},{5,6},{6,5},{7,4},{8,11},{9,10},{10,... | collective-permute-start | bytes 98312 | tf_op jit(solution)/shard_map/ppermute | solution.py:35
  16.1 1.1 %collective-permute-done.1.refs_1_ = s32[8,128]{1,0:T(8,128)S(1)} collective-permute-done((s32[8,128]{1,0:T(8,128)S(1)}, s32[8,128]{1,0:T(8,128)S(1)}, u32[]{:S(2)}, u32[]{:S(2)}) %collective-permute-start.1) | collective-permute-done | bytes 4128 | tf_op jit(solution)/shard_map/ppermute | solution.py:40
  17.2 1.4 %collective-permute-done.4.refs_7_ = bf16[128,128]{1,0:T(8,128)(2,1)S(1)} collective-permute-done((bf16[128,128]{1,0:T(8,128)(2,1)S(1)}, bf16[128,128]{1,0:T(8,128)(2,1)S(1)}, u32[]{:S(2)}, u32[]{:S(2)}) %collective-permute-start.4) | collective-permute-done | bytes 32800 | tf_op jit(solution)/shard_map/ppermute | solution.py:35
  18.6 2.1 %shard_map.97 = (f32[8,128,128]{2,1,0:T(8,128)S(1)}, bf16[40,128,128]{2,1,0:T(8,128)(2,1)S(1)}, s32[8,128]{1,0:T(8,128)S(4)}) custom-call(s32[8,128]{1,0:T(8,128)S(4)} %get-tuple-element.33.refs_0_, s32[8,128]{1,0:T(8,128)S(1)} %collective-permute-done.1.refs_1_, bf16[3,40,128,128]{3,2,1,0:T(8,128)(2,1)} %bitcast.74, ...), custom_call_target="tpu_custom_call" | custom-call | tf_op jit(solution)/shard_map/pallas_call | solution.py:235
  20.8 0.7 %all-to-all-done = bf16[8,128,128]{2,1,0:T(8,128)(2,1)S(1)} async-done(((bf16[8,128,128]{2,1,0:T(8,128)(2,1)}), bf16[8,128,128]{2,1,0:T(8,128)(2,1)S(1)}, u32[]{:S(2)}, u32[]{:S(2)}) %all-to-all-start) | async-done | bytes 262176 | tf_op jit(solution)/shard_map/all_to_all | solution.py:258
  21.6 0.7 %collective-permute-start.5 = (bf16[128,128]{1,0:T(8,128)(2,1)S(1)}, bf16[128,128]{1,0:T(8,128)(2,1)S(1)}, u32[]{:S(2)}, u32[]{:S(2)}) collective-permute-start(bf16[128,128]{1,0:T(8,128)(2,1)S(1)} %fusion.refs_4_.refs_5_.refs_8_), channel_id=1, source_target_pairs={{0,2},{1,3},{2,0},{3,1},{4,6},{5,7},{6,4},{7,5},{8,10},{9,11},{10,... | collective-permute-start | bytes 98312 | tf_op jit(solution)/shard_map/ppermute | solution.py:35
  22.3 1.5 %collective-permute-start.7 = (bf16[128,128]{1,0:T(8,128)(2,1)S(1)}, bf16[128,128]{1,0:T(8,128)(2,1)S(1)}, u32[]{:S(2)}, u32[]{:S(2)}) collective-permute-start(bf16[128,128]{1,0:T(8,128)(2,1)S(1)} %fusion.refs_4_.refs_5_.refs_8_), channel_id=1, source_target_pairs={{0,3},{1,2},{2,1},{3,0},{4,7},{5,6},{6,5},{7,4},{8,11},{9,10},{10,... | collective-permute-start | bytes 98312 | tf_op jit(solution)/shard_map/ppermute | solution.py:35
  23.8 1.3 %shard_map.98 = (f32[8,128,128]{2,1,0:T(8,128)S(1)}, bf16[40,128,128]{2,1,0:T(8,128)(2,1)S(1)}) custom-call(s32[8,128]{1,0:T(8,128)S(4)} %get-tuple-element.33.refs_0_, s32[8,128]{1,0:T(8,128)S(4)} %get-tuple-element.40.refs_1_, bf16[3,40,128,128]{3,2,1,0:T(8,128)(2,1)} %bitcast.75, bf16[3,40,128,128]{3,2,1,0:T(8,128)(2,1)} %collective-permute-done.2.refs_3_, ...), custom_call_target="tpu_custom_call" | custom-call | tf_op jit(solution)/shard_map/pallas_call | solution.py:235
  25.1 0.7 %collective-permute-done.5.refs_5_.refs_9_ = bf16[128,128]{1,0:T(8,128)(2,1)S(1)} collective-permute-done((bf16[128,128]{1,0:T(8,128)(2,1)S(1)}, bf16[128,128]{1,0:T(8,128)(2,1)S(1)}, u32[]{:S(2)}, u32[]{:S(2)}) %collective-permute-start.5) | collective-permute-done | bytes 32800 | tf_op jit(solution)/shard_map/ppermute | solution.py:35
  25.9 1.3 %shard_map.99 = bf16[8,128,128]{2,1,0:T(8,128)(2,1)} custom-call(s32[8,128]{1,0:T(8,128)S(4)} %get-tuple-element.33.refs_0_, s32[8,128]{1,0:T(8,128)S(4)} %get-tuple-element.40.refs_1_, bf16[3,40,128,128]{3,2,1,0:T(8,128)(2,1)} %bitcast.76, bf16[3,40,128,128]{3,2,1,0:T(8,128)(2,1)} %collective-permute-done.2.refs_3_, ...), custom_call_target="tpu_custom_call" | custom-call | tf_op jit(solution)/shard_map/pallas_call | solution.py:235
  27.2 5.5 %all-to-all-start.1 = ((bf16[8,128,128]{2,1,0:T(8,128)(2,1)}), bf16[8,128,128]{2,1,0:T(8,128)(2,1)S(1)}, u32[]{:S(2)}, u32[]{:S(2)}) async-start(bf16[8,128,128]{2,1,0:T(8,128)(2,1)} %shard_map.99), calls=%async_computation.1 | async-start | bytes 524288 | tf_op jit(solution)/shard_map/all_to_all | solution.py:258
  32.7 3.0 %shard_map.100 = (f32[8,128,128]{2,1,0:T(8,128)S(1)}, bf16[40,128,128]{2,1,0:T(8,128)(2,1)S(1)}) custom-call(s32[8,128]{1,0:T(8,128)S(4)} %get-tuple-element.33.refs_0_, s32[8,128]{1,0:T(8,128)S(4)} %get-tuple-element.40.refs_1_, bf16[3,40,128,128]{3,2,1,0:T(8,128)(2,1)} %bitcast.77, bf16[3,40,128,128]{3,2,1,0:T(8,128)(2,1)} %collective-permute-done.2.refs_3_, ...), custom_call_target="tpu_custom_call" | custom-call | tf_op jit(solution)/shard_map/pallas_call | solution.py:235
  35.7 4.3 %all-to-all-done.1 = bf16[8,128,128]{2,1,0:T(8,128)(2,1)S(1)} async-done(((bf16[8,128,128]{2,1,0:T(8,128)(2,1)}), bf16[8,128,128]{2,1,0:T(8,128)(2,1)S(1)}, u32[]{:S(2)}, u32[]{:S(2)}) %all-to-all-start.1) | async-done | bytes 262176 | tf_op jit(solution)/shard_map/all_to_all | solution.py:258
  40.2 1.1 %collective-permute-start.8 = (bf16[128,128]{1,0:T(8,128)(2,1)S(1)}, bf16[128,128]{1,0:T(8,128)(2,1)S(1)}, u32[]{:S(2)}, u32[]{:S(2)}) collective-permute-start(bf16[128,128]{1,0:T(8,128)(2,1)S(1)} %bitcast.66), channel_id=1, source_target_pairs={{0,2},{1,3},{2,0},{3,1},{4,6},{5,7},{6,4},{7,5},{8,10},{9,11},{10,... | collective-permute-start | bytes 98312 | tf_op jit(solution)/shard_map/ppermute | solution.py:35
  41.3 1.6 %shard_map.101 = (f32[8,128,128]{2,1,0:T(8,128)S(1)}, bf16[40,128,128]{2,1,0:T(8,128)(2,1)S(1)}) custom-call(s32[8,128]{1,0:T(8,128)S(4)} %get-tuple-element.33.refs_0_, s32[8,128]{1,0:T(8,128)S(4)} %get-tuple-element.40.refs_1_, bf16[3,40,128,128]{3,2,1,0:T(8,128)(2,1)} %bitcast.78, bf16[3,40,128,128]{3,2,1,0:T(8,128)(2,1)} %collective-permute-done.2.refs_3_, ...), custom_call_target="tpu_custom_call" | custom-call | tf_op jit(solution)/shard_map/pallas_call | solution.py:235
  42.9 1.2 %collective-permute-done.8.refs_5_ = bf16[128,128]{1,0:T(8,128)(2,1)S(1)} collective-permute-done((bf16[128,128]{1,0:T(8,128)(2,1)S(1)}, bf16[128,128]{1,0:T(8,128)(2,1)S(1)}, u32[]{:S(2)}, u32[]{:S(2)}) %collective-permute-start.8) | collective-permute-done | bytes 32800 | tf_op jit(solution)/shard_map/ppermute | solution.py:35
  44.1 1.5 %shard_map.102 = bf16[8,128,128]{2,1,0:T(8,128)(2,1)} custom-call(s32[8,128]{1,0:T(8,128)S(4)} %get-tuple-element.33.refs_0_, s32[8,128]{1,0:T(8,128)S(4)} %get-tuple-element.40.refs_1_, bf16[3,40,128,128]{3,2,1,0:T(8,128)(2,1)} %bitcast.79, bf16[3,40,128,128]{3,2,1,0:T(8,128)(2,1)} %collective-permute-done.2.refs_3_, bf16[128,128]{1,0:T(8,128)(2,1)S(1)} %bitcast.69, ...), custom_call_target="tpu_custom_call" | custom-call | tf_op jit(solution)/shard_map/pallas_call | solution.py:235
  45.6 5.3 %all-to-all-start.2 = ((bf16[8,128,128]{2,1,0:T(8,128)(2,1)}), bf16[8,128,128]{2,1,0:T(8,128)(2,1)S(1)}, u32[]{:S(2)}, u32[]{:S(2)}) async-start(bf16[8,128,128]{2,1,0:T(8,128)(2,1)} %shard_map.102), calls=%async_computation.2 | async-start | bytes 524288 | tf_op jit(solution)/shard_map/all_to_all | solution.py:258
  51.6 5.2 %all-to-all-done.2 = bf16[8,128,128]{2,1,0:T(8,128)(2,1)S(1)} async-done(((bf16[8,128,128]{2,1,0:T(8,128)(2,1)}), bf16[8,128,128]{2,1,0:T(8,128)(2,1)S(1)}, u32[]{:S(2)}, u32[]{:S(2)}) %all-to-all-start.2) | async-done | bytes 262176 | tf_op jit(solution)/shard_map/all_to_all | solution.py:258
  (25 shorter events, 2.5 us)
Async XLA Ops:
  1.5 17.1 %collective-permute-start.2 = (bf16[3,40,128,128]{3,2,1,0:T(8,128)(2,1)}, bf16[3,40,128,128]{3,2,1,0:T(8,128)(2,1)}, u32[]{:S(2)}, u32[]{:S(2)}) collective-permute-start(bf16[3,40,128,128]{3,2,1,0:T(8,128)(2,1)} %bitcast.71), channel_id=1, source_target_pairs={{0,1},{1,0},{2,3},{3,2},{4,5},{5,4},{6,7},{7,6},{8,9},{9,8},{10,11... | collective-permute-start | bytes 11796488 | tf_op jit(solution)/shard_map/ppermute | solution.py:40
  2.0 5.6 %collective-permute-start = (bf16[128,128]{1,0:T(8,128)(2,1)S(1)}, bf16[128,128]{1,0:T(8,128)(2,1)S(1)}, u32[]{:S(2)}, u32[]{:S(2)}) collective-permute-start(bf16[128,128]{1,0:T(8,128)(2,1)S(1)} %convolution_convert_fusion.3.refs_2_.refs_4_), channel_id=1, source_target_pairs={{0,2},{1,3},{2,0},{3,1},{4,6},{5,7},{6,4},{7,5},{8,10},{9,11},{10,... | collective-permute-start | bytes 98312 | tf_op jit(solution)/shard_map/ppermute | solution.py:35
  8.8 12.6 %all-to-all-start = ((bf16[8,128,128]{2,1,0:T(8,128)(2,1)}), bf16[8,128,128]{2,1,0:T(8,128)(2,1)S(1)}, u32[]{:S(2)}, u32[]{:S(2)}) async-start(bf16[8,128,128]{2,1,0:T(8,128)(2,1)} %shard_map.96), calls=%async_computation | async-start | bytes 524288 | tf_op jit(solution)/shard_map/all_to_all | solution.py:258
  15.2 6.3 %copy-start = (bf16[1,1,1,2,128,128]{5,4,3,2,1,0:T(8,128)(2,1)S(1)}, bf16[1,1,1,2,128,128]{5,4,3,2,1,0:T(8,128)(2,1)}, u32[]{:S(2)}) copy-start(bf16[1,1,1,2,128,128]{5,4,3,2,1,0:T(8,128)(2,1)} %param.12) | copy-start | bytes 196612
  15.2 6.3 %copy-start.1 = (bf16[1,1,1,2,128,128]{5,4,3,2,1,0:T(8,128)(2,1)S(1)}, bf16[1,1,1,2,128,128]{5,4,3,2,1,0:T(8,128)(2,1)}, u32[]{:S(2)}) copy-start(bf16[1,1,1,2,128,128]{5,4,3,2,1,0:T(8,128)(2,1)} %param.14) | copy-start | bytes 196612
  15.2 2.0 %collective-permute-start.3 = (bf16[128,128]{1,0:T(8,128)(2,1)S(1)}, bf16[128,128]{1,0:T(8,128)(2,1)S(1)}, u32[]{:S(2)}, u32[]{:S(2)}) collective-permute-start(bf16[128,128]{1,0:T(8,128)(2,1)S(1)} %convolution_convert_fusion.3.refs_2_.refs_4_), channel_id=1, source_target_pairs={{0,1},{1,0},{2,3},{3,2},{4,5},{5,4},{6,7},{7,6},{8,9},{9,8},{10,11... | collective-permute-start | bytes 98312 | tf_op jit(solution)/shard_map/ppermute | solution.py:35
  15.2 3.4 %collective-permute-start.4 = (bf16[128,128]{1,0:T(8,128)(2,1)S(1)}, bf16[128,128]{1,0:T(8,128)(2,1)S(1)}, u32[]{:S(2)}, u32[]{:S(2)}) collective-permute-start(bf16[128,128]{1,0:T(8,128)(2,1)S(1)} %convolution_convert_fusion.3.refs_2_.refs_4_), channel_id=1, source_target_pairs={{0,3},{1,2},{2,1},{3,0},{4,7},{5,6},{6,5},{7,4},{8,11},{9,10},{10,... | collective-permute-start | bytes 98312 | tf_op jit(solution)/shard_map/ppermute | solution.py:35
  16.0 1.2 %collective-permute-start.1 = (s32[8,128]{1,0:T(8,128)S(1)}, s32[8,128]{1,0:T(8,128)S(1)}, u32[]{:S(2)}, u32[]{:S(2)}) collective-permute-start(s32[8,128]{1,0:T(8,128)S(1)} %get-tuple-element.37), channel_id=1, source_target_pairs={{0,1},{1,0},{2,3},{3,2},{4,5},{5,4},{6,7},{7,6},{8,9},{9,8},{10,11... | collective-permute-start | bytes 12296 | tf_op jit(solution)/shard_map/ppermute | solution.py:40
  21.6 4.2 %collective-permute-start.5 = (bf16[128,128]{1,0:T(8,128)(2,1)S(1)}, bf16[128,128]{1,0:T(8,128)(2,1)S(1)}, u32[]{:S(2)}, u32[]{:S(2)}) collective-permute-start(bf16[128,128]{1,0:T(8,128)(2,1)S(1)} %fusion.refs_4_.refs_5_.refs_8_), channel_id=1, source_target_pairs={{0,2},{1,3},{2,0},{3,1},{4,6},{5,7},{6,4},{7,5},{8,10},{9,11},{10,... | collective-permute-start | bytes 98312 | tf_op jit(solution)/shard_map/ppermute | solution.py:35
  22.3 3.5 %collective-permute-start.6 = (bf16[128,128]{1,0:T(8,128)(2,1)S(1)}, bf16[128,128]{1,0:T(8,128)(2,1)S(1)}, u32[]{:S(2)}, u32[]{:S(2)}) collective-permute-start(bf16[128,128]{1,0:T(8,128)(2,1)S(1)} %fusion.refs_4_.refs_5_.refs_8_), channel_id=1, source_target_pairs={{0,1},{1,0},{2,3},{3,2},{4,5},{5,4},{6,7},{7,6},{8,9},{9,8},{10,11... | collective-permute-start | bytes 98312 | tf_op jit(solution)/shard_map/ppermute | solution.py:35
  22.3 3.6 %collective-permute-start.7 = (bf16[128,128]{1,0:T(8,128)(2,1)S(1)}, bf16[128,128]{1,0:T(8,128)(2,1)S(1)}, u32[]{:S(2)}, u32[]{:S(2)}) collective-permute-start(bf16[128,128]{1,0:T(8,128)(2,1)S(1)} %fusion.refs_4_.refs_5_.refs_8_), channel_id=1, source_target_pairs={{0,3},{1,2},{2,1},{3,0},{4,7},{5,6},{6,5},{7,4},{8,11},{9,10},{10,... | collective-permute-start | bytes 98312 | tf_op jit(solution)/shard_map/ppermute | solution.py:35
  27.2 12.8 %all-to-all-start.1 = ((bf16[8,128,128]{2,1,0:T(8,128)(2,1)}), bf16[8,128,128]{2,1,0:T(8,128)(2,1)S(1)}, u32[]{:S(2)}, u32[]{:S(2)}) async-start(bf16[8,128,128]{2,1,0:T(8,128)(2,1)} %shard_map.99), calls=%async_computation.1 | async-start | bytes 524288 | tf_op jit(solution)/shard_map/all_to_all | solution.py:258
  32.7 7.3 %copy-start.2 = (bf16[1,1,2,128,128]{4,3,2,1,0:T(8,128)(2,1)S(1)}, bf16[1,1,2,128,128]{4,3,2,1,0:T(8,128)(2,1)}, u32[]{:S(2)}) copy-start(bf16[1,1,2,128,128]{4,3,2,1,0:T(8,128)(2,1)} %param.15) | copy-start | bytes 196612
  32.7 7.3 %copy-start.3 = (bf16[1,1,2,128,128]{4,3,2,1,0:T(8,128)(2,1)S(1)}, bf16[1,1,2,128,128]{4,3,2,1,0:T(8,128)(2,1)}, u32[]{:S(2)}) copy-start(bf16[1,1,2,128,128]{4,3,2,1,0:T(8,128)(2,1)} %param.13) | copy-start | bytes 196612
  40.2 3.9 %collective-permute-start.8 = (bf16[128,128]{1,0:T(8,128)(2,1)S(1)}, bf16[128,128]{1,0:T(8,128)(2,1)S(1)}, u32[]{:S(2)}, u32[]{:S(2)}) collective-permute-start(bf16[128,128]{1,0:T(8,128)(2,1)S(1)} %bitcast.66), channel_id=1, source_target_pairs={{0,2},{1,3},{2,0},{3,1},{4,6},{5,7},{6,4},{7,5},{8,10},{9,11},{10,... | collective-permute-start | bytes 98312 | tf_op jit(solution)/shard_map/ppermute | solution.py:35
  45.6 11.2 %all-to-all-start.2 = ((bf16[8,128,128]{2,1,0:T(8,128)(2,1)}), bf16[8,128,128]{2,1,0:T(8,128)(2,1)S(1)}, u32[]{:S(2)}, u32[]{:S(2)}) async-start(bf16[8,128,128]{2,1,0:T(8,128)(2,1)} %shard_map.102), calls=%async_computation.2 | async-start | bytes 524288 | tf_op jit(solution)/shard_map/all_to_all | solution.py:258

commit v3 on v2

--- a/solution.py
+++ b/solution.py
@@ -114,6 +114,28 @@
     )(in_hbm(sources), in_hbm(targets), in_hbm(counts), blocks)
 
 
+def low_lanes(value):
+    return lax.broadcasted_iota(jnp.int32, value.shape, 1) < value.shape[1] // 2
+
+
+def turned(value):
+    return pltpu.roll(value, value.shape[1] // 2, 1)
+
+
+def half_first(value):
+    return jnp.where(lax.axis_index("zgrid") == 0, value, turned(value))
+
+
+def packed(value):
+    half = value.shape[0] // 2
+    upper = value[:half]
+    return jnp.where(low_lanes(upper), upper, turned(value[half:]))
+
+
+def unpacked(value):
+    return jnp.concatenate([value, turned(value)], axis=0)
+
+
 def exchange_order(row_count):
     return [(row + row_count // 2) % row_count for row in range(row_count)]
 
@@ -124,7 +146,7 @@
 
 
 def update_kernel(config, *refs):
-    lists, layer_count, groups_of_solutions, cols, row_count, resident, stages, carries, keeps_plan = config
+    lists, layer_count, groups_of_solutions, cols, row_count, resident, stages, carries, keeps_plan, form = config
     refs = list(refs)
     plans_in = [refs.pop(0) for _ in range(layer_count)]
     blocks = [refs.pop(0) for _ in range(layer_count)]
@@ -157,7 +179,10 @@
         loads[stages].start()
 
     for j, solution_ref in enumerate(solutions):
-        chosen[j] = solution_ref[...]
+        if solution_ref.shape == chosen.shape[1:]:
+            chosen[j] = solution_ref[...]
+        else:
+            chosen[j] = unpacked(solution_ref[...].astype(jnp.float32)).astype(jnp.bfloat16)
     if carries:
         total[:row_count] = total_in[...]
     else:
@@ -189,20 +214,24 @@
         live = plans[layer][pair, plans[layer].shape[1] - 1]
         lax.fori_loop(0, (live + slot_group - 1) // slot_group, one_group, 0)
 
-    if out.dtype == jnp.bfloat16:
+    if form == "summed":
+        out[...] = total[:row_count]
+    elif form == "turned":
+        for row in range(row_count):
+            out[row] = half_first(total[row])
+    else:
         for k, row in enumerate(exchange_order(row_count)):
-            out[k] = total[row].astype(jnp.bfloat16)
-    else:
-        out[...] = total[:row_count]
+            value = half_first(total[row]) if form == "half" else total[row]
+            out[k] = (value if form == "whole" else packed(value)).astype(jnp.bfloat16)
     for load in loads.values():
         load.wait()
 
 
 def update(
-    lists, plans, blocks, solution_groups, total_in, row_count, sends, resident, stages, keeps_plan=False
+    lists, plans, blocks, solution_groups, total_in, row_count, form, resident, stages, keeps_plan=False
 ):
     cols = len(solution_groups[0])
-    width, sides = solution_groups[0][0].shape
+    width, sides = blocks[0].shape[-1], solution_groups[0][0].shape[-1]
     solutions = [part for group in solution_groups for part in group]
     operands = plans + blocks + solutions
     specs = [smem] * len(plans) + [hbm] * len(blocks) + [vmem] * len(solutions)
@@ -212,7 +241,12 @@
             specs.append(vmem)
     fetched = fetched_levels(lists, tuple(resident) + ((stages,) if stages else ()))
     shape = (row_count, width, sides)
-    outs = [pltpu.VMEM(shape, jnp.bfloat16) if sends else jax.ShapeDtypeStruct(shape, jnp.float32)]
+    if form in ("half", "rest"):
+        shape = (row_count, width // 2, sides)
+    if form in ("summed", "turned"):
+        outs = [jax.ShapeDtypeStruct(shape, jnp.float32)]
+    else:
+        outs = [pltpu.VMEM(shape, jnp.bfloat16)]
     if stages:
         outs.append(pltpu.VMEM(blocks[0].shape[1:], blocks[0].dtype))
     places = [vmem] * len(outs)
@@ -222,7 +256,7 @@
         places.append(smem)
     config = (
         lists, len(plans), len(solution_groups), cols, row_count, tuple(resident), stages,
-        total_in is not None, keeps_plan,
+        total_in is not None, keeps_plan, form,
     )
     scratch = [
         pltpu.VMEM((len(solutions), width, sides), jnp.bfloat16),
@@ -243,6 +277,54 @@
     return found if len(outs) > 1 else found[0]
 
 
+def half_solve_kernel(level, received, given, inverse, *refs):
+    incoming = received[0].astype(jnp.float32)
+    for row in range(1, received.shape[0]):
+        incoming = incoming + received[row].astype(jnp.float32)
+    right = half_first(given[level].astype(jnp.float32))
+    residual = (right - unpacked(incoming)).astype(jnp.bfloat16)
+    found = jnp.dot(inverse[level], residual, preferred_element_type=jnp.float32)
+    found = packed(found).astype(jnp.bfloat16)
+    if len(refs) == 1:
+        refs[0][...] = found
+    else:
+        earlier, out = refs
+        out[0] = earlier[...]
+        out[1] = found
+
+
+def half_solve(level, received, given, inverse, earlier):
+    shape = received.shape[1:]
+    operands = [received, given, inverse] + ([] if earlier is None else [earlier])
+    return pl.pallas_call(
+        functools.partial(half_solve_kernel, level),
+        out_shape=jax.ShapeDtypeStruct(shape if earlier is None else (2,) + shape, jnp.bfloat16),
+        in_specs=[vmem] * len(operands),
+        out_specs=vmem,
+        compiler_params=params,
+    )(*operands)
+
+
+def join_kernel(own, other, out):
+    first_core = lax.axis_index("zgrid") == 0
+    for level in range(own.shape[0]):
+        mine, theirs = own[level].astype(jnp.float32), other[level].astype(jnp.float32)
+        first = unpacked(jnp.where(first_core, mine, theirs))
+        second = unpacked(jnp.where(first_core, theirs, mine))
+        out[0, 0, level] = jnp.where(low_lanes(first), first, turned(second)).astype(jnp.bfloat16)
+
+
+def join_halves(own, other):
+    levels, half, sides = own.shape
+    return pl.pallas_call(
+        join_kernel,
+        out_shape=jax.ShapeDtypeStruct((1, 1, levels, 2 * half, sides), jnp.bfloat16),
+        in_specs=[vmem, vmem],
+        out_specs=vmem,
+        compiler_params=params,
+    )(own, other)
+
+
 def solve_block(inverse, residual):
     return jnp.dot(inverse, residual, preferred_element_type=jnp.float32).astype(jnp.bfloat16)
 
@@ -280,14 +362,14 @@
     both = [block_own, in_hbm(from_other_core(block_sent))]
 
     send = update(
-        [(0, 0, 0)], [own_plan], both[:1], [zero_own], None, row_count, True, {(0, 0): staged}, None
+        [(0, 0, 0)], [own_plan], both[:1], [zero_own], None, row_count, "whole", {(0, 0): staged}, None
     )
     send, zero_sent, plan_sent = lax.optimization_barrier((send, level_zero, plan))
     received = exchange(send)
     zero_other = sibling_values(zero_sent, 1)
     plans = [own_plan, from_other_core(plan_sent)]
     second, staged, plans[1] = update(
-        [(1, 0, 0), (1, 1, 1)], plans, both, [zero_own, zero_other], None, row_count, False,
+        [(1, 0, 0), (1, 1, 1)], plans, both, [zero_own, zero_other], None, row_count, "summed",
         {}, (0, 1), True,
     )
     received, second, staged = lax.optimization_barrier((received, second, staged))
@@ -297,34 +379,34 @@
 
     resident = {(0, 1): staged}
     second, resident[(1, 1)] = update(
-        [(3, 0, 0)], plans, both, [[level_one] * cols], second, row_count, False, resident, (1, 1)
+        [(3, 0, 0)], plans, both, [[level_one] * cols], second, row_count, "summed", resident, (1, 1)
     )
     send = update(
         [(4, 0, 0), (3, 1, 1), (4, 1, 1)], plans, both, [one_own, one_other], second, row_count,
-        True, resident, None,
+        "half", resident, None,
     )
     send, one_own, one_other = lax.optimization_barrier((send, one_own, one_other))
     received = exchange(send)
     third, staged = update(
         [(2, 0, 0), (2, 1, 1), (5, 0, 2), (5, 1, 3)], plans, both,
-        [zero_own, zero_other, one_own, one_other], None, row_count, False, {}, (0, 2),
+        [zero_own, zero_other, one_own, one_other], None, row_count, "turned", {}, (0, 2),
     )
     received, third, staged = lax.optimization_barrier((received, third, staged))
-    level_two = reduced_solve(received, right_top[0], factor_top[0])
+    level_two = half_solve(0, received, right_top, factor_top, None)
     two_own = sibling_values(level_two, 0)
 
     resident = {(0, 2): staged}
     third, resident[(1, 2)] = update(
-        [(6, 0, 0), (6, 1, 0)], plans, both, [[level_two] * cols], third, row_count, False, resident,
-        (1, 2),
+        [(6, 0, 0), (6, 1, 0)], plans, both, [[level_two] * cols], third, row_count, "summed",
+        resident, (1, 2),
     )
     send = update(
-        [(7, 0, 0), (7, 1, 0)], plans, both, [two_own], third, row_count, True, resident, None
+        [(7, 0, 0), (7, 1, 0)], plans, both, [two_own], third, row_count, "rest", resident, None
     )
     send, level_zero, level_one = lax.optimization_barrier((send, level_zero, level_one))
-    level_three = reduced_solve(exchange(send), right_top[1], factor_top[1])
+    halves = half_solve(1, exchange(send), right_top, factor_top, level_two)
+    solved_top = join_halves(halves, from_other_core(halves))
     solved_sub = jnp.stack([level_zero, level_one])[None, None, None]
-    solved_top = jnp.stack([level_two, level_three])[None, None]
     return (solved_sub, solved_top)
 
 

time: 58.5 us -> 55.5 us (0.949); the launches traced: 57.6 us -> 55.2 us
  blocking collectives: 0 us -> 8.98 us
  waiting for transfers between devices: 14.7 us -> 8.19 us
  starting transfers between devices: 24.5 us -> 20.3 us
  other arithmetic: 1.4 us -> 0.68 us
    all_to_all x0 -> x1, blocking collectives: none -> 8.98 us  [exchange(): lax.all_to_all(send, 'prow', 0, 0, tiled=True, axis_index_groups=[order])]
    all_to_all x3 -> x2, waiting for transfers between devices: 10.2 us -> 3.94 us  [exchange(): lax.all_to_all(send, 'prow', 0, 0, tiled=True, axis_index_groups=[order])]
    all_to_all x3 -> x2, starting transfers between devices: 17.2 us -> 12.1 us  [exchange(): lax.all_to_all(send, 'prow', 0, 0, tiled=True, axis_index_groups=[order])]
    pallas_call x0 -> x3, Pallas kernels: none -> 1.34 us  [the longest x1 0.78 us: join_halves(): pl.pallas_call(join_kernel, out_shape=jax.ShapeDtypeStruct((1, 1, levels,...]
    ppermute x7, starting transfers between devices: 6.71 us -> 7.6 us  [sibling_values(): found.append(lax.ppermute(value, ('pcol', 'zgrid'), moves))]
    pallas_call x1, Pallas kernels: 2.96 us -> 2.08 us  [make_plan(): pl.pallas_call(functools.partial(plan_kernel, row_count, cols), out_shape...]
    ppermute x7, waiting for transfers between devices: 3.39 us -> 2.6 us  [sibling_values(): found.append(lax.ppermute(value, ('pcol', 'zgrid'), moves))]
    broadcast_in_dim x1 -> x0, other arithmetic: 0.65 us -> none  [local(): solved_top = jnp.stack([level_two, level_three])[None, None]]
where the time goes in v3:
time: 55.5 us; the launch traced here: 55.2 us
  starting transfers between devices  20.3 us (37%)
  Pallas kernels  15.3 us (28%)
  blocking collectives  8.98 us (16%)
  waiting for transfers between devices  8.19 us (15%)
  matrix products  1.03 us (2%)
  between operations  0.74 us (1%)
  other arithmetic  0.68 us (1%)
    all_to_all x2, starting transfers between devices, exchange(): lax.all_to_all(send, 'prow', 0, 0, tiled=True, axis_index_groups=[order])  12.1 us
    pallas_call x7, Pallas kernels, update(): pl.pallas_call(functools.partial(update_kernel, config), out_shape=outs,...  11.8 us
    all_to_all x1, blocking collectives, exchange(): lax.all_to_all(send, 'prow', 0, 0, tiled=True, axis_index_groups=[order])  8.98 us
    ppermute x7, starting transfers between devices, sibling_values(): found.append(lax.ppermute(value, ('pcol', 'zgrid'), moves))  7.6 us
    all_to_all x2, waiting for transfers between devices, exchange(): lax.all_to_all(send, 'prow', 0, 0, tiled=True, axis_index_groups=[order])  3.94 us
    ppermute x7, waiting for transfers between devices, sibling_values(): found.append(lax.ppermute(value, ('pcol', 'zgrid'), moves))  2.6 us
    pallas_call x1, Pallas kernels, make_plan(): pl.pallas_call(functools.partial(plan_kernel, row_count, cols), out_shape...  2.08 us
    ppermute x3, waiting for transfers between devices, from_other_core(): return lax.ppermute(value, 'zgrid', [(0, 1), (1, 0)])  1.65 us
  transfers between devices with their start and end apart: 12, of which 8 were waited for; matrix products, arithmetic and copies ran while one was open for 1% of the time, Pallas kernels for 21%

profile of v3, /device:TPU:0, one launch (start us, length us, event | category | flops | bytes accessed | tf_op | source)
XLA Modules:
  0.0 55.2 jit_solution(6068487743761107192)
XLA Ops:
  0.6 0.9 %convolution_convert_fusion.1.refs_2_.refs_4_ = bf16[128,128]{1,0:T(8,128)(2,1)S(1)} fusion(bf16[1,1,1,2,128,128]{5,4,3,2,1,0:T(8,128)(2,1)} %param.12, bf16[1,1,1,2,128,128]{5,4,3,2,1,0:T(8,128)(2,1)} %param.14), kind=kOutput, calls=%fused_computation.1 | convolution fusion | flops 4210688 | bytes 98304 | tf_op jit(solution)/shard_map/dot_general | solution.py:329
  2.0 2.6 %collective-permute-start = (bf16[128,128]{1,0:T(8,128)(2,1)S(1)}, bf16[128,128]{1,0:T(8,128)(2,1)S(1)}, u32[]{:S(2)}, u32[]{:S(2)}) collective-permute-start(bf16[128,128]{1,0:T(8,128)(2,1)S(1)} %convolution_convert_fusion.1.refs_2_.refs_4_), channel_id=1, source_target_pairs={{0,2},{1,3},{2,0},{3,1},{4,6},{5,7},{6,4},{7,5},{8,10},{9,11},{10,... | collective-permute-start | bytes 98312 | tf_op jit(solution)/shard_map/ppermute | solution.py:35
  4.6 2.1 %shard_map.95 = (s32[8,128]{1,0:T(8,128)S(1)}, s32[8,128]{1,0:T(8,128)S(4)}, bf16[40,128,128]{2,1,0:T(8,128)(2,1)S(1)}) custom-call(s32[3,1,40]{2,1,0:T(1,128)} %bitcast.46, s32[3,1,40]{2,1,0:T(1,128)} %bitcast.47, s32[3]{0:T(128)} %bitcast.48, bf16[3,40,128,128]{3,2,1,0:T(8,128)(2,1)} %bitcast.38), custom_call_target="tpu_custom_call" | custom-call | tf_op jit(solution)/shard_map/pallas_call | solution.py:98
  6.7 1.0 %shard_map.96 = bf16[8,128,128]{2,1,0:T(8,128)(2,1)} custom-call(s32[8,128]{1,0:T(8,128)S(4)} %get-tuple-element.33.refs_0_, bf16[3,40,128,128]{3,2,1,0:T(8,128)(2,1)} %bitcast.39, bf16[128,128]{1,0:T(8,128)(2,1)S(1)} %convolution_convert_fusion.1.refs_2_.refs_4_, bf16[128,128]{1,0:T(8,128)(2,1)S(1)} %collective-permute-done.refs_3_.refs_5_, ...), custom_call_target="tpu_custom_call" | custom-call | tf_op jit(solution)/shard_map/pallas_call | solution.py:269
  7.7 6.6 %all-to-all-start = ((bf16[8,128,128]{2,1,0:T(8,128)(2,1)}), bf16[8,128,128]{2,1,0:T(8,128)(2,1)S(1)}, u32[]{:S(2)}, u32[]{:S(2)}) async-start(bf16[8,128,128]{2,1,0:T(8,128)(2,1)} %shard_map.96), calls=%async_computation | async-start | bytes 524288 | tf_op jit(solution)/shard_map/all_to_all | solution.py:340
  14.4 1.7 %collective-permute-start.4 = (bf16[128,128]{1,0:T(8,128)(2,1)S(1)}, bf16[128,128]{1,0:T(8,128)(2,1)S(1)}, u32[]{:S(2)}, u32[]{:S(2)}) collective-permute-start(bf16[128,128]{1,0:T(8,128)(2,1)S(1)} %convolution_convert_fusion.1.refs_2_.refs_4_), channel_id=1, source_target_pairs={{0,3},{1,2},{2,1},{3,0},{4,7},{5,6},{6,5},{7,4},{8,11},{9,10},{10,... | collective-permute-start | bytes 98312 | tf_op jit(solution)/shard_map/ppermute | solution.py:35
  16.1 1.1 %collective-permute-done.1.refs_1_ = s32[8,128]{1,0:T(8,128)S(1)} collective-permute-done((s32[8,128]{1,0:T(8,128)S(1)}, s32[8,128]{1,0:T(8,128)S(1)}, u32[]{:S(2)}, u32[]{:S(2)}) %collective-permute-start.1) | collective-permute-done | bytes 4128 | tf_op jit(solution)/shard_map/ppermute | solution.py:40
  17.7 2.2 %shard_map.97 = (f32[8,128,128]{2,1,0:T(8,128)S(1)}, bf16[40,128,128]{2,1,0:T(8,128)(2,1)S(1)}, s32[8,128]{1,0:T(8,128)S(4)}) custom-call(s32[8,128]{1,0:T(8,128)S(4)} %get-tuple-element.33.refs_0_, s32[8,128]{1,0:T(8,128)S(1)} %collective-permute-done.1.refs_1_, bf16[3,40,128,128]{3,2,1,0:T(8,128)(2,1)} %bitcast.40, ...), custom_call_target="tpu_custom_call" | custom-call | tf_op jit(solution)/shard_map/pallas_call | solution.py:269
  20.0 1.6 %all-to-all-done = bf16[8,128,128]{2,1,0:T(8,128)(2,1)S(1)} async-done(((bf16[8,128,128]{2,1,0:T(8,128)(2,1)}), bf16[8,128,128]{2,1,0:T(8,128)(2,1)S(1)}, u32[]{:S(2)}, u32[]{:S(2)}) %all-to-all-start) | async-done | bytes 262176 | tf_op jit(solution)/shard_map/all_to_all | solution.py:340
  21.8 1.2 %collective-permute-start.5 = (bf16[128,128]{1,0:T(8,128)(2,1)S(1)}, bf16[128,128]{1,0:T(8,128)(2,1)S(1)}, u32[]{:S(2)}, u32[]{:S(2)}) collective-permute-start(bf16[128,128]{1,0:T(8,128)(2,1)S(1)} %fusion.refs_4_.refs_5_.refs_8_), channel_id=1, source_target_pairs={{0,2},{1,3},{2,0},{3,1},{4,6},{5,7},{6,4},{7,5},{8,10},{9,11},{10,... | collective-permute-start | bytes 98312 | tf_op jit(solution)/shard_map/ppermute | solution.py:35
  23.0 1.0 %collective-permute-start.7 = (bf16[128,128]{1,0:T(8,128)(2,1)S(1)}, bf16[128,128]{1,0:T(8,128)(2,1)S(1)}, u32[]{:S(2)}, u32[]{:S(2)}) collective-permute-start(bf16[128,128]{1,0:T(8,128)(2,1)S(1)} %fusion.refs_4_.refs_5_.refs_8_), channel_id=1, source_target_pairs={{0,3},{1,2},{2,1},{3,0},{4,7},{5,6},{6,5},{7,4},{8,11},{9,10},{10,... | collective-permute-start | bytes 98312 | tf_op jit(solution)/shard_map/ppermute | solution.py:35
  24.0 1.3 %shard_map.98 = (f32[8,128,128]{2,1,0:T(8,128)S(1)}, bf16[40,128,128]{2,1,0:T(8,128)(2,1)S(1)}) custom-call(s32[8,128]{1,0:T(8,128)S(4)} %get-tuple-element.33.refs_0_, s32[8,128]{1,0:T(8,128)S(4)} %get-tuple-element.40.refs_1_, bf16[3,40,128,128]{3,2,1,0:T(8,128)(2,1)} %bitcast.41, bf16[3,40,128,128]{3,2,1,0:T(8,128)(2,1)} %collective-permute-done.2.refs_3_, ...), custom_call_target="tpu_custom_call" | custom-call | tf_op jit(solution)/shard_map/pallas_call | solution.py:269
  25.7 0.6 %collective-permute-done.7.refs_7_.refs_11_ = bf16[128,128]{1,0:T(8,128)(2,1)S(1)} collective-permute-done((bf16[128,128]{1,0:T(8,128)(2,1)S(1)}, bf16[128,128]{1,0:T(8,128)(2,1)S(1)}, u32[]{:S(2)}, u32[]{:S(2)}) %collective-permute-start.7) | collective-permute-done | bytes 32800 | tf_op jit(solution)/shard_map/ppermute | solution.py:35
  26.3 1.5 %shard_map.99 = bf16[8,64,128]{2,1,0:T(8,128)(2,1)} custom-call(s32[8,128]{1,0:T(8,128)S(4)} %get-tuple-element.33.refs_0_, s32[8,128]{1,0:T(8,128)S(4)} %get-tuple-element.40.refs_1_, bf16[3,40,128,128]{3,2,1,0:T(8,128)(2,1)} %bitcast.42, bf16[3,40,128,128]{3,2,1,0:T(8,128)(2,1)} %collective-permute-done.2.refs_3_, ...), custom_call_target="tpu_custom_call" | custom-call | tf_op jit(solution)/shard_map/pallas_call | solution.py:269
  27.8 5.5 %all-to-all-start.1 = ((bf16[8,64,128]{2,1,0:T(8,128)(2,1)}), bf16[8,64,128]{2,1,0:T(8,128)(2,1)S(1)}, u32[]{:S(2)}, u32[]{:S(2)}) async-start(bf16[8,64,128]{2,1,0:T(8,128)(2,1)} %shard_map.99), calls=%async_computation.1 | async-start | bytes 262144 | tf_op jit(solution)/shard_map/all_to_all | solution.py:340
  33.4 3.2 %shard_map.100 = (f32[8,128,128]{2,1,0:T(8,128)S(1)}, bf16[40,128,128]{2,1,0:T(8,128)(2,1)S(1)}) custom-call(s32[8,128]{1,0:T(8,128)S(4)} %get-tuple-element.33.refs_0_, s32[8,128]{1,0:T(8,128)S(4)} %get-tuple-element.40.refs_1_, bf16[3,40,128,128]{3,2,1,0:T(8,128)(2,1)} %bitcast.43, bf16[3,40,128,128]{3,2,1,0:T(8,128)(2,1)} %collective-permute-done.2.refs_3_, ...), custom_call_target="tpu_custom_call" | custom-call | tf_op jit(solution)/shard_map/pallas_call | solution.py:269
  36.6 2.3 %all-to-all-done.1.received = bf16[8,64,128]{2,1,0:T(8,128)(2,1)S(1)} async-done(((bf16[8,64,128]{2,1,0:T(8,128)(2,1)}), bf16[8,64,128]{2,1,0:T(8,128)(2,1)S(1)}, u32[]{:S(2)}, u32[]{:S(2)}) %all-to-all-start.1) | async-done | bytes 131104 | tf_op jit(solution)/shard_map/all_to_all | solution.py:340
  39.2 1.1 %collective-permute-start.8 = (bf16[64,128]{1,0:T(8,128)(2,1)S(1)}, bf16[64,128]{1,0:T(8,128)(2,1)S(1)}, u32[]{:S(2)}, u32[]{:S(2)}) collective-permute-start(bf16[64,128]{1,0:T(8,128)(2,1)S(1)} %shard_map.101.refs_4_.refs_5_.refs_0_), channel_id=1, source_target_pairs={{0,2},{1,3},{2,0},{3,1},{4,6},{5,7},{6,4},{7,5},{8,10},{9,11},{10,... | collective-permute-start | bytes 49160 | tf_op jit(solution)/shard_map/ppermute | solution.py:35
  40.3 1.6 %shard_map.102 = (f32[8,128,128]{2,1,0:T(8,128)S(1)}, bf16[40,128,128]{2,1,0:T(8,128)(2,1)S(1)}) custom-call(s32[8,128]{1,0:T(8,128)S(4)} %get-tuple-element.33.refs_0_, s32[8,128]{1,0:T(8,128)S(4)} %get-tuple-element.40.refs_1_, bf16[3,40,128,128]{3,2,1,0:T(8,128)(2,1)} %bitcast.44, bf16[3,40,128,128]{3,2,1,0:T(8,128)(2,1)} %collective-permute-done.2.refs_3_, ...), custom_call_target="tpu_custom_call" | custom-call | tf_op jit(solution)/shard_map/pallas_call | solution.py:269
  41.9 1.1 %collective-permute-done.8.refs_5_ = bf16[64,128]{1,0:T(8,128)(2,1)S(1)} collective-permute-done((bf16[64,128]{1,0:T(8,128)(2,1)S(1)}, bf16[64,128]{1,0:T(8,128)(2,1)S(1)}, u32[]{:S(2)}, u32[]{:S(2)}) %collective-permute-start.8) | collective-permute-done | bytes 16416 | tf_op jit(solution)/shard_map/ppermute | solution.py:35
  43.0 0.9 %shard_map.103 = bf16[8,64,128]{2,1,0:T(8,128)(2,1)S(1)} custom-call(s32[8,128]{1,0:T(8,128)S(4)} %get-tuple-element.33.refs_0_, s32[8,128]{1,0:T(8,128)S(4)} %get-tuple-element.40.refs_1_, bf16[3,40,128,128]{3,2,1,0:T(8,128)(2,1)} %bitcast.45, bf16[3,40,128,128]{3,2,1,0:T(8,128)(2,1)} %collective-permute-done.2.refs_3_, ...), custom_call_target="tpu_custom_call" | custom-call | tf_op jit(solution)/shard_map/pallas_call | solution.py:269
  43.9 9.0 %all_to_all.15.received = bf16[8,64,128]{2,1,0:T(8,128)(2,1)S(1)} all-to-all(bf16[8,64,128]{2,1,0:T(8,128)(2,1)S(1)} %shard_map.103), channel_id=1, replica_groups={{16,20,24,28,0,4,8,12},{17,21,25,29,1,5,9,13},{18,22,26,30,2,6,10,14},{..., dimensions={0} | all-to-all | bytes 262144 | tf_op jit(solution)/shard_map/all_to_all | solution.py:340
  53.2 0.6 %maximum_bitcast_fusion = bf16[1,1,1,2,128,128]{5,4,3,2,1,0:T(8,128)(2,1)} fusion(bf16[1,128,128]{2,1,0:T(8,128)(2,1)S(1)} %bitcast.31, bf16[1,128,128]{2,1,0:T(8,128)(2,1)S(1)} %bitcast.32), kind=kLoop, calls=%fused_computation.4 | loop fusion | flops 32768 | bytes 131072 | tf_op jit(solution)/shard_map/broadcast_in_dim | solution.py:409
  54.4 0.8 %shard_map.105 = bf16[1,1,2,128,128]{4,3,2,1,0:T(8,128)(2,1)} custom-call(bf16[2,64,128]{2,1,0:T(8,128)(2,1)S(1)} %shard_map.104.own, bf16[2,64,128]{2,1,0:T(8,128)(2,1)S(1)} %collective-permute-done.9.other), custom_call_target="tpu_custom_call" | custom-call | tf_op jit(solution)/shard_map/pallas_call | solution.py:319
  (24 shorter events, 2.9 us)
Async XLA Ops:
  1.5 16.2 %collective-permute-start.2 = (bf16[3,40,128,128]{3,2,1,0:T(8,128)(2,1)}, bf16[3,40,128,128]{3,2,1,0:T(8,128)(2,1)}, u32[]{:S(2)}, u32[]{:S(2)}) collective-permute-start(bf16[3,40,128,128]{3,2,1,0:T(8,128)(2,1)} %bitcast.37), channel_id=1, source_target_pairs={{0,1},{1,0},{2,3},{3,2},{4,5},{5,4},{6,7},{7,6},{8,9},{9,8},{10,11... | collective-permute-start | bytes 11796488 | tf_op jit(solution)/shard_map/ppermute | solution.py:40
  2.0 4.7 %collective-permute-start = (bf16[128,128]{1,0:T(8,128)(2,1)S(1)}, bf16[128,128]{1,0:T(8,128)(2,1)S(1)}, u32[]{:S(2)}, u32[]{:S(2)}) collective-permute-start(bf16[128,128]{1,0:T(8,128)(2,1)S(1)} %convolution_convert_fusion.1.refs_2_.refs_4_), channel_id=1, source_target_pairs={{0,2},{1,3},{2,0},{3,1},{4,6},{5,7},{6,4},{7,5},{8,10},{9,11},{10,... | collective-permute-start | bytes 98312 | tf_op jit(solution)/shard_map/ppermute | solution.py:35
  7.7 13.9 %all-to-all-start = ((bf16[8,128,128]{2,1,0:T(8,128)(2,1)}), bf16[8,128,128]{2,1,0:T(8,128)(2,1)S(1)}, u32[]{:S(2)}, u32[]{:S(2)}) async-start(bf16[8,128,128]{2,1,0:T(8,128)(2,1)} %shard_map.96), calls=%async_computation | async-start | bytes 524288 | tf_op jit(solution)/shard_map/all_to_all | solution.py:340
  14.3 7.4 %copy-start.2 = (bf16[1,1,1,2,128,128]{5,4,3,2,1,0:T(8,128)(2,1)S(1)}, bf16[1,1,1,2,128,128]{5,4,3,2,1,0:T(8,128)(2,1)}, u32[]{:S(2)}) copy-start(bf16[1,1,1,2,128,128]{5,4,3,2,1,0:T(8,128)(2,1)} %param.12) | copy-start | bytes 196612
  14.3 7.4 %copy-start.3 = (bf16[1,1,1,2,128,128]{5,4,3,2,1,0:T(8,128)(2,1)S(1)}, bf16[1,1,1,2,128,128]{5,4,3,2,1,0:T(8,128)(2,1)}, u32[]{:S(2)}) copy-start(bf16[1,1,1,2,128,128]{5,4,3,2,1,0:T(8,128)(2,1)} %param.14) | copy-start | bytes 196612
  14.3 2.9 %collective-permute-start.3 = (bf16[128,128]{1,0:T(8,128)(2,1)S(1)}, bf16[128,128]{1,0:T(8,128)(2,1)S(1)}, u32[]{:S(2)}, u32[]{:S(2)}) collective-permute-start(bf16[128,128]{1,0:T(8,128)(2,1)S(1)} %convolution_convert_fusion.1.refs_2_.refs_4_), channel_id=1, source_target_pairs={{0,1},{1,0},{2,3},{3,2},{4,5},{5,4},{6,7},{7,6},{8,9},{9,8},{10,11... | collective-permute-start | bytes 98312 | tf_op jit(solution)/shard_map/ppermute | solution.py:35
  14.4 3.4 %collective-permute-start.4 = (bf16[128,128]{1,0:T(8,128)(2,1)S(1)}, bf16[128,128]{1,0:T(8,128)(2,1)S(1)}, u32[]{:S(2)}, u32[]{:S(2)}) collective-permute-start(bf16[128,128]{1,0:T(8,128)(2,1)S(1)} %convolution_convert_fusion.1.refs_2_.refs_4_), channel_id=1, source_target_pairs={{0,3},{1,2},{2,1},{3,0},{4,7},{5,6},{6,5},{7,4},{8,11},{9,10},{10,... | collective-permute-start | bytes 98312 | tf_op jit(solution)/shard_map/ppermute | solution.py:35
  16.0 1.2 %collective-permute-start.1 = (s32[8,128]{1,0:T(8,128)S(1)}, s32[8,128]{1,0:T(8,128)S(1)}, u32[]{:S(2)}, u32[]{:S(2)}) collective-permute-start(s32[8,128]{1,0:T(8,128)S(1)} %get-tuple-element.37), channel_id=1, source_target_pairs={{0,1},{1,0},{2,3},{3,2},{4,5},{5,4},{6,7},{7,6},{8,9},{9,8},{10,11... | collective-permute-start | bytes 12296 | tf_op jit(solution)/shard_map/ppermute | solution.py:40
  21.8 3.9 %collective-permute-start.5 = (bf16[128,128]{1,0:T(8,128)(2,1)S(1)}, bf16[128,128]{1,0:T(8,128)(2,1)S(1)}, u32[]{:S(2)}, u32[]{:S(2)}) collective-permute-start(bf16[128,128]{1,0:T(8,128)(2,1)S(1)} %fusion.refs_4_.refs_5_.refs_8_), channel_id=1, source_target_pairs={{0,2},{1,3},{2,0},{3,1},{4,6},{5,7},{6,4},{7,5},{8,10},{9,11},{10,... | collective-permute-start | bytes 98312 | tf_op jit(solution)/shard_map/ppermute | solution.py:35
  23.0 2.7 %collective-permute-start.6 = (bf16[128,128]{1,0:T(8,128)(2,1)S(1)}, bf16[128,128]{1,0:T(8,128)(2,1)S(1)}, u32[]{:S(2)}, u32[]{:S(2)}) collective-permute-start(bf16[128,128]{1,0:T(8,128)(2,1)S(1)} %fusion.refs_4_.refs_5_.refs_8_), channel_id=1, source_target_pairs={{0,1},{1,0},{2,3},{3,2},{4,5},{5,4},{6,7},{7,6},{8,9},{9,8},{10,11... | collective-permute-start | bytes 98312 | tf_op jit(solution)/shard_map/ppermute | solution.py:35
  23.0 3.3 %collective-permute-start.7 = (bf16[128,128]{1,0:T(8,128)(2,1)S(1)}, bf16[128,128]{1,0:T(8,128)(2,1)S(1)}, u32[]{:S(2)}, u32[]{:S(2)}) collective-permute-start(bf16[128,128]{1,0:T(8,128)(2,1)S(1)} %fusion.refs_4_.refs_5_.refs_8_), channel_id=1, source_target_pairs={{0,3},{1,2},{2,1},{3,0},{4,7},{5,6},{6,5},{7,4},{8,11},{9,10},{10,... | collective-permute-start | bytes 98312 | tf_op jit(solution)/shard_map/ppermute | solution.py:35
  27.8 11.1 %all-to-all-start.1 = ((bf16[8,64,128]{2,1,0:T(8,128)(2,1)}), bf16[8,64,128]{2,1,0:T(8,128)(2,1)S(1)}, u32[]{:S(2)}, u32[]{:S(2)}) async-start(bf16[8,64,128]{2,1,0:T(8,128)(2,1)} %shard_map.99), calls=%async_computation.1 | async-start | bytes 262144 | tf_op jit(solution)/shard_map/all_to_all | solution.py:340
  33.4 5.5 %copy-start = (bf16[1,1,2,128,128]{4,3,2,1,0:T(8,128)(2,1)S(1)}, bf16[1,1,2,128,128]{4,3,2,1,0:T(8,128)(2,1)}, u32[]{:S(2)}) copy-start(bf16[1,1,2,128,128]{4,3,2,1,0:T(8,128)(2,1)} %param.13) | copy-start | bytes 196612
  33.4 5.5 %copy-start.1 = (bf16[1,1,2,128,128]{4,3,2,1,0:T(8,128)(2,1)S(1)}, bf16[1,1,2,128,128]{4,3,2,1,0:T(8,128)(2,1)}, u32[]{:S(2)}) copy-start(bf16[1,1,2,128,128]{4,3,2,1,0:T(8,128)(2,1)} %param.15) | copy-start | bytes 196612
  39.2 3.8 %collective-permute-start.8 = (bf16[64,128]{1,0:T(8,128)(2,1)S(1)}, bf16[64,128]{1,0:T(8,128)(2,1)S(1)}, u32[]{:S(2)}, u32[]{:S(2)}) collective-permute-start(bf16[64,128]{1,0:T(8,128)(2,1)S(1)} %shard_map.101.refs_4_.refs_5_.refs_0_), channel_id=1, source_target_pairs={{0,2},{1,3},{2,0},{3,1},{4,6},{5,7},{6,4},{7,5},{8,10},{9,11},{10,... | collective-permute-start | bytes 49160 | tf_op jit(solution)/shard_map/ppermute | solution.py:35
  53.2 1.2 %collective-permute-start.9 = (bf16[2,64,128]{2,1,0:T(8,128)(2,1)S(1)}, bf16[2,64,128]{2,1,0:T(8,128)(2,1)S(1)}, u32[]{:S(2)}, u32[]{:S(2)}) collective-permute-start(bf16[2,64,128]{2,1,0:T(8,128)(2,1)S(1)} %shard_map.104.own), channel_id=1, source_target_pairs={{0,1},{1,0},{2,3},{3,2},{4,5},{5,4},{6,7},{7,6},{8,9},{9,8},{10,11... | collective-permute-start | bytes 98312 | tf_op jit(solution)/shard_map/ppermute | solution.py:40

commit v4 on v3

--- a/solution.py
+++ b/solution.py
@@ -179,8 +179,10 @@
         loads[stages].start()
 
     for j, solution_ref in enumerate(solutions):
-        if solution_ref.shape == chosen.shape[1:]:
+        if form == "whole":
             chosen[j] = solution_ref[...]
+        elif solution_ref.shape == chosen.shape[1:]:
+            chosen[j] = half_first(solution_ref[...].astype(jnp.float32)).astype(jnp.bfloat16)
         else:
             chosen[j] = unpacked(solution_ref[...].astype(jnp.float32)).astype(jnp.bfloat16)
     if carries:
@@ -216,13 +218,10 @@
 
     if form == "summed":
         out[...] = total[:row_count]
-    elif form == "turned":
-        for row in range(row_count):
-            out[row] = half_first(total[row])
     else:
         for k, row in enumerate(exchange_order(row_count)):
-            value = half_first(total[row]) if form == "half" else total[row]
-            out[k] = (value if form == "whole" else packed(value)).astype(jnp.bfloat16)
+            value = total[row] if form == "whole" else packed(total[row])
+            out[k] = value.astype(jnp.bfloat16)
     for load in loads.values():
         load.wait()
 
@@ -241,9 +240,9 @@
             specs.append(vmem)
     fetched = fetched_levels(lists, tuple(resident) + ((stages,) if stages else ()))
     shape = (row_count, width, sides)
-    if form in ("half", "rest"):
+    if form == "half":
         shape = (row_count, width // 2, sides)
-    if form in ("summed", "turned"):
+    if form == "summed":
         outs = [jax.ShapeDtypeStruct(shape, jnp.float32)]
     else:
         outs = [pltpu.VMEM(shape, jnp.bfloat16)]
@@ -277,6 +276,30 @@
     return found if len(outs) > 1 else found[0]
 
 
+def sub_solve_kernel(received, given, inverse, out, kept, sent):
+    incoming = received[0].astype(jnp.float32)
+    for row in range(1, received.shape[0]):
+        incoming = incoming + received[row].astype(jnp.float32)
+    residual = (given[1].astype(jnp.float32) - incoming).astype(jnp.bfloat16)
+    found = jnp.dot(inverse[1], residual, preferred_element_type=jnp.float32)
+    out[...] = found.astype(jnp.bfloat16)
+    mine = half_first(found)
+    kept[...] = packed(mine).astype(jnp.bfloat16)
+    sent[...] = packed(turned(mine)).astype(jnp.bfloat16)
+
+
+def sub_solve(received, given, inverse):
+    _, width, sides = received.shape
+    half = jax.ShapeDtypeStruct((width // 2, sides), jnp.bfloat16)
+    return pl.pallas_call(
+        sub_solve_kernel,
+        out_shape=[jax.ShapeDtypeStruct((width, sides), jnp.bfloat16), half, half],
+        in_specs=[vmem] * 3,
+        out_specs=[vmem] * 3,
+        compiler_params=params,
+    )(received, given, inverse)
+
+
 def half_solve_kernel(level, received, given, inverse, *refs):
     incoming = received[0].astype(jnp.float32)
     for row in range(1, received.shape[0]):
@@ -329,12 +352,6 @@
     return jnp.dot(inverse, residual, preferred_element_type=jnp.float32).astype(jnp.bfloat16)
 
 
-def reduced_solve(received, given, inverse):
-    incoming = jnp.sum(received.astype(jnp.float32), axis=0)
-    residual = (given.astype(jnp.float32) - incoming).astype(jnp.bfloat16)
-    return solve_block(inverse, residual)
-
-
 def exchange(send):
     order = exchange_order(lax.axis_size("prow"))
     return lax.all_to_all(send, "prow", 0, 0, tiled=True, axis_index_groups=[order])
@@ -373,13 +390,13 @@
         {}, (0, 1), True,
     )
     received, second, staged = lax.optimization_barrier((received, second, staged))
-    level_one = reduced_solve(received, right_sub[1], factor_sub[1])
-    one_own = sibling_values(level_one, 0)
-    one_other = sibling_values(level_one, 1)
+    level_one, one_kept, one_sent = sub_solve(received, right_sub, factor_sub)
+    one_own = sibling_values(one_kept, 0)
+    one_other = sibling_values(one_sent, 1)
 
     resident = {(0, 1): staged}
     second, resident[(1, 1)] = update(
-        [(3, 0, 0)], plans, both, [[level_one] * cols], second, row_count, "summed", resident, (1, 1)
+        [(3, 0, 0)], plans, both, [[one_kept] * cols], second, row_count, "summed", resident, (1, 1)
     )
     send = update(
         [(4, 0, 0), (3, 1, 1), (4, 1, 1)], plans, both, [one_own, one_other], second, row_count,
@@ -389,7 +406,7 @@
     received = exchange(send)
     third, staged = update(
         [(2, 0, 0), (2, 1, 1), (5, 0, 2), (5, 1, 3)], plans, both,
-        [zero_own, zero_other, one_own, one_other], None, row_count, "turned", {}, (0, 2),
+        [zero_own, zero_other, one_own, one_other], None, row_count, "summed", {}, (0, 2),
     )
     received, third, staged = lax.optimization_barrier((received, third, staged))
     level_two = half_solve(0, received, right_top, factor_top, None)
@@ -401,7 +418,7 @@
         resident, (1, 2),
     )
     send = update(
-        [(7, 0, 0), (7, 1, 0)], plans, both, [two_own], third, row_count, "rest", resident, None
+        [(7, 0, 0), (7, 1, 0)], plans, both, [two_own], third, row_count, "half", resident, None
     )
     send, level_zero, level_one = lax.optimization_barrier((send, level_zero, level_one))
     halves = half_solve(1, exchange(send), right_top, factor_top, level_two)

time: 55.5 us -> 54.9 us (0.989)
  waiting for transfers between devices: 8.19 us -> 7.22 us
    ppermute x7, waiting for transfers between devices: 2.6 us -> 1.74 us  [sibling_values(): found.append(lax.ppermute(value, ('pcol', 'zgrid'), moves))]
    pallas_call x7, Pallas kernels: 11.8 us -> 11.2 us  [update(): pl.pallas_call(functools.partial(update_kernel, config), out_shape=outs,...]
    all_to_all x2, starting transfers between devices: 12.1 us -> 11.5 us  [exchange(): lax.all_to_all(send, 'prow', 0, 0, tiled=True, axis_index_groups=[order])]
  transfers between devices with their start and end apart: 12 -> 12, of which waited for: 8 -> 7; matrix products, arithmetic and copies ran while one was open for 1% -> 1% of each run, Pallas kernels for 21% -> 22%
where the time goes in v4:
time: 54.9 us; the launch traced here: 54.1 us
  starting transfers between devices  19.9 us (36%)
  Pallas kernels  15.4 us (28%)
  blocking collectives  9.32 us (17%)
  waiting for transfers between devices  7.22 us (13%)
  matrix products  0.9 us (2%)
  between operations  0.73 us (1%)
  other arithmetic  0.64 us (1%)
    all_to_all x2, starting transfers between devices, exchange(): lax.all_to_all(send, 'prow', 0, 0, tiled=True, axis_index_groups=[order])  11.5 us
    pallas_call x7, Pallas kernels, update(): pl.pallas_call(functools.partial(update_kernel, config), out_shape=outs,...  11.2 us
    all_to_all x1, blocking collectives, exchange(): lax.all_to_all(send, 'prow', 0, 0, tiled=True, axis_index_groups=[order])  9.32 us
    ppermute x7, starting transfers between devices, sibling_values(): found.append(lax.ppermute(value, ('pcol', 'zgrid'), moves))  7.81 us
    all_to_all x2, waiting for transfers between devices, exchange(): lax.all_to_all(send, 'prow', 0, 0, tiled=True, axis_index_groups=[order])  3.83 us
    pallas_call x1, Pallas kernels, make_plan(): pl.pallas_call(functools.partial(plan_kernel, row_count, cols), out_shape...  2.51 us
    ppermute x7, waiting for transfers between devices, sibling_values(): found.append(lax.ppermute(value, ('pcol', 'zgrid'), moves))  1.74 us
    ppermute x3, waiting for transfers between devices, from_other_core(): return lax.ppermute(value, 'zgrid', [(0, 1), (1, 0)])  1.65 us
  transfers between devices with their start and end apart: 12, of which 7 were waited for; matrix products, arithmetic and copies ran while one was open for 1% of the time, Pallas kernels for 22%

profile of v4, /device:TPU:0, one launch (start us, length us, event | category | flops | bytes accessed | tf_op | source)
XLA Modules:
  0.0 54.1 jit_solution(5798459485560913940)
XLA Ops:
  0.6 0.9 %convolution_convert_fusion.refs_2_.refs_4_ = bf16[128,128]{1,0:T(8,128)(2,1)S(1)} fusion(bf16[1,1,1,2,128,128]{5,4,3,2,1,0:T(8,128)(2,1)} %param.12, bf16[1,1,1,2,128,128]{5,4,3,2,1,0:T(8,128)(2,1)} %param.14), kind=kOutput, calls=%fused_computation | convolution fusion | flops 4210688 | bytes 98304 | tf_op jit(solution)/shard_map/dot_general | solution.py:352
  2.0 2.6 %collective-permute-start = (bf16[128,128]{1,0:T(8,128)(2,1)S(1)}, bf16[128,128]{1,0:T(8,128)(2,1)S(1)}, u32[]{:S(2)}, u32[]{:S(2)}) collective-permute-start(bf16[128,128]{1,0:T(8,128)(2,1)S(1)} %convolution_convert_fusion.refs_2_.refs_4_), channel_id=1, source_target_pairs={{0,2},{1,3},{2,0},{3,1},{4,6},{5,7},{6,4},{7,5},{8,10},{9,11},{10,... | collective-permute-start | bytes 98312 | tf_op jit(solution)/shard_map/ppermute | solution.py:35
  4.6 2.5 %shard_map.95 = (s32[8,128]{1,0:T(8,128)S(1)}, s32[8,128]{1,0:T(8,128)S(4)}, bf16[40,128,128]{2,1,0:T(8,128)(2,1)S(1)}) custom-call(s32[3,1,40]{2,1,0:T(1,128)} %bitcast.35, s32[3,1,40]{2,1,0:T(1,128)} %bitcast.36, s32[3]{0:T(128)} %bitcast.37, bf16[3,40,128,128]{3,2,1,0:T(8,128)(2,1)} %bitcast.27), custom_call_target="tpu_custom_call" | custom-call | tf_op jit(solution)/shard_map/pallas_call | solution.py:98
  7.1 1.0 %shard_map.96 = bf16[8,128,128]{2,1,0:T(8,128)(2,1)} custom-call(s32[8,128]{1,0:T(8,128)S(4)} %get-tuple-element.36.refs_0_, bf16[3,40,128,128]{3,2,1,0:T(8,128)(2,1)} %bitcast.28, bf16[128,128]{1,0:T(8,128)(2,1)S(1)} %convolution_convert_fusion.refs_2_.refs_4_, bf16[128,128]{1,0:T(8,128)(2,1)S(1)} %collective-permute-done.refs_3_.refs_5_, ...), custom_call_target="tpu_custom_call" | custom-call | tf_op jit(solution)/shard_map/pallas_call | solution.py:268
  8.2 6.3 %all-to-all-start = ((bf16[8,128,128]{2,1,0:T(8,128)(2,1)}), bf16[8,128,128]{2,1,0:T(8,128)(2,1)S(1)}, u32[]{:S(2)}, u32[]{:S(2)}) async-start(bf16[8,128,128]{2,1,0:T(8,128)(2,1)} %shard_map.96), calls=%async_computation | async-start | bytes 524288 | tf_op jit(solution)/shard_map/all_to_all | solution.py:357
  14.4 1.6 %collective-permute-start.4 = (bf16[128,128]{1,0:T(8,128)(2,1)S(1)}, bf16[128,128]{1,0:T(8,128)(2,1)S(1)}, u32[]{:S(2)}, u32[]{:S(2)}) collective-permute-start(bf16[128,128]{1,0:T(8,128)(2,1)S(1)} %convolution_convert_fusion.refs_2_.refs_4_), channel_id=1, source_target_pairs={{0,3},{1,2},{2,1},{3,0},{4,7},{5,6},{6,5},{7,4},{8,11},{9,10},{10,... | collective-permute-start | bytes 98312 | tf_op jit(solution)/shard_map/ppermute | solution.py:35
  16.1 1.1 %collective-permute-done.1.refs_1_ = s32[8,128]{1,0:T(8,128)S(1)} collective-permute-done((s32[8,128]{1,0:T(8,128)S(1)}, s32[8,128]{1,0:T(8,128)S(1)}, u32[]{:S(2)}, u32[]{:S(2)}) %collective-permute-start.1) | collective-permute-done | bytes 4128 | tf_op jit(solution)/shard_map/ppermute | solution.py:40
  17.2 0.6 %collective-permute-done.4.refs_7_ = bf16[128,128]{1,0:T(8,128)(2,1)S(1)} collective-permute-done((bf16[128,128]{1,0:T(8,128)(2,1)S(1)}, bf16[128,128]{1,0:T(8,128)(2,1)S(1)}, u32[]{:S(2)}, u32[]{:S(2)}) %collective-permute-start.4) | collective-permute-done | bytes 32800 | tf_op jit(solution)/shard_map/ppermute | solution.py:35
  17.8 2.2 %shard_map.97 = (f32[8,128,128]{2,1,0:T(8,128)S(1)}, bf16[40,128,128]{2,1,0:T(8,128)(2,1)S(1)}, s32[8,128]{1,0:T(8,128)S(4)}) custom-call(s32[8,128]{1,0:T(8,128)S(4)} %get-tuple-element.36.refs_0_, s32[8,128]{1,0:T(8,128)S(1)} %collective-permute-done.1.refs_1_, bf16[3,40,128,128]{3,2,1,0:T(8,128)(2,1)} %bitcast.29, ...), custom_call_target="tpu_custom_call" | custom-call | tf_op jit(solution)/shard_map/pallas_call | solution.py:268
  20.0 1.5 %all-to-all-done.received = bf16[8,128,128]{2,1,0:T(8,128)(2,1)S(1)} async-done(((bf16[8,128,128]{2,1,0:T(8,128)(2,1)}), bf16[8,128,128]{2,1,0:T(8,128)(2,1)S(1)}, u32[]{:S(2)}, u32[]{:S(2)}) %all-to-all-start) | async-done | bytes 262176 | tf_op jit(solution)/shard_map/all_to_all | solution.py:357
  21.9 0.5 collective-permute-start.5
  22.4 1.6 %collective-permute-start.7 = (bf16[64,128]{1,0:T(8,128)(2,1)S(1)}, bf16[64,128]{1,0:T(8,128)(2,1)S(1)}, u32[]{:S(2)}, u32[]{:S(2)}) collective-permute-start(bf16[64,128]{1,0:T(8,128)(2,1)S(1)} %get-tuple-element.49), channel_id=1, source_target_pairs={{0,3},{1,2},{2,1},{3,0},{4,7},{5,6},{6,5},{7,4},{8,11},{9,10},{10,... | collective-permute-start | bytes 49160 | tf_op jit(solution)/shard_map/ppermute | solution.py:35
  24.1 1.3 %shard_map.99 = (f32[8,128,128]{2,1,0:T(8,128)S(1)}, bf16[40,128,128]{2,1,0:T(8,128)(2,1)S(1)}) custom-call(s32[8,128]{1,0:T(8,128)S(4)} %get-tuple-element.36.refs_0_, s32[8,128]{1,0:T(8,128)S(4)} %get-tuple-element.43.refs_1_, bf16[3,40,128,128]{3,2,1,0:T(8,128)(2,1)} %bitcast.30, bf16[3,40,128,128]{3,2,1,0:T(8,128)(2,1)} %collective-permute-done.2.refs_3_, ...), custom_call_target="tpu_custom_call" | custom-call | tf_op jit(solution)/shard_map/pallas_call | solution.py:268
  25.8 1.6 %shard_map.100 = bf16[8,64,128]{2,1,0:T(8,128)(2,1)} custom-call(s32[8,128]{1,0:T(8,128)S(4)} %get-tuple-element.36.refs_0_, s32[8,128]{1,0:T(8,128)S(4)} %get-tuple-element.43.refs_1_, bf16[3,40,128,128]{3,2,1,0:T(8,128)(2,1)} %bitcast.31, bf16[3,40,128,128]{3,2,1,0:T(8,128)(2,1)} %collective-permute-done.2.refs_3_, ...), custom_call_target="tpu_custom_call" | custom-call | tf_op jit(solution)/shard_map/pallas_call | solution.py:268
  27.4 5.2 %all-to-all-start.1 = ((bf16[8,64,128]{2,1,0:T(8,128)(2,1)}), bf16[8,64,128]{2,1,0:T(8,128)(2,1)S(1)}, u32[]{:S(2)}, u32[]{:S(2)}) async-start(bf16[8,64,128]{2,1,0:T(8,128)(2,1)} %shard_map.100), calls=%async_computation.1 | async-start | bytes 262144 | tf_op jit(solution)/shard_map/all_to_all | solution.py:357
  32.6 3.0 %shard_map.101 = (f32[8,128,128]{2,1,0:T(8,128)S(1)}, bf16[40,128,128]{2,1,0:T(8,128)(2,1)S(1)}) custom-call(s32[8,128]{1,0:T(8,128)S(4)} %get-tuple-element.36.refs_0_, s32[8,128]{1,0:T(8,128)S(4)} %get-tuple-element.43.refs_1_, bf16[3,40,128,128]{3,2,1,0:T(8,128)(2,1)} %bitcast.32, bf16[3,40,128,128]{3,2,1,0:T(8,128)(2,1)} %collective-permute-done.2.refs_3_, ...), custom_call_target="tpu_custom_call" | custom-call | tf_op jit(solution)/shard_map/pallas_call | solution.py:268
  35.6 2.3 %all-to-all-done.1.received = bf16[8,64,128]{2,1,0:T(8,128)(2,1)S(1)} async-done(((bf16[8,64,128]{2,1,0:T(8,128)(2,1)}), bf16[8,64,128]{2,1,0:T(8,128)(2,1)S(1)}, u32[]{:S(2)}, u32[]{:S(2)}) %all-to-all-start.1) | async-done | bytes 131104 | tf_op jit(solution)/shard_map/all_to_all | solution.py:357
  38.2 1.4 %collective-permute-start.8 = (bf16[64,128]{1,0:T(8,128)(2,1)S(1)}, bf16[64,128]{1,0:T(8,128)(2,1)S(1)}, u32[]{:S(2)}, u32[]{:S(2)}) collective-permute-start(bf16[64,128]{1,0:T(8,128)(2,1)S(1)} %shard_map.102.refs_4_.refs_5_.refs_0_), channel_id=1, source_target_pairs={{0,2},{1,3},{2,0},{3,1},{4,6},{5,7},{6,4},{7,5},{8,10},{9,11},{10,... | collective-permute-start | bytes 49160 | tf_op jit(solution)/shard_map/ppermute | solution.py:35
  39.6 1.6 %shard_map.103 = (f32[8,128,128]{2,1,0:T(8,128)S(1)}, bf16[40,128,128]{2,1,0:T(8,128)(2,1)S(1)}) custom-call(s32[8,128]{1,0:T(8,128)S(4)} %get-tuple-element.36.refs_0_, s32[8,128]{1,0:T(8,128)S(4)} %get-tuple-element.43.refs_1_, bf16[3,40,128,128]{3,2,1,0:T(8,128)(2,1)} %bitcast.33, bf16[3,40,128,128]{3,2,1,0:T(8,128)(2,1)} %collective-permute-done.2.refs_3_, ...), custom_call_target="tpu_custom_call" | custom-call | tf_op jit(solution)/shard_map/pallas_call | solution.py:268
  41.3 0.8 %collective-permute-done.8.refs_5_ = bf16[64,128]{1,0:T(8,128)(2,1)S(1)} collective-permute-done((bf16[64,128]{1,0:T(8,128)(2,1)S(1)}, bf16[64,128]{1,0:T(8,128)(2,1)S(1)}, u32[]{:S(2)}, u32[]{:S(2)}) %collective-permute-start.8) | collective-permute-done | bytes 16416 | tf_op jit(solution)/shard_map/ppermute | solution.py:35
  42.5 9.3 %all_to_all.15.received = bf16[8,64,128]{2,1,0:T(8,128)(2,1)S(1)} all-to-all(bf16[8,64,128]{2,1,0:T(8,128)(2,1)S(1)} %shard_map.104), channel_id=1, replica_groups={{16,20,24,28,0,4,8,12},{17,21,25,29,1,5,9,13},{18,22,26,30,2,6,10,14},{..., dimensions={0} | all-to-all | bytes 262144 | tf_op jit(solution)/shard_map/all_to_all | solution.py:357
  52.1 0.6 %maximum_bitcast_fusion = bf16[1,1,1,2,128,128]{5,4,3,2,1,0:T(8,128)(2,1)} fusion(bf16[1,128,128]{2,1,0:T(8,128)(2,1)S(1)} %bitcast.25, bf16[1,128,128]{2,1,0:T(8,128)(2,1)S(1)} %bitcast.18), kind=kLoop, calls=%fused_computation.1 | loop fusion | flops 32768 | bytes 131072 | tf_op jit(solution)/shard_map/broadcast_in_dim | solution.py:426
  52.8 0.6 %collective-permute-done.9.other = bf16[2,64,128]{2,1,0:T(8,128)(2,1)S(1)} collective-permute-done((bf16[2,64,128]{2,1,0:T(8,128)(2,1)S(1)}, bf16[2,64,128]{2,1,0:T(8,128)(2,1)S(1)}, u32[]{:S(2)}, u32[]{:S(2)}) %collective-permute-start.9) | collective-permute-done | bytes 32800 | tf_op jit(solution)/shard_map/ppermute | solution.py:40
  53.3 0.8 %shard_map.106 = bf16[1,1,2,128,128]{4,3,2,1,0:T(8,128)(2,1)} custom-call(bf16[2,64,128]{2,1,0:T(8,128)(2,1)S(1)} %shard_map.105.own, bf16[2,64,128]{2,1,0:T(8,128)(2,1)S(1)} %collective-permute-done.9.other), custom_call_target="tpu_custom_call" | custom-call | tf_op jit(solution)/shard_map/pallas_call | solution.py:342
  (23 shorter events, 2.4 us)
Async XLA Ops:
  1.5 16.3 %collective-permute-start.2 = (bf16[3,40,128,128]{3,2,1,0:T(8,128)(2,1)}, bf16[3,40,128,128]{3,2,1,0:T(8,128)(2,1)}, u32[]{:S(2)}, u32[]{:S(2)}) collective-permute-start(bf16[3,40,128,128]{3,2,1,0:T(8,128)(2,1)} %bitcast.26), channel_id=1, source_target_pairs={{0,1},{1,0},{2,3},{3,2},{4,5},{5,4},{6,7},{7,6},{8,9},{9,8},{10,11... | collective-permute-start | bytes 11796488 | tf_op jit(solution)/shard_map/ppermute | solution.py:40
  2.0 5.1 %collective-permute-start = (bf16[128,128]{1,0:T(8,128)(2,1)S(1)}, bf16[128,128]{1,0:T(8,128)(2,1)S(1)}, u32[]{:S(2)}, u32[]{:S(2)}) collective-permute-start(bf16[128,128]{1,0:T(8,128)(2,1)S(1)} %convolution_convert_fusion.refs_2_.refs_4_), channel_id=1, source_target_pairs={{0,2},{1,3},{2,0},{3,1},{4,6},{5,7},{6,4},{7,5},{8,10},{9,11},{10,... | collective-permute-start | bytes 98312 | tf_op jit(solution)/shard_map/ppermute | solution.py:35
  8.2 13.3 %all-to-all-start = ((bf16[8,128,128]{2,1,0:T(8,128)(2,1)}), bf16[8,128,128]{2,1,0:T(8,128)(2,1)S(1)}, u32[]{:S(2)}, u32[]{:S(2)}) async-start(bf16[8,128,128]{2,1,0:T(8,128)(2,1)} %shard_map.96), calls=%async_computation | async-start | bytes 524288 | tf_op jit(solution)/shard_map/all_to_all | solution.py:357
  14.4 7.1 %copy-start.2 = (bf16[1,1,1,2,128,128]{5,4,3,2,1,0:T(8,128)(2,1)S(1)}, bf16[1,1,1,2,128,128]{5,4,3,2,1,0:T(8,128)(2,1)}, u32[]{:S(2)}) copy-start(bf16[1,1,1,2,128,128]{5,4,3,2,1,0:T(8,128)(2,1)} %param.12) | copy-start | bytes 196612
  14.4 7.1 %copy-start.3 = (bf16[1,1,1,2,128,128]{5,4,3,2,1,0:T(8,128)(2,1)S(1)}, bf16[1,1,1,2,128,128]{5,4,3,2,1,0:T(8,128)(2,1)}, u32[]{:S(2)}) copy-start(bf16[1,1,1,2,128,128]{5,4,3,2,1,0:T(8,128)(2,1)} %param.14) | copy-start | bytes 196612
  14.4 2.8 %collective-permute-start.3 = (bf16[128,128]{1,0:T(8,128)(2,1)S(1)}, bf16[128,128]{1,0:T(8,128)(2,1)S(1)}, u32[]{:S(2)}, u32[]{:S(2)}) collective-permute-start(bf16[128,128]{1,0:T(8,128)(2,1)S(1)} %convolution_convert_fusion.refs_2_.refs_4_), channel_id=1, source_target_pairs={{0,1},{1,0},{2,3},{3,2},{4,5},{5,4},{6,7},{7,6},{8,9},{9,8},{10,11... | collective-permute-start | bytes 98312 | tf_op jit(solution)/shard_map/ppermute | solution.py:35
  14.4 3.4 %collective-permute-start.4 = (bf16[128,128]{1,0:T(8,128)(2,1)S(1)}, bf16[128,128]{1,0:T(8,128)(2,1)S(1)}, u32[]{:S(2)}, u32[]{:S(2)}) collective-permute-start(bf16[128,128]{1,0:T(8,128)(2,1)S(1)} %convolution_convert_fusion.refs_2_.refs_4_), channel_id=1, source_target_pairs={{0,3},{1,2},{2,1},{3,0},{4,7},{5,6},{6,5},{7,4},{8,11},{9,10},{10,... | collective-permute-start | bytes 98312 | tf_op jit(solution)/shard_map/ppermute | solution.py:35
  16.1 1.2 %collective-permute-start.1 = (s32[8,128]{1,0:T(8,128)S(1)}, s32[8,128]{1,0:T(8,128)S(1)}, u32[]{:S(2)}, u32[]{:S(2)}) collective-permute-start(s32[8,128]{1,0:T(8,128)S(1)} %get-tuple-element.40), channel_id=1, source_target_pairs={{0,1},{1,0},{2,3},{3,2},{4,5},{5,4},{6,7},{7,6},{8,9},{9,8},{10,11... | collective-permute-start | bytes 12296 | tf_op jit(solution)/shard_map/ppermute | solution.py:40
  21.9 3.9 %collective-permute-start.5 = (bf16[64,128]{1,0:T(8,128)(2,1)S(1)}, bf16[64,128]{1,0:T(8,128)(2,1)S(1)}, u32[]{:S(2)}, u32[]{:S(2)}) collective-permute-start(bf16[64,128]{1,0:T(8,128)(2,1)S(1)} %get-tuple-element.55.refs_4_.refs_5_.refs_8_), channel_id=1, source_target_pairs={{0,2},{1,3},{2,0},{3,1},{4,6},{5,7},{6,4},{7,5},{8,10},{9,11},{10,... | collective-permute-start | bytes 49160 | tf_op jit(solution)/shard_map/ppermute | solution.py:35
  22.4 3.4 %collective-permute-start.6 = (bf16[64,128]{1,0:T(8,128)(2,1)S(1)}, bf16[64,128]{1,0:T(8,128)(2,1)S(1)}, u32[]{:S(2)}, u32[]{:S(2)}) collective-permute-start(bf16[64,128]{1,0:T(8,128)(2,1)S(1)} %get-tuple-element.49), channel_id=1, source_target_pairs={{0,1},{1,0},{2,3},{3,2},{4,5},{5,4},{6,7},{7,6},{8,9},{9,8},{10,11... | collective-permute-start | bytes 49160 | tf_op jit(solution)/shard_map/ppermute | solution.py:35
  22.4 3.3 %collective-permute-start.7 = (bf16[64,128]{1,0:T(8,128)(2,1)S(1)}, bf16[64,128]{1,0:T(8,128)(2,1)S(1)}, u32[]{:S(2)}, u32[]{:S(2)}) collective-permute-start(bf16[64,128]{1,0:T(8,128)(2,1)S(1)} %get-tuple-element.49), channel_id=1, source_target_pairs={{0,3},{1,2},{2,1},{3,0},{4,7},{5,6},{6,5},{7,4},{8,11},{9,10},{10,... | collective-permute-start | bytes 49160 | tf_op jit(solution)/shard_map/ppermute | solution.py:35
  27.4 10.6 %all-to-all-start.1 = ((bf16[8,64,128]{2,1,0:T(8,128)(2,1)}), bf16[8,64,128]{2,1,0:T(8,128)(2,1)S(1)}, u32[]{:S(2)}, u32[]{:S(2)}) async-start(bf16[8,64,128]{2,1,0:T(8,128)(2,1)} %shard_map.100), calls=%async_computation.1 | async-start | bytes 262144 | tf_op jit(solution)/shard_map/all_to_all | solution.py:357
  32.6 5.4 %copy-start = (bf16[1,1,2,128,128]{4,3,2,1,0:T(8,128)(2,1)S(1)}, bf16[1,1,2,128,128]{4,3,2,1,0:T(8,128)(2,1)}, u32[]{:S(2)}) copy-start(bf16[1,1,2,128,128]{4,3,2,1,0:T(8,128)(2,1)} %param.13) | copy-start | bytes 196612
  32.6 5.4 %copy-start.1 = (bf16[1,1,2,128,128]{4,3,2,1,0:T(8,128)(2,1)S(1)}, bf16[1,1,2,128,128]{4,3,2,1,0:T(8,128)(2,1)}, u32[]{:S(2)}) copy-start(bf16[1,1,2,128,128]{4,3,2,1,0:T(8,128)(2,1)} %param.15) | copy-start | bytes 196612
  38.2 3.8 %collective-permute-start.8 = (bf16[64,128]{1,0:T(8,128)(2,1)S(1)}, bf16[64,128]{1,0:T(8,128)(2,1)S(1)}, u32[]{:S(2)}, u32[]{:S(2)}) collective-permute-start(bf16[64,128]{1,0:T(8,128)(2,1)S(1)} %shard_map.102.refs_4_.refs_5_.refs_0_), channel_id=1, source_target_pairs={{0,2},{1,3},{2,0},{3,1},{4,6},{5,7},{6,4},{7,5},{8,10},{9,11},{10,... | collective-permute-start | bytes 49160 | tf_op jit(solution)/shard_map/ppermute | solution.py:35
  52.1 1.2 %collective-permute-start.9 = (bf16[2,64,128]{2,1,0:T(8,128)(2,1)S(1)}, bf16[2,64,128]{2,1,0:T(8,128)(2,1)S(1)}, u32[]{:S(2)}, u32[]{:S(2)}) collective-permute-start(bf16[2,64,128]{2,1,0:T(8,128)(2,1)S(1)} %shard_map.105.own), channel_id=1, source_target_pairs={{0,1},{1,0},{2,3},{3,2},{4,5},{5,4},{6,7},{7,6},{8,9},{9,8},{10,11... | collective-permute-start | bytes 98312 | tf_op jit(solution)/shard_map/ppermute | solution.py:40

commit v5 on v4

--- a/solution.py
+++ b/solution.py
@@ -179,7 +179,13 @@
         loads[stages].start()
 
     for j, solution_ref in enumerate(solutions):
-        if form == "whole":
+        if len(solution_ref.shape) == 3:
+            depth = lax.axis_size("zgrid")
+            column = lax.rem(lax.axis_index("pcol") + j % cols, cols)
+            layer = lax.rem(lax.axis_index("zgrid") + (j // cols) % depth, depth)
+            value = solution_ref[column * depth + layer].astype(jnp.float32)
+            chosen[j] = unpacked(value).astype(jnp.bfloat16)
+        elif form == "whole":
             chosen[j] = solution_ref[...]
         elif solution_ref.shape == chosen.shape[1:]:
             chosen[j] = half_first(solution_ref[...].astype(jnp.float32)).astype(jnp.bfloat16)
@@ -285,15 +291,21 @@
     out[...] = found.astype(jnp.bfloat16)
     mine = half_first(found)
     kept[...] = packed(mine).astype(jnp.bfloat16)
-    sent[...] = packed(turned(mine)).astype(jnp.bfloat16)
+    halves = [packed(found).astype(jnp.bfloat16), packed(turned(found)).astype(jnp.bfloat16)]
+    for device in range(sent.shape[0]):
+        sent[device] = halves[device % 2]
 
 
 def sub_solve(received, given, inverse):
     _, width, sides = received.shape
-    half = jax.ShapeDtypeStruct((width // 2, sides), jnp.bfloat16)
+    devices = lax.axis_size("pcol") * lax.axis_size("zgrid")
     return pl.pallas_call(
         sub_solve_kernel,
-        out_shape=[jax.ShapeDtypeStruct((width, sides), jnp.bfloat16), half, half],
+        out_shape=[
+            jax.ShapeDtypeStruct((width, sides), jnp.bfloat16),
+            jax.ShapeDtypeStruct((width // 2, sides), jnp.bfloat16),
+            jax.ShapeDtypeStruct((devices, width // 2, sides), jnp.bfloat16),
+        ],
         in_specs=[vmem] * 3,
         out_specs=[vmem] * 3,
         compiler_params=params,
@@ -391,22 +403,21 @@
     )
     received, second, staged = lax.optimization_barrier((received, second, staged))
     level_one, one_kept, one_sent = sub_solve(received, right_sub, factor_sub)
-    one_own = sibling_values(one_kept, 0)
-    one_other = sibling_values(one_sent, 1)
+    one_row = lax.all_to_all(one_sent, ("pcol", "zgrid"), 0, 0, tiled=True)
 
     resident = {(0, 1): staged}
     second, resident[(1, 1)] = update(
         [(3, 0, 0)], plans, both, [[one_kept] * cols], second, row_count, "summed", resident, (1, 1)
     )
     send = update(
-        [(4, 0, 0), (3, 1, 1), (4, 1, 1)], plans, both, [one_own, one_other], second, row_count,
-        "half", resident, None,
-    )
-    send, one_own, one_other = lax.optimization_barrier((send, one_own, one_other))
+        [(4, 0, 0), (3, 1, 1), (4, 1, 1)], plans, both, [[one_row] * cols] * 2, second,
+        row_count, "half", resident, None,
+    )
+    send, one_row = lax.optimization_barrier((send, one_row))
     received = exchange(send)
     third, staged = update(
         [(2, 0, 0), (2, 1, 1), (5, 0, 2), (5, 1, 3)], plans, both,
-        [zero_own, zero_other, one_own, one_other], None, row_count, "summed", {}, (0, 2),
+        [zero_own, zero_other] + [[one_row] * cols] * 2, None, row_count, "summed", {}, (0, 2),
     )
     received, third, staged = lax.optimization_barrier((received, third, staged))
     level_two = half_solve(0, received, right_top, factor_top, None)

time: 54.9 us -> 60 us (1.093)
  waiting for transfers between devices: 7.22 us -> 9.18 us
  local copies, waits for them, and re-layouts: 0.01 us -> 1.86 us
  Pallas kernels: 15.4 us -> 17 us
    ppermute x7 -> x4, starting transfers between devices: 7.81 us -> 3.65 us  [sibling_values(): found.append(lax.ppermute(value, ('pcol', 'zgrid'), moves))]
    all_to_all x0 -> x1, starting transfers between devices: none -> 3.28 us  [local(): one_row = lax.all_to_all(one_sent, ('pcol', 'zgrid'), 0, 0, tiled=True)]
    all_to_all x0 -> x1, waiting for transfers between devices: none -> 1.92 us  [local(): one_row = lax.all_to_all(one_sent, ('pcol', 'zgrid'), 0, 0, tiled=True)]
    unnamed x8 -> x12, local copies, waits for them, and re-layouts: 0.01 us -> 1.86 us
    all_to_all x2, waiting for transfers between devices: 3.83 us -> 2.5 us  [exchange(): lax.all_to_all(send, 'prow', 0, 0, tiled=True, axis_index_groups=[order])]
    ppermute x7 -> x4, waiting for transfers between devices: 1.74 us -> 3.04 us  [sibling_values(): found.append(lax.ppermute(value, ('pcol', 'zgrid'), moves))]
    pallas_call x7, Pallas kernels: 11.2 us -> 12.2 us  [update(): pl.pallas_call(functools.partial(update_kernel, config), out_shape=outs,...]
    all_to_all x2, starting transfers between devices: 11.5 us -> 12.2 us  [exchange(): lax.all_to_all(send, 'prow', 0, 0, tiled=True, axis_index_groups=[order])]
  transfers between devices with their start and end apart: 12 -> 10, of which waited for: 7 -> 7; matrix products, arithmetic and copies ran while one was open for 1% -> 1% of each run, Pallas kernels for 22% -> 21%
where the time goes in v5:
time: 60 us; the launch traced here: 59.2 us
  starting transfers between devices  19.6 us (33%)
  Pallas kernels  17 us (28%)
  blocking collectives  9.27 us (15%)
  waiting for transfers between devices  9.18 us (15%)
  local copies, waits for them, and re-layouts  1.86 us (3%)
  matrix products  0.9 us (2%)
  between operations  0.75 us (1%)
  other arithmetic  0.64 us (1%)
    pallas_call x7, Pallas kernels, update(): pl.pallas_call(functools.partial(update_kernel, config), out_shape=outs,...  12.2 us
    all_to_all x2, starting transfers between devices, exchange(): lax.all_to_all(send, 'prow', 0, 0, tiled=True, axis_index_groups=[order])  12.2 us
    all_to_all x1, blocking collectives, exchange(): lax.all_to_all(send, 'prow', 0, 0, tiled=True, axis_index_groups=[order])  9.27 us
    ppermute x4, starting transfers between devices, sibling_values(): found.append(lax.ppermute(value, ('pcol', 'zgrid'), moves))  3.65 us
    all_to_all x1, starting transfers between devices, local(): one_row = lax.all_to_all(one_sent, ('pcol', 'zgrid'), 0, 0, tiled=True)  3.28 us
    ppermute x4, waiting for transfers between devices, sibling_values(): found.append(lax.ppermute(value, ('pcol', 'zgrid'), moves))  3.04 us
    all_to_all x2, waiting for transfers between devices, exchange(): lax.all_to_all(send, 'prow', 0, 0, tiled=True, axis_index_groups=[order])  2.5 us
    pallas_call x1, Pallas kernels, make_plan(): pl.pallas_call(functools.partial(plan_kernel, row_count, cols), out_shape...  2.49 us
  transfers between devices with their start and end apart: 10, of which 7 were waited for; matrix products, arithmetic and copies ran while one was open for 1% of the time, Pallas kernels for 21%

profile of v5, /device:TPU:0, one launch (start us, length us, event | category | flops | bytes accessed | tf_op | source)
XLA Modules:
  0.0 59.2 jit_solution(10185609236031322261)
XLA Ops:
  0.6 0.9 %convolution_convert_fusion.refs_2_.refs_4_ = bf16[128,128]{1,0:T(8,128)(2,1)S(1)} fusion(bf16[1,1,1,2,128,128]{5,4,3,2,1,0:T(8,128)(2,1)} %param.12, bf16[1,1,1,2,128,128]{5,4,3,2,1,0:T(8,128)(2,1)} %param.14), kind=kOutput, calls=%fused_computation | convolution fusion | flops 4210688 | bytes 98304 | tf_op jit(solution)/shard_map/dot_general | solution.py:364
  2.0 2.6 %collective-permute-start = (bf16[128,128]{1,0:T(8,128)(2,1)S(1)}, bf16[128,128]{1,0:T(8,128)(2,1)S(1)}, u32[]{:S(2)}, u32[]{:S(2)}) collective-permute-start(bf16[128,128]{1,0:T(8,128)(2,1)S(1)} %convolution_convert_fusion.refs_2_.refs_4_), channel_id=1, source_target_pairs={{0,2},{1,3},{2,0},{3,1},{4,6},{5,7},{6,4},{7,5},{8,10},{9,11},{10,... | collective-permute-start | bytes 98312 | tf_op jit(solution)/shard_map/ppermute | solution.py:35
  4.6 2.5 %shard_map.95 = (s32[8,128]{1,0:T(8,128)S(1)}, s32[8,128]{1,0:T(8,128)S(4)}, bf16[40,128,128]{2,1,0:T(8,128)(2,1)S(1)}) custom-call(s32[3,1,40]{2,1,0:T(1,128)} %bitcast.35, s32[3,1,40]{2,1,0:T(1,128)} %bitcast.36, s32[3]{0:T(128)} %bitcast.37, bf16[3,40,128,128]{3,2,1,0:T(8,128)(2,1)} %bitcast.27), custom_call_target="tpu_custom_call" | custom-call | tf_op jit(solution)/shard_map/pallas_call | solution.py:98
  7.1 1.0 %shard_map.96 = bf16[8,128,128]{2,1,0:T(8,128)(2,1)} custom-call(s32[8,128]{1,0:T(8,128)S(4)} %get-tuple-element.33.refs_0_, bf16[3,40,128,128]{3,2,1,0:T(8,128)(2,1)} %bitcast.28, bf16[128,128]{1,0:T(8,128)(2,1)S(1)} %convolution_convert_fusion.refs_2_.refs_4_, bf16[128,128]{1,0:T(8,128)(2,1)S(1)} %collective-permute-done.refs_3_.refs_5_, ...), custom_call_target="tpu_custom_call" | custom-call | tf_op jit(solution)/shard_map/pallas_call | solution.py:274
  8.1 6.9 %all-to-all-start = ((bf16[8,128,128]{2,1,0:T(8,128)(2,1)}), bf16[8,128,128]{2,1,0:T(8,128)(2,1)S(1)}, u32[]{:S(2)}, u32[]{:S(2)}) async-start(bf16[8,128,128]{2,1,0:T(8,128)(2,1)} %shard_map.96), calls=%async_computation | async-start | bytes 524288 | tf_op jit(solution)/shard_map/all_to_all | solution.py:369
  15.0 1.0 %collective-permute-start.3 = (bf16[128,128]{1,0:T(8,128)(2,1)S(1)}, bf16[128,128]{1,0:T(8,128)(2,1)S(1)}, u32[]{:S(2)}, u32[]{:S(2)}) collective-permute-start(bf16[128,128]{1,0:T(8,128)(2,1)S(1)} %convolution_convert_fusion.refs_2_.refs_4_), channel_id=1, source_target_pairs={{0,1},{1,0},{2,3},{3,2},{4,5},{5,4},{6,7},{7,6},{8,9},{9,8},{10,11... | collective-permute-start | bytes 98312 | tf_op jit(solution)/shard_map/ppermute | solution.py:35
  16.0 1.2 %collective-permute-done.1.refs_1_ = s32[8,128]{1,0:T(8,128)S(1)} collective-permute-done((s32[8,128]{1,0:T(8,128)S(1)}, s32[8,128]{1,0:T(8,128)S(1)}, u32[]{:S(2)}, u32[]{:S(2)}) %collective-permute-start.1) | collective-permute-done | bytes 4128 | tf_op jit(solution)/shard_map/ppermute | solution.py:40
  17.2 1.2 %collective-permute-done.4.refs_7_ = bf16[128,128]{1,0:T(8,128)(2,1)S(1)} collective-permute-done((bf16[128,128]{1,0:T(8,128)(2,1)S(1)}, bf16[128,128]{1,0:T(8,128)(2,1)S(1)}, u32[]{:S(2)}, u32[]{:S(2)}) %collective-permute-start.4) | collective-permute-done | bytes 32800 | tf_op jit(solution)/shard_map/ppermute | solution.py:35
  18.4 2.3 %shard_map.97 = (f32[8,128,128]{2,1,0:T(8,128)S(1)}, bf16[40,128,128]{2,1,0:T(8,128)(2,1)S(1)}, s32[8,128]{1,0:T(8,128)S(4)}) custom-call(s32[8,128]{1,0:T(8,128)S(4)} %get-tuple-element.33.refs_0_, s32[8,128]{1,0:T(8,128)S(1)} %collective-permute-done.1.refs_1_, bf16[3,40,128,128]{3,2,1,0:T(8,128)(2,1)} %bitcast.29, ...), custom_call_target="tpu_custom_call" | custom-call | tf_op jit(solution)/shard_map/pallas_call | solution.py:274
  20.7 1.0 %all-to-all-done.received = bf16[8,128,128]{2,1,0:T(8,128)(2,1)S(1)} async-done(((bf16[8,128,128]{2,1,0:T(8,128)(2,1)}), bf16[8,128,128]{2,1,0:T(8,128)(2,1)S(1)}, u32[]{:S(2)}, u32[]{:S(2)}) %all-to-all-start) | async-done | bytes 262176 | tf_op jit(solution)/shard_map/all_to_all | solution.py:369
  21.7 0.9 %shard_map.98 = (bf16[128,128]{1,0:T(8,128)(2,1)S(1)}, bf16[64,128]{1,0:T(8,128)(2,1)S(1)}, bf16[4,64,128]{2,1,0:T(8,128)(2,1)}) custom-call(bf16[8,128,128]{2,1,0:T(8,128)(2,1)S(1)} %all-to-all-done.received, bf16[2,128,128]{2,1,0:T(8,128)(2,1)S(1)} %bitcast.23, bf16[2,128,128]{2,1,0:T(8,128)(2,1)S(1)} %bitcast.24), custom_call_target="tpu_custom_call" | custom-call | tf_op jit(solution)/shard_map/pallas_call | solution.py:302
  22.6 3.3 %all-to-all-start.1 = ((bf16[4,64,128]{2,1,0:T(8,128)(2,1)}), bf16[4,64,128]{2,1,0:T(8,128)(2,1)S(1)}, u32[]{:S(2)}, u32[]{:S(2)}) async-start(bf16[4,64,128]{2,1,0:T(8,128)(2,1)} %get-tuple-element.45), calls=%async_computation.1 | async-start | bytes 131072 | tf_op jit(solution)/shard_map/all_to_all | solution.py:406
  25.9 1.3 %shard_map.99 = (f32[8,128,128]{2,1,0:T(8,128)S(1)}, bf16[40,128,128]{2,1,0:T(8,128)(2,1)S(1)}) custom-call(s32[8,128]{1,0:T(8,128)S(4)} %get-tuple-element.33.refs_0_, s32[8,128]{1,0:T(8,128)S(4)} %get-tuple-element.40.refs_1_, bf16[3,40,128,128]{3,2,1,0:T(8,128)(2,1)} %bitcast.30, bf16[3,40,128,128]{3,2,1,0:T(8,128)(2,1)} %collective-permute-done.2.refs_3_, ...), custom_call_target="tpu_custom_call" | custom-call | tf_op jit(solution)/shard_map/pallas_call | solution.py:274
  27.3 0.8 %copy-done = f32[8,128,128]{2,1,0:T(8,128)} copy-done((f32[8,128,128]{2,1,0:T(8,128)}, f32[8,128,128]{2,1,0:T(8,128)S(1)}, u32[]{:S(2)}) %copy-start) | copy-done | bytes 524312
  28.1 1.9 %all-to-all-done.1.refs_4_.refs_5_.refs_6_.refs_7_.refs_8_.refs_9_.refs_10_.refs_11_ = bf16[4,64,128]{2,1,0:T(8,128)(2,1)S(1)} async-done(((bf16[4,64,128]{2,1,0:T(8,128)(2,1)}), bf16[4,64,128]{2,1,0:T(8,128)(2,1)S(1)}, u32[]{:S(2)}, u32[]{:S(2)}) %all-to-all-start.1) | async-done | bytes 65568 | tf_op jit(solution)/shard_map/all_to_all | solution.py:406
  30.0 1.0 %copy-done.1 = f32[8,128,128]{2,1,0:T(8,128)S(1)} copy-done((f32[8,128,128]{2,1,0:T(8,128)S(1)}, f32[8,128,128]{2,1,0:T(8,128)}, u32[]{:S(2)}) %copy-start.1) | copy-done | bytes 524312
  31.1 1.8 %shard_map.100 = bf16[8,64,128]{2,1,0:T(8,128)(2,1)} custom-call(s32[8,128]{1,0:T(8,128)S(4)} %get-tuple-element.33.refs_0_, s32[8,128]{1,0:T(8,128)S(4)} %get-tuple-element.40.refs_1_, bf16[3,40,128,128]{3,2,1,0:T(8,128)(2,1)} %bitcast.31, bf16[3,40,128,128]{3,2,1,0:T(8,128)(2,1)} %collective-permute-done.2.refs_3_, ...), custom_call_target="tpu_custom_call" | custom-call | tf_op jit(solution)/shard_map/pallas_call | solution.py:274
  32.9 5.3 %all-to-all-start.2 = ((bf16[8,64,128]{2,1,0:T(8,128)(2,1)}), bf16[8,64,128]{2,1,0:T(8,128)(2,1)S(1)}, u32[]{:S(2)}, u32[]{:S(2)}) async-start(bf16[8,64,128]{2,1,0:T(8,128)(2,1)} %shard_map.100), calls=%async_computation.2 | async-start | bytes 262144 | tf_op jit(solution)/shard_map/all_to_all | solution.py:369
  38.2 3.5 %shard_map.101 = (f32[8,128,128]{2,1,0:T(8,128)S(1)}, bf16[40,128,128]{2,1,0:T(8,128)(2,1)S(1)}) custom-call(s32[8,128]{1,0:T(8,128)S(4)} %get-tuple-element.33.refs_0_, s32[8,128]{1,0:T(8,128)S(4)} %get-tuple-element.40.refs_1_, bf16[3,40,128,128]{3,2,1,0:T(8,128)(2,1)} %bitcast.32, bf16[3,40,128,128]{3,2,1,0:T(8,128)(2,1)} %collective-permute-done.2.refs_3_, ...), custom_call_target="tpu_custom_call" | custom-call | tf_op jit(solution)/shard_map/pallas_call | solution.py:274
  41.7 1.5 %all-to-all-done.2.received = bf16[8,64,128]{2,1,0:T(8,128)(2,1)S(1)} async-done(((bf16[8,64,128]{2,1,0:T(8,128)(2,1)}), bf16[8,64,128]{2,1,0:T(8,128)(2,1)S(1)}, u32[]{:S(2)}, u32[]{:S(2)}) %all-to-all-start.2) | async-done | bytes 131104 | tf_op jit(solution)/shard_map/all_to_all | solution.py:369
  43.5 1.8 %shard_map.103 = (f32[8,128,128]{2,1,0:T(8,128)S(1)}, bf16[40,128,128]{2,1,0:T(8,128)(2,1)S(1)}) custom-call(s32[8,128]{1,0:T(8,128)S(4)} %get-tuple-element.33.refs_0_, s32[8,128]{1,0:T(8,128)S(4)} %get-tuple-element.40.refs_1_, bf16[3,40,128,128]{3,2,1,0:T(8,128)(2,1)} %bitcast.33, bf16[3,40,128,128]{3,2,1,0:T(8,128)(2,1)} %collective-permute-done.2.refs_3_, ...), custom_call_target="tpu_custom_call" | custom-call | tf_op jit(solution)/shard_map/pallas_call | solution.py:274
  45.3 1.9 %collective-permute-done.5.refs_5_ = bf16[64,128]{1,0:T(8,128)(2,1)S(1)} collective-permute-done((bf16[64,128]{1,0:T(8,128)(2,1)S(1)}, bf16[64,128]{1,0:T(8,128)(2,1)S(1)}, u32[]{:S(2)}, u32[]{:S(2)}) %collective-permute-start.5) | collective-permute-done | bytes 16416 | tf_op jit(solution)/shard_map/ppermute | solution.py:35
  47.7 9.3 %all_to_all.20.received = bf16[8,64,128]{2,1,0:T(8,128)(2,1)S(1)} all-to-all(bf16[8,64,128]{2,1,0:T(8,128)(2,1)S(1)} %shard_map.104), channel_id=1, replica_groups={{16,20,24,28,0,4,8,12},{17,21,25,29,1,5,9,13},{18,22,26,30,2,6,10,14},{..., dimensions={0} | all-to-all | bytes 262144 | tf_op jit(solution)/shard_map/all_to_all | solution.py:369
  58.5 0.8 %shard_map.106 = bf16[1,1,2,128,128]{4,3,2,1,0:T(8,128)(2,1)} custom-call(bf16[2,64,128]{2,1,0:T(8,128)(2,1)S(1)} %shard_map.105.own, bf16[2,64,128]{2,1,0:T(8,128)(2,1)S(1)} %collective-permute-done.6.other), custom_call_target="tpu_custom_call" | custom-call | tf_op jit(solution)/shard_map/pallas_call | solution.py:354
  (23 shorter events, 2.8 us)
Async XLA Ops:
  1.5 16.8 %collective-permute-start.2 = (bf16[3,40,128,128]{3,2,1,0:T(8,128)(2,1)}, bf16[3,40,128,128]{3,2,1,0:T(8,128)(2,1)}, u32[]{:S(2)}, u32[]{:S(2)}) collective-permute-start(bf16[3,40,128,128]{3,2,1,0:T(8,128)(2,1)} %bitcast.26), channel_id=1, source_target_pairs={{0,1},{1,0},{2,3},{3,2},{4,5},{5,4},{6,7},{7,6},{8,9},{9,8},{10,11... | collective-permute-start | bytes 11796488 | tf_op jit(solution)/shard_map/ppermute | solution.py:40
  2.0 5.1 %collective-permute-start = (bf16[128,128]{1,0:T(8,128)(2,1)S(1)}, bf16[128,128]{1,0:T(8,128)(2,1)S(1)}, u32[]{:S(2)}, u32[]{:S(2)}) collective-permute-start(bf16[128,128]{1,0:T(8,128)(2,1)S(1)} %convolution_convert_fusion.refs_2_.refs_4_), channel_id=1, source_target_pairs={{0,2},{1,3},{2,0},{3,1},{4,6},{5,7},{6,4},{7,5},{8,10},{9,11},{10,... | collective-permute-start | bytes 98312 | tf_op jit(solution)/shard_map/ppermute | solution.py:35
  8.1 13.5 %all-to-all-start = ((bf16[8,128,128]{2,1,0:T(8,128)(2,1)}), bf16[8,128,128]{2,1,0:T(8,128)(2,1)S(1)}, u32[]{:S(2)}, u32[]{:S(2)}) async-start(bf16[8,128,128]{2,1,0:T(8,128)(2,1)} %shard_map.96), calls=%async_computation | async-start | bytes 524288 | tf_op jit(solution)/shard_map/all_to_all | solution.py:369
  15.0 6.7 %copy-start.4 = (bf16[1,1,1,2,128,128]{5,4,3,2,1,0:T(8,128)(2,1)S(1)}, bf16[1,1,1,2,128,128]{5,4,3,2,1,0:T(8,128)(2,1)}, u32[]{:S(2)}) copy-start(bf16[1,1,1,2,128,128]{5,4,3,2,1,0:T(8,128)(2,1)} %param.12) | copy-start | bytes 196612
  15.0 6.7 %copy-start.5 = (bf16[1,1,1,2,128,128]{5,4,3,2,1,0:T(8,128)(2,1)S(1)}, bf16[1,1,1,2,128,128]{5,4,3,2,1,0:T(8,128)(2,1)}, u32[]{:S(2)}) copy-start(bf16[1,1,1,2,128,128]{5,4,3,2,1,0:T(8,128)(2,1)} %param.14) | copy-start | bytes 196612
  15.0 3.3 %collective-permute-start.4 = (bf16[128,128]{1,0:T(8,128)(2,1)S(1)}, bf16[128,128]{1,0:T(8,128)(2,1)S(1)}, u32[]{:S(2)}, u32[]{:S(2)}) collective-permute-start(bf16[128,128]{1,0:T(8,128)(2,1)S(1)} %convolution_convert_fusion.refs_2_.refs_4_), channel_id=1, source_target_pairs={{0,3},{1,2},{2,1},{3,0},{4,7},{5,6},{6,5},{7,4},{8,11},{9,10},{10,... | collective-permute-start | bytes 98312 | tf_op jit(solution)/shard_map/ppermute | solution.py:35
  15.0 3.3 %collective-permute-start.3 = (bf16[128,128]{1,0:T(8,128)(2,1)S(1)}, bf16[128,128]{1,0:T(8,128)(2,1)S(1)}, u32[]{:S(2)}, u32[]{:S(2)}) collective-permute-start(bf16[128,128]{1,0:T(8,128)(2,1)S(1)} %convolution_convert_fusion.refs_2_.refs_4_), channel_id=1, source_target_pairs={{0,1},{1,0},{2,3},{3,2},{4,5},{5,4},{6,7},{7,6},{8,9},{9,8},{10,11... | collective-permute-start | bytes 98312 | tf_op jit(solution)/shard_map/ppermute | solution.py:35
  16.0 1.2 %collective-permute-start.1 = (s32[8,128]{1,0:T(8,128)S(1)}, s32[8,128]{1,0:T(8,128)S(1)}, u32[]{:S(2)}, u32[]{:S(2)}) collective-permute-start(s32[8,128]{1,0:T(8,128)S(1)} %get-tuple-element.37), channel_id=1, source_target_pairs={{0,1},{1,0},{2,3},{3,2},{4,5},{5,4},{6,7},{7,6},{8,9},{9,8},{10,11... | collective-permute-start | bytes 12296 | tf_op jit(solution)/shard_map/ppermute | solution.py:40
  22.6 7.4 %all-to-all-start.1 = ((bf16[4,64,128]{2,1,0:T(8,128)(2,1)}), bf16[4,64,128]{2,1,0:T(8,128)(2,1)S(1)}, u32[]{:S(2)}, u32[]{:S(2)}) async-start(bf16[4,64,128]{2,1,0:T(8,128)(2,1)} %get-tuple-element.45), calls=%async_computation.1 | async-start | bytes 131072 | tf_op jit(solution)/shard_map/all_to_all | solution.py:406
  27.3 0.8 %copy-start = (f32[8,128,128]{2,1,0:T(8,128)}, f32[8,128,128]{2,1,0:T(8,128)S(1)}, u32[]{:S(2)}) copy-start(f32[8,128,128]{2,1,0:T(8,128)S(1)} %get-tuple-element.50.refs_10_) | copy-start | bytes 1572868
  30.0 1.0 %copy-start.1 = (f32[8,128,128]{2,1,0:T(8,128)S(1)}, f32[8,128,128]{2,1,0:T(8,128)}, u32[]{:S(2)}) copy-start(f32[8,128,128]{2,1,0:T(8,128)} %copy-done) | copy-start | bytes 1572868
  32.9 10.3 %all-to-all-start.2 = ((bf16[8,64,128]{2,1,0:T(8,128)(2,1)}), bf16[8,64,128]{2,1,0:T(8,128)(2,1)S(1)}, u32[]{:S(2)}, u32[]{:S(2)}) async-start(bf16[8,64,128]{2,1,0:T(8,128)(2,1)} %shard_map.100), calls=%async_computation.2 | async-start | bytes 262144 | tf_op jit(solution)/shard_map/all_to_all | solution.py:369
  38.2 5.0 %copy-start.2 = (bf16[1,1,2,128,128]{4,3,2,1,0:T(8,128)(2,1)S(1)}, bf16[1,1,2,128,128]{4,3,2,1,0:T(8,128)(2,1)}, u32[]{:S(2)}) copy-start(bf16[1,1,2,128,128]{4,3,2,1,0:T(8,128)(2,1)} %param.13) | copy-start | bytes 196612
  38.2 5.0 %copy-start.3 = (bf16[1,1,2,128,128]{4,3,2,1,0:T(8,128)(2,1)S(1)}, bf16[1,1,2,128,128]{4,3,2,1,0:T(8,128)(2,1)}, u32[]{:S(2)}) copy-start(bf16[1,1,2,128,128]{4,3,2,1,0:T(8,128)(2,1)} %param.15) | copy-start | bytes 196612
  43.4 3.8 %collective-permute-start.5 = (bf16[64,128]{1,0:T(8,128)(2,1)S(1)}, bf16[64,128]{1,0:T(8,128)(2,1)S(1)}, u32[]{:S(2)}, u32[]{:S(2)}) collective-permute-start(bf16[64,128]{1,0:T(8,128)(2,1)S(1)} %shard_map.102.refs_4_.refs_5_.refs_0_), channel_id=1, source_target_pairs={{0,2},{1,3},{2,0},{3,1},{4,6},{5,7},{6,4},{7,5},{8,10},{9,11},{10,... | collective-permute-start | bytes 49160 | tf_op jit(solution)/shard_map/ppermute | solution.py:35
  57.2 1.2 %collective-permute-start.6 = (bf16[2,64,128]{2,1,0:T(8,128)(2,1)S(1)}, bf16[2,64,128]{2,1,0:T(8,128)(2,1)S(1)}, u32[]{:S(2)}, u32[]{:S(2)}) collective-permute-start(bf16[2,64,128]{2,1,0:T(8,128)(2,1)S(1)} %shard_map.105.own), channel_id=1, source_target_pairs={{0,1},{1,0},{2,3},{3,2},{4,5},{5,4},{6,7},{7,6},{8,9},{9,8},{10,11... | collective-permute-start | bytes 98312 | tf_op jit(solution)/shard_map/ppermute | solution.py:40

commit v6 on v4

--- a/solution.py
+++ b/solution.py
@@ -276,6 +276,34 @@
     return found if len(outs) > 1 else found[0]
 
 
+def first_solve_kernel(given, inverse, out, right, factor, semaphores):
+    loads = [
+        pltpu.make_async_copy(given.at[0], right, semaphores.at[0]),
+        pltpu.make_async_copy(inverse.at[0], factor, semaphores.at[1]),
+    ]
+    for load in loads:
+        load.start()
+    for load in loads:
+        load.wait()
+    out[...] = solve_block(factor[...], right[...])
+
+
+def first_solve(given, inverse):
+    shape = given.shape[1:]
+    return pl.pallas_call(
+        first_solve_kernel,
+        out_shape=jax.ShapeDtypeStruct(shape, jnp.bfloat16),
+        in_specs=[hbm] * 2,
+        out_specs=vmem,
+        scratch_shapes=[
+            pltpu.VMEM(shape, jnp.bfloat16),
+            pltpu.VMEM(inverse.shape[1:], jnp.bfloat16),
+            pltpu.SemaphoreType.DMA((2,)),
+        ],
+        compiler_params=params,
+    )(in_hbm(given), in_hbm(inverse))
+
+
 def sub_solve_kernel(received, given, inverse, out, kept, sent):
     incoming = received[0].astype(jnp.float32)
     for row in range(1, received.shape[0]):
@@ -367,7 +395,7 @@
     right_top = given_top[0, 0]
     factor_top = inverse_top[0, 0]
 
-    level_zero = solve_block(factor_sub[0], right_sub[0])
+    level_zero = first_solve(right_sub, factor_sub)
     zero_own = sibling_values(level_zero, 0)
     block_own = in_hbm(block_set)
     block_sent, level_zero = lax.optimization_barrier((block_set, level_zero))

time: 54.9 us -> 55.4 us (level)
  starting transfers between devices: 19.9 us -> 21.2 us
  matrix products: 0.9 us -> 0 us
  Pallas kernels: 15.4 us -> 16 us
    all_to_all x2, starting transfers between devices: 11.5 us -> 12.7 us  [exchange(): lax.all_to_all(send, 'prow', 0, 0, tiled=True, axis_index_groups=[order])]
    pallas_call x0 -> x1, Pallas kernels: none -> 0.93 us  [first_solve(): pl.pallas_call(first_solve_kernel, out_shape=jax.ShapeDtypeStruct(shape,...]
    dot_general x1 -> x0, matrix products: 0.9 us -> none  [solve_block(): jnp.dot(inverse, residual, preferred_element_type=jnp.float32)]
  transfers between devices with their start and end apart: 12 -> 12, of which waited for: 7 -> 7; matrix products, arithmetic and copies ran while one was open for 1% -> 1% of each run, Pallas kernels for 22% -> 20%
where the time goes in v6:
time: 55.4 us; the launch traced here: 54.6 us
  starting transfers between devices  21.2 us (38%)
  Pallas kernels  16 us (29%)
  blocking collectives  9.07 us (16%)
  waiting for transfers between devices  7 us (13%)
  between operations  0.75 us (1%)
  other arithmetic  0.64 us (1%)
    all_to_all x2, starting transfers between devices, exchange(): lax.all_to_all(send, 'prow', 0, 0, tiled=True, axis_index_groups=[order])  12.7 us
    pallas_call x7, Pallas kernels, update(): pl.pallas_call(functools.partial(update_kernel, config), out_shape=outs,...  11.1 us
    all_to_all x1, blocking collectives, exchange(): lax.all_to_all(send, 'prow', 0, 0, tiled=True, axis_index_groups=[order])  9.07 us
    ppermute x7, starting transfers between devices, sibling_values(): found.append(lax.ppermute(value, ('pcol', 'zgrid'), moves))  7.9 us
    all_to_all x2, waiting for transfers between devices, exchange(): lax.all_to_all(send, 'prow', 0, 0, tiled=True, axis_index_groups=[order])  3.72 us
    pallas_call x1, Pallas kernels, make_plan(): pl.pallas_call(functools.partial(plan_kernel, row_count, cols), out_shape...  2.18 us
    ppermute x3, waiting for transfers between devices, from_other_core(): return lax.ppermute(value, 'zgrid', [(0, 1), (1, 0)])  1.65 us
    ppermute x7, waiting for transfers between devices, sibling_values(): found.append(lax.ppermute(value, ('pcol', 'zgrid'), moves))  1.64 us
  transfers between devices with their start and end apart: 12, of which 7 were waited for; matrix products, arithmetic and copies ran while one was open for 1% of the time, Pallas kernels for 20%

profile of v6, /device:TPU:0, one launch (start us, length us, event | category | flops | bytes accessed | tf_op | source)
XLA Modules:
  0.0 54.6 jit_solution(17346071005317160572)
XLA Ops:
  0.6 0.9 %shard_map.96.refs_2_.refs_4_ = bf16[128,128]{1,0:T(8,128)(2,1)S(1)} custom-call(bf16[2,128,128]{2,1,0:T(8,128)(2,1)} %bitcast.17, bf16[2,128,128]{2,1,0:T(8,128)(2,1)} %bitcast.19), custom_call_target="tpu_custom_call" | custom-call | tf_op jit(solution)/shard_map/pallas_call | solution.py:293
  1.6 0.5 collective-permute-start.2
  2.1 2.6 %collective-permute-start = (bf16[128,128]{1,0:T(8,128)(2,1)S(1)}, bf16[128,128]{1,0:T(8,128)(2,1)S(1)}, u32[]{:S(2)}, u32[]{:S(2)}) collective-permute-start(bf16[128,128]{1,0:T(8,128)(2,1)S(1)} %shard_map.96.refs_2_.refs_4_), channel_id=1, source_target_pairs={{0,2},{1,3},{2,0},{3,1},{4,6},{5,7},{6,4},{7,5},{8,10},{9,11},{10,... | collective-permute-start | bytes 98312 | tf_op jit(solution)/shard_map/ppermute | solution.py:35
  4.7 2.2 %shard_map.95 = (s32[8,128]{1,0:T(8,128)S(1)}, s32[8,128]{1,0:T(8,128)S(4)}, bf16[40,128,128]{2,1,0:T(8,128)(2,1)S(1)}) custom-call(s32[3,1,40]{2,1,0:T(1,128)} %bitcast.31, s32[3,1,40]{2,1,0:T(1,128)} %bitcast.32, s32[3]{0:T(128)} %bitcast.33, bf16[3,40,128,128]{3,2,1,0:T(8,128)(2,1)} %bitcast.23), custom_call_target="tpu_custom_call" | custom-call | tf_op jit(solution)/shard_map/pallas_call | solution.py:98
  6.9 0.8 %shard_map.97 = bf16[8,128,128]{2,1,0:T(8,128)(2,1)} custom-call(s32[8,128]{1,0:T(8,128)S(4)} %get-tuple-element.36.refs_0_, bf16[3,40,128,128]{3,2,1,0:T(8,128)(2,1)} %bitcast.24, bf16[128,128]{1,0:T(8,128)(2,1)S(1)} %shard_map.96.refs_2_.refs_4_, bf16[128,128]{1,0:T(8,128)(2,1)S(1)} %collective-permute-done.refs_3_.refs_5_, ...), custom_call_target="tpu_custom_call" | custom-call | tf_op jit(solution)/shard_map/pallas_call | solution.py:268
  7.7 7.1 %all-to-all-start = ((bf16[8,128,128]{2,1,0:T(8,128)(2,1)}), bf16[8,128,128]{2,1,0:T(8,128)(2,1)S(1)}, u32[]{:S(2)}, u32[]{:S(2)}) async-start(bf16[8,128,128]{2,1,0:T(8,128)(2,1)} %shard_map.97), calls=%async_computation | async-start | bytes 524288 | tf_op jit(solution)/shard_map/all_to_all | solution.py:385
  15.0 1.2 %collective-permute-start.4 = (bf16[128,128]{1,0:T(8,128)(2,1)S(1)}, bf16[128,128]{1,0:T(8,128)(2,1)S(1)}, u32[]{:S(2)}, u32[]{:S(2)}) collective-permute-start(bf16[128,128]{1,0:T(8,128)(2,1)S(1)} %shard_map.96.refs_2_.refs_4_), channel_id=1, source_target_pairs={{0,3},{1,2},{2,1},{3,0},{4,7},{5,6},{6,5},{7,4},{8,11},{9,10},{10,... | collective-permute-start | bytes 98312 | tf_op jit(solution)/shard_map/ppermute | solution.py:35
  16.2 1.1 %collective-permute-done.1.refs_1_ = s32[8,128]{1,0:T(8,128)S(1)} collective-permute-done((s32[8,128]{1,0:T(8,128)S(1)}, s32[8,128]{1,0:T(8,128)S(1)}, u32[]{:S(2)}, u32[]{:S(2)}) %collective-permute-start.1) | collective-permute-done | bytes 4128 | tf_op jit(solution)/shard_map/ppermute | solution.py:40
  17.3 1.0 %collective-permute-done.4.refs_7_ = bf16[128,128]{1,0:T(8,128)(2,1)S(1)} collective-permute-done((bf16[128,128]{1,0:T(8,128)(2,1)S(1)}, bf16[128,128]{1,0:T(8,128)(2,1)S(1)}, u32[]{:S(2)}, u32[]{:S(2)}) %collective-permute-start.4) | collective-permute-done | bytes 32800 | tf_op jit(solution)/shard_map/ppermute | solution.py:35
  18.3 2.2 %shard_map.98 = (f32[8,128,128]{2,1,0:T(8,128)S(1)}, bf16[40,128,128]{2,1,0:T(8,128)(2,1)S(1)}, s32[8,128]{1,0:T(8,128)S(4)}) custom-call(s32[8,128]{1,0:T(8,128)S(4)} %get-tuple-element.36.refs_0_, s32[8,128]{1,0:T(8,128)S(1)} %collective-permute-done.1.refs_1_, bf16[3,40,128,128]{3,2,1,0:T(8,128)(2,1)} %bitcast.25, ...), custom_call_target="tpu_custom_call" | custom-call | tf_op jit(solution)/shard_map/pallas_call | solution.py:268
  20.5 1.7 %all-to-all-done.received = bf16[8,128,128]{2,1,0:T(8,128)(2,1)S(1)} async-done(((bf16[8,128,128]{2,1,0:T(8,128)(2,1)}), bf16[8,128,128]{2,1,0:T(8,128)(2,1)S(1)}, u32[]{:S(2)}, u32[]{:S(2)}) %all-to-all-start) | async-done | bytes 262176 | tf_op jit(solution)/shard_map/all_to_all | solution.py:385
  22.8 2.0 %collective-permute-start.7 = (bf16[64,128]{1,0:T(8,128)(2,1)S(1)}, bf16[64,128]{1,0:T(8,128)(2,1)S(1)}, u32[]{:S(2)}, u32[]{:S(2)}) collective-permute-start(bf16[64,128]{1,0:T(8,128)(2,1)S(1)} %get-tuple-element.49), channel_id=1, source_target_pairs={{0,3},{1,2},{2,1},{3,0},{4,7},{5,6},{6,5},{7,4},{8,11},{9,10},{10,... | collective-permute-start | bytes 49160 | tf_op jit(solution)/shard_map/ppermute | solution.py:35
  24.8 1.3 %shard_map.100 = (f32[8,128,128]{2,1,0:T(8,128)S(1)}, bf16[40,128,128]{2,1,0:T(8,128)(2,1)S(1)}) custom-call(s32[8,128]{1,0:T(8,128)S(4)} %get-tuple-element.36.refs_0_, s32[8,128]{1,0:T(8,128)S(4)} %get-tuple-element.43.refs_1_, bf16[3,40,128,128]{3,2,1,0:T(8,128)(2,1)} %bitcast.26, bf16[3,40,128,128]{3,2,1,0:T(8,128)(2,1)} %collective-permute-done.2.refs_3_, ...), custom_call_target="tpu_custom_call" | custom-call | tf_op jit(solution)/shard_map/pallas_call | solution.py:268
  26.4 1.6 %shard_map.101 = bf16[8,64,128]{2,1,0:T(8,128)(2,1)} custom-call(s32[8,128]{1,0:T(8,128)S(4)} %get-tuple-element.36.refs_0_, s32[8,128]{1,0:T(8,128)S(4)} %get-tuple-element.43.refs_1_, bf16[3,40,128,128]{3,2,1,0:T(8,128)(2,1)} %bitcast.27, bf16[3,40,128,128]{3,2,1,0:T(8,128)(2,1)} %collective-permute-done.2.refs_3_, ...), custom_call_target="tpu_custom_call" | custom-call | tf_op jit(solution)/shard_map/pallas_call | solution.py:268
  28.0 5.5 %all-to-all-start.1 = ((bf16[8,64,128]{2,1,0:T(8,128)(2,1)}), bf16[8,64,128]{2,1,0:T(8,128)(2,1)S(1)}, u32[]{:S(2)}, u32[]{:S(2)}) async-start(bf16[8,64,128]{2,1,0:T(8,128)(2,1)} %shard_map.101), calls=%async_computation.1 | async-start | bytes 262144 | tf_op jit(solution)/shard_map/all_to_all | solution.py:385
  33.5 3.0 %shard_map.102 = (f32[8,128,128]{2,1,0:T(8,128)S(1)}, bf16[40,128,128]{2,1,0:T(8,128)(2,1)S(1)}) custom-call(s32[8,128]{1,0:T(8,128)S(4)} %get-tuple-element.36.refs_0_, s32[8,128]{1,0:T(8,128)S(4)} %get-tuple-element.43.refs_1_, bf16[3,40,128,128]{3,2,1,0:T(8,128)(2,1)} %bitcast.28, bf16[3,40,128,128]{3,2,1,0:T(8,128)(2,1)} %collective-permute-done.2.refs_3_, ...), custom_call_target="tpu_custom_call" | custom-call | tf_op jit(solution)/shard_map/pallas_call | solution.py:268
  36.5 2.0 %all-to-all-done.1.received = bf16[8,64,128]{2,1,0:T(8,128)(2,1)S(1)} async-done(((bf16[8,64,128]{2,1,0:T(8,128)(2,1)}), bf16[8,64,128]{2,1,0:T(8,128)(2,1)S(1)}, u32[]{:S(2)}, u32[]{:S(2)}) %all-to-all-start.1) | async-done | bytes 131104 | tf_op jit(solution)/shard_map/all_to_all | solution.py:385
  38.8 1.8 %collective-permute-start.8 = (bf16[64,128]{1,0:T(8,128)(2,1)S(1)}, bf16[64,128]{1,0:T(8,128)(2,1)S(1)}, u32[]{:S(2)}, u32[]{:S(2)}) collective-permute-start(bf16[64,128]{1,0:T(8,128)(2,1)S(1)} %shard_map.103.refs_4_.refs_5_.refs_0_), channel_id=1, source_target_pairs={{0,2},{1,3},{2,0},{3,1},{4,6},{5,7},{6,4},{7,5},{8,10},{9,11},{10,... | collective-permute-start | bytes 49160 | tf_op jit(solution)/shard_map/ppermute | solution.py:35
  40.6 1.6 %shard_map.104 = (f32[8,128,128]{2,1,0:T(8,128)S(1)}, bf16[40,128,128]{2,1,0:T(8,128)(2,1)S(1)}) custom-call(s32[8,128]{1,0:T(8,128)S(4)} %get-tuple-element.36.refs_0_, s32[8,128]{1,0:T(8,128)S(4)} %get-tuple-element.43.refs_1_, bf16[3,40,128,128]{3,2,1,0:T(8,128)(2,1)} %bitcast.29, bf16[3,40,128,128]{3,2,1,0:T(8,128)(2,1)} %collective-permute-done.2.refs_3_, ...), custom_call_target="tpu_custom_call" | custom-call | tf_op jit(solution)/shard_map/pallas_call | solution.py:268
  42.6 0.7 %shard_map.105 = bf16[8,64,128]{2,1,0:T(8,128)(2,1)S(1)} custom-call(s32[8,128]{1,0:T(8,128)S(4)} %get-tuple-element.36.refs_0_, s32[8,128]{1,0:T(8,128)S(4)} %get-tuple-element.43.refs_1_, bf16[3,40,128,128]{3,2,1,0:T(8,128)(2,1)} %bitcast.30, bf16[3,40,128,128]{3,2,1,0:T(8,128)(2,1)} %collective-permute-done.2.refs_3_, ...), custom_call_target="tpu_custom_call" | custom-call | tf_op jit(solution)/shard_map/pallas_call | solution.py:268
  43.3 9.1 %all_to_all.15.received = bf16[8,64,128]{2,1,0:T(8,128)(2,1)S(1)} all-to-all(bf16[8,64,128]{2,1,0:T(8,128)(2,1)S(1)} %shard_map.105), channel_id=1, replica_groups={{16,20,24,28,0,4,8,12},{17,21,25,29,1,5,9,13},{18,22,26,30,2,6,10,14},{..., dimensions={0} | all-to-all | bytes 262144 | tf_op jit(solution)/shard_map/all_to_all | solution.py:385
  52.7 0.6 %maximum_bitcast_fusion = bf16[1,1,1,2,128,128]{5,4,3,2,1,0:T(8,128)(2,1)} fusion(bf16[1,128,128]{2,1,0:T(8,128)(2,1)S(1)} %bitcast.21, bf16[1,128,128]{2,1,0:T(8,128)(2,1)S(1)} %bitcast.12), kind=kLoop, calls=%fused_computation | loop fusion | flops 32768 | bytes 131072 | tf_op jit(solution)/shard_map/broadcast_in_dim | solution.py:454
  53.3 0.6 %collective-permute-done.9.other = bf16[2,64,128]{2,1,0:T(8,128)(2,1)S(1)} collective-permute-done((bf16[2,64,128]{2,1,0:T(8,128)(2,1)S(1)}, bf16[2,64,128]{2,1,0:T(8,128)(2,1)S(1)}, u32[]{:S(2)}, u32[]{:S(2)}) %collective-permute-start.9) | collective-permute-done | bytes 32800 | tf_op jit(solution)/shard_map/ppermute | solution.py:40
  53.9 0.8 %shard_map.107 = bf16[1,1,2,128,128]{4,3,2,1,0:T(8,128)(2,1)} custom-call(bf16[2,64,128]{2,1,0:T(8,128)(2,1)S(1)} %shard_map.106.own, bf16[2,64,128]{2,1,0:T(8,128)(2,1)S(1)} %collective-permute-done.9.other), custom_call_target="tpu_custom_call" | custom-call | tf_op jit(solution)/shard_map/pallas_call | solution.py:370
  (23 shorter events, 2.0 us)
Async XLA Ops:
  1.6 16.8 %collective-permute-start.2 = (bf16[3,40,128,128]{3,2,1,0:T(8,128)(2,1)}, bf16[3,40,128,128]{3,2,1,0:T(8,128)(2,1)}, u32[]{:S(2)}, u32[]{:S(2)}) collective-permute-start(bf16[3,40,128,128]{3,2,1,0:T(8,128)(2,1)} %bitcast.22), channel_id=1, source_target_pairs={{0,1},{1,0},{2,3},{3,2},{4,5},{5,4},{6,7},{7,6},{8,9},{9,8},{10,11... | collective-permute-start | bytes 11796488 | tf_op jit(solution)/shard_map/ppermute | solution.py:40
  2.1 4.8 %collective-permute-start = (bf16[128,128]{1,0:T(8,128)(2,1)S(1)}, bf16[128,128]{1,0:T(8,128)(2,1)S(1)}, u32[]{:S(2)}, u32[]{:S(2)}) collective-permute-start(bf16[128,128]{1,0:T(8,128)(2,1)S(1)} %shard_map.96.refs_2_.refs_4_), channel_id=1, source_target_pairs={{0,2},{1,3},{2,0},{3,1},{4,6},{5,7},{6,4},{7,5},{8,10},{9,11},{10,... | collective-permute-start | bytes 98312 | tf_op jit(solution)/shard_map/ppermute | solution.py:35
  7.7 14.6 %all-to-all-start = ((bf16[8,128,128]{2,1,0:T(8,128)(2,1)}), bf16[8,128,128]{2,1,0:T(8,128)(2,1)S(1)}, u32[]{:S(2)}, u32[]{:S(2)}) async-start(bf16[8,128,128]{2,1,0:T(8,128)(2,1)} %shard_map.97), calls=%async_computation | async-start | bytes 524288 | tf_op jit(solution)/shard_map/all_to_all | solution.py:385
  14.8 7.4 %copy-start.2 = (bf16[1,1,1,2,128,128]{5,4,3,2,1,0:T(8,128)(2,1)S(1)}, bf16[1,1,1,2,128,128]{5,4,3,2,1,0:T(8,128)(2,1)}, u32[]{:S(2)}) copy-start(bf16[1,1,1,2,128,128]{5,4,3,2,1,0:T(8,128)(2,1)} %param.12) | copy-start | bytes 196612
  14.8 7.4 %copy-start.3 = (bf16[1,1,1,2,128,128]{5,4,3,2,1,0:T(8,128)(2,1)S(1)}, bf16[1,1,1,2,128,128]{5,4,3,2,1,0:T(8,128)(2,1)}, u32[]{:S(2)}) copy-start(bf16[1,1,1,2,128,128]{5,4,3,2,1,0:T(8,128)(2,1)} %param.14) | copy-start | bytes 196612
  14.8 2.5 %collective-permute-start.3 = (bf16[128,128]{1,0:T(8,128)(2,1)S(1)}, bf16[128,128]{1,0:T(8,128)(2,1)S(1)}, u32[]{:S(2)}, u32[]{:S(2)}) collective-permute-start(bf16[128,128]{1,0:T(8,128)(2,1)S(1)} %shard_map.96.refs_2_.refs_4_), channel_id=1, source_target_pairs={{0,1},{1,0},{2,3},{3,2},{4,5},{5,4},{6,7},{7,6},{8,9},{9,8},{10,11... | collective-permute-start | bytes 98312 | tf_op jit(solution)/shard_map/ppermute | solution.py:35
  15.0 3.4 %collective-permute-start.4 = (bf16[128,128]{1,0:T(8,128)(2,1)S(1)}, bf16[128,128]{1,0:T(8,128)(2,1)S(1)}, u32[]{:S(2)}, u32[]{:S(2)}) collective-permute-start(bf16[128,128]{1,0:T(8,128)(2,1)S(1)} %shard_map.96.refs_2_.refs_4_), channel_id=1, source_target_pairs={{0,3},{1,2},{2,1},{3,0},{4,7},{5,6},{6,5},{7,4},{8,11},{9,10},{10,... | collective-permute-start | bytes 98312 | tf_op jit(solution)/shard_map/ppermute | solution.py:35
  16.1 1.2 %collective-permute-start.1 = (s32[8,128]{1,0:T(8,128)S(1)}, s32[8,128]{1,0:T(8,128)S(1)}, u32[]{:S(2)}, u32[]{:S(2)}) collective-permute-start(s32[8,128]{1,0:T(8,128)S(1)} %get-tuple-element.40), channel_id=1, source_target_pairs={{0,1},{1,0},{2,3},{3,2},{4,5},{5,4},{6,7},{7,6},{8,9},{9,8},{10,11... | collective-permute-start | bytes 12296 | tf_op jit(solution)/shard_map/ppermute | solution.py:40
  22.6 3.8 %collective-permute-start.5 = (bf16[64,128]{1,0:T(8,128)(2,1)S(1)}, bf16[64,128]{1,0:T(8,128)(2,1)S(1)}, u32[]{:S(2)}, u32[]{:S(2)}) collective-permute-start(bf16[64,128]{1,0:T(8,128)(2,1)S(1)} %get-tuple-element.55.refs_4_.refs_5_.refs_8_), channel_id=1, source_target_pairs={{0,2},{1,3},{2,0},{3,1},{4,6},{5,7},{6,4},{7,5},{8,10},{9,11},{10,... | collective-permute-start | bytes 49160 | tf_op jit(solution)/shard_map/ppermute | solution.py:35
  22.7 3.7 %collective-permute-start.6 = (bf16[64,128]{1,0:T(8,128)(2,1)S(1)}, bf16[64,128]{1,0:T(8,128)(2,1)S(1)}, u32[]{:S(2)}, u32[]{:S(2)}) collective-permute-start(bf16[64,128]{1,0:T(8,128)(2,1)S(1)} %get-tuple-element.49), channel_id=1, source_target_pairs={{0,1},{1,0},{2,3},{3,2},{4,5},{5,4},{6,7},{7,6},{8,9},{9,8},{10,11... | collective-permute-start | bytes 49160 | tf_op jit(solution)/shard_map/ppermute | solution.py:35
  22.8 3.7 %collective-permute-start.7 = (bf16[64,128]{1,0:T(8,128)(2,1)S(1)}, bf16[64,128]{1,0:T(8,128)(2,1)S(1)}, u32[]{:S(2)}, u32[]{:S(2)}) collective-permute-start(bf16[64,128]{1,0:T(8,128)(2,1)S(1)} %get-tuple-element.49), channel_id=1, source_target_pairs={{0,3},{1,2},{2,1},{3,0},{4,7},{5,6},{6,5},{7,4},{8,11},{9,10},{10,... | collective-permute-start | bytes 49160 | tf_op jit(solution)/shard_map/ppermute | solution.py:35
  28.0 10.5 %all-to-all-start.1 = ((bf16[8,64,128]{2,1,0:T(8,128)(2,1)}), bf16[8,64,128]{2,1,0:T(8,128)(2,1)S(1)}, u32[]{:S(2)}, u32[]{:S(2)}) async-start(bf16[8,64,128]{2,1,0:T(8,128)(2,1)} %shard_map.101), calls=%async_computation.1 | async-start | bytes 262144 | tf_op jit(solution)/shard_map/all_to_all | solution.py:385
  33.5 5.0 %copy-start = (bf16[1,1,2,128,128]{4,3,2,1,0:T(8,128)(2,1)S(1)}, bf16[1,1,2,128,128]{4,3,2,1,0:T(8,128)(2,1)}, u32[]{:S(2)}) copy-start(bf16[1,1,2,128,128]{4,3,2,1,0:T(8,128)(2,1)} %param.13) | copy-start | bytes 196612
  33.5 5.0 %copy-start.1 = (bf16[1,1,2,128,128]{4,3,2,1,0:T(8,128)(2,1)S(1)}, bf16[1,1,2,128,128]{4,3,2,1,0:T(8,128)(2,1)}, u32[]{:S(2)}) copy-start(bf16[1,1,2,128,128]{4,3,2,1,0:T(8,128)(2,1)} %param.15) | copy-start | bytes 196612
  38.8 3.8 %collective-permute-start.8 = (bf16[64,128]{1,0:T(8,128)(2,1)S(1)}, bf16[64,128]{1,0:T(8,128)(2,1)S(1)}, u32[]{:S(2)}, u32[]{:S(2)}) collective-permute-start(bf16[64,128]{1,0:T(8,128)(2,1)S(1)} %shard_map.103.refs_4_.refs_5_.refs_0_), channel_id=1, source_target_pairs={{0,2},{1,3},{2,0},{3,1},{4,6},{5,7},{6,4},{7,5},{8,10},{9,11},{10,... | collective-permute-start | bytes 49160 | tf_op jit(solution)/shard_map/ppermute | solution.py:35
  52.6 1.2 %collective-permute-start.9 = (bf16[2,64,128]{2,1,0:T(8,128)(2,1)S(1)}, bf16[2,64,128]{2,1,0:T(8,128)(2,1)S(1)}, u32[]{:S(2)}, u32[]{:S(2)}) collective-permute-start(bf16[2,64,128]{2,1,0:T(8,128)(2,1)S(1)} %shard_map.106.own), channel_id=1, source_target_pairs={{0,1},{1,0},{2,3},{3,2},{4,5},{5,4},{6,7},{7,6},{8,9},{9,8},{10,11... | collective-permute-start | bytes 98312 | tf_op jit(solution)/shard_map/ppermute | solution.py:40

commit v7 on v3

--- a/solution.py
+++ b/solution.py
@@ -60,12 +60,14 @@
     me = lax.axis_index("pcol")
     spare = row_count << field
     width = plan.shape[1]
-    for level in range(3):
-        first_list = pairs.index((level, level + 1))
-        steps = 3 - level
-        lists = sum(pair[0] == level for pair in pairs)
-
-        def one_slot(slot, found):
+    live = [counts[level] for level in range(3)]
+
+    def one_slot(slot, found):
+        found = list(found)
+        for level in range(3):
+            first_list = pairs.index((level, level + 1))
+            steps = 3 - level
+            lists = sum(pair[0] == level for pair in pairs)
             target = targets[level, 0, slot]
             higher = [(target >= (level + j) * row_count).astype(jnp.int32) for j in range(1, steps)]
             step = sum(higher, jnp.int32(0))
@@ -75,26 +77,32 @@
             kind = step
             if lists > steps:
                 kind = step + ((step > 0) | (column > 0)).astype(jnp.int32)
-            place = found[lists - 1]
+            alive = slot < live[level]
+            place = found[first_list + lists - 1]
             for j in range(lists - 1):
-                place = jnp.where(kind == j, found[j], place)
+                place = jnp.where(kind == j, found[first_list + j], place)
+            place = jnp.where(alive, place, width - 2)
             entry = (slot << (2 * field)) + (row << field) + column
             plan[first_list + kind, place] = entry
             kept[first_list + kind, place] = entry
-            return tuple(found[j] + (kind == j).astype(jnp.int32) for j in range(lists))
-
-        found = lax.fori_loop(0, counts[level], one_slot, (jnp.int32(0),) * lists)
-        for j in range(lists):
-            plan[first_list + j, width - 1] = found[j]
-            kept[first_list + j, width - 1] = found[j]
-            for extra in range(slot_group):
-                plan[first_list + j, found[j] + extra] = spare
-                kept[first_list + j, found[j] + extra] = spare
+            for j in range(lists):
+                found[first_list + j] += ((kind == j) & alive).astype(jnp.int32)
+        return tuple(found)
+
+    found = lax.fori_loop(
+        0, sources.shape[2], one_slot, (jnp.int32(0),) * len(pairs), unroll=2
+    )
+    for which in range(len(pairs)):
+        plan[which, width - 1] = found[which]
+        kept[which, width - 1] = found[which]
+        for extra in range(slot_group):
+            plan[which, found[which] + extra] = spare
+            kept[which, found[which] + extra] = spare
     stage.wait()
 
 
 def make_plan(row_count, cols, sources, targets, counts, blocks):
-    width = -(-(sources.shape[-1] + slot_group + 1) // 128) * 128
+    width = -(-(sources.shape[-1] + slot_group + 2) // 128) * 128
     return pl.pallas_call(
         functools.partial(plan_kernel, row_count, cols),
         out_shape=[

time: 55.5 us -> 55.5 us (level)
  Pallas kernels: 15.3 us -> 16 us
  starting transfers between devices: 20.3 us -> 19.6 us
    pallas_call x1, Pallas kernels: 2.08 us -> 3.41 us  [make_plan(): pl.pallas_call(functools.partial(plan_kernel, row_count, cols), out_shape...]
    all_to_all x2, waiting for transfers between devices: 3.94 us -> 3.25 us  [exchange(): lax.all_to_all(send, 'prow', 0, 0, tiled=True, axis_index_groups=[order])]
    pallas_call x7, Pallas kernels: 11.8 us -> 11.3 us  [update(): pl.pallas_call(functools.partial(update_kernel, config), out_shape=outs,...]
  transfers between devices with their start and end apart: 12 -> 12, of which waited for: 8 -> 7; matrix products, arithmetic and copies ran while one was open for 1% -> 1% of each run, Pallas kernels for 21% -> 23%
where the time goes in v7:
time: 55.5 us; the launch traced here: 55 us
  starting transfers between devices  19.6 us (35%)
  Pallas kernels  16 us (29%)
  blocking collectives  9.19 us (17%)
  waiting for transfers between devices  7.65 us (14%)
  matrix products  1.03 us (2%)
  between operations  0.75 us (1%)
  other arithmetic  0.68 us (1%)
    all_to_all x2, starting transfers between devices, exchange(): lax.all_to_all(send, 'prow', 0, 0, tiled=True, axis_index_groups=[order])  11.9 us
    pallas_call x7, Pallas kernels, update(): pl.pallas_call(functools.partial(update_kernel, config), out_shape=outs,...  11.3 us
    all_to_all x1, blocking collectives, exchange(): lax.all_to_all(send, 'prow', 0, 0, tiled=True, axis_index_groups=[order])  9.19 us
    ppermute x7, starting transfers between devices, sibling_values(): found.append(lax.ppermute(value, ('pcol', 'zgrid'), moves))  7.13 us
    pallas_call x1, Pallas kernels, make_plan(): pl.pallas_call(functools.partial(plan_kernel, row_count, cols), out_shape...  3.41 us
    all_to_all x2, waiting for transfers between devices, exchange(): lax.all_to_all(send, 'prow', 0, 0, tiled=True, axis_index_groups=[order])  3.25 us
    ppermute x7, waiting for transfers between devices, sibling_values(): found.append(lax.ppermute(value, ('pcol', 'zgrid'), moves))  2.75 us
    ppermute x3, waiting for transfers between devices, from_other_core(): return lax.ppermute(value, 'zgrid', [(0, 1), (1, 0)])  1.65 us
  transfers between devices with their start and end apart: 12, of which 7 were waited for; matrix products, arithmetic and copies ran while one was open for 1% of the time, Pallas kernels for 23%

profile of v7, /device:TPU:0, one launch (start us, length us, event | category | flops | bytes accessed | tf_op | source)
XLA Modules:
  0.0 55.0 jit_solution(15548960847242542785)
XLA Ops:
  0.6 0.9 %convolution_convert_fusion.1.refs_2_.refs_4_ = bf16[128,128]{1,0:T(8,128)(2,1)S(1)} fusion(bf16[1,1,1,2,128,128]{5,4,3,2,1,0:T(8,128)(2,1)} %param.12, bf16[1,1,1,2,128,128]{5,4,3,2,1,0:T(8,128)(2,1)} %param.14), kind=kOutput, calls=%fused_computation.1 | convolution fusion | flops 4210688 | bytes 98304 | tf_op jit(solution)/shard_map/dot_general | solution.py:337
  2.0 2.6 %collective-permute-start = (bf16[128,128]{1,0:T(8,128)(2,1)S(1)}, bf16[128,128]{1,0:T(8,128)(2,1)S(1)}, u32[]{:S(2)}, u32[]{:S(2)}) collective-permute-start(bf16[128,128]{1,0:T(8,128)(2,1)S(1)} %convolution_convert_fusion.1.refs_2_.refs_4_), channel_id=1, source_target_pairs={{0,2},{1,3},{2,0},{3,1},{4,6},{5,7},{6,4},{7,5},{8,10},{9,11},{10,... | collective-permute-start | bytes 98312 | tf_op jit(solution)/shard_map/ppermute | solution.py:35
  4.6 3.4 %shard_map.95 = (s32[8,128]{1,0:T(8,128)S(1)}, s32[8,128]{1,0:T(8,128)S(4)}, bf16[40,128,128]{2,1,0:T(8,128)(2,1)S(1)}) custom-call(s32[3,1,40]{2,1,0:T(1,128)} %bitcast.46, s32[3,1,40]{2,1,0:T(1,128)} %bitcast.47, s32[3]{0:T(128)} %bitcast.48, bf16[3,40,128,128]{3,2,1,0:T(8,128)(2,1)} %bitcast.38), custom_call_target="tpu_custom_call" | custom-call | tf_op jit(solution)/shard_map/pallas_call | solution.py:106
  8.0 0.8 %shard_map.96 = bf16[8,128,128]{2,1,0:T(8,128)(2,1)} custom-call(s32[8,128]{1,0:T(8,128)S(4)} %get-tuple-element.33.refs_0_, bf16[3,40,128,128]{3,2,1,0:T(8,128)(2,1)} %bitcast.39, bf16[128,128]{1,0:T(8,128)(2,1)S(1)} %convolution_convert_fusion.1.refs_2_.refs_4_, bf16[128,128]{1,0:T(8,128)(2,1)S(1)} %collective-permute-done.refs_3_.refs_5_, ...), custom_call_target="tpu_custom_call" | custom-call | tf_op jit(solution)/shard_map/pallas_call | solution.py:277
  8.8 6.6 %all-to-all-start = ((bf16[8,128,128]{2,1,0:T(8,128)(2,1)}), bf16[8,128,128]{2,1,0:T(8,128)(2,1)S(1)}, u32[]{:S(2)}, u32[]{:S(2)}) async-start(bf16[8,128,128]{2,1,0:T(8,128)(2,1)} %shard_map.96), calls=%async_computation | async-start | bytes 524288 | tf_op jit(solution)/shard_map/all_to_all | solution.py:348
  15.5 0.6 %collective-permute-start.4 = (bf16[128,128]{1,0:T(8,128)(2,1)S(1)}, bf16[128,128]{1,0:T(8,128)(2,1)S(1)}, u32[]{:S(2)}, u32[]{:S(2)}) collective-permute-start(bf16[128,128]{1,0:T(8,128)(2,1)S(1)} %convolution_convert_fusion.1.refs_2_.refs_4_), channel_id=1, source_target_pairs={{0,3},{1,2},{2,1},{3,0},{4,7},{5,6},{6,5},{7,4},{8,11},{9,10},{10,... | collective-permute-start | bytes 98312 | tf_op jit(solution)/shard_map/ppermute | solution.py:35
  16.1 1.1 %collective-permute-done.1.refs_1_ = s32[8,128]{1,0:T(8,128)S(1)} collective-permute-done((s32[8,128]{1,0:T(8,128)S(1)}, s32[8,128]{1,0:T(8,128)S(1)}, u32[]{:S(2)}, u32[]{:S(2)}) %collective-permute-start.1) | collective-permute-done | bytes 4128 | tf_op jit(solution)/shard_map/ppermute | solution.py:40
  17.2 1.6 %collective-permute-done.4.refs_7_ = bf16[128,128]{1,0:T(8,128)(2,1)S(1)} collective-permute-done((bf16[128,128]{1,0:T(8,128)(2,1)S(1)}, bf16[128,128]{1,0:T(8,128)(2,1)S(1)}, u32[]{:S(2)}, u32[]{:S(2)}) %collective-permute-start.4) | collective-permute-done | bytes 32800 | tf_op jit(solution)/shard_map/ppermute | solution.py:35
  18.9 2.1 %shard_map.97 = (f32[8,128,128]{2,1,0:T(8,128)S(1)}, bf16[40,128,128]{2,1,0:T(8,128)(2,1)S(1)}, s32[8,128]{1,0:T(8,128)S(4)}) custom-call(s32[8,128]{1,0:T(8,128)S(4)} %get-tuple-element.33.refs_0_, s32[8,128]{1,0:T(8,128)S(1)} %collective-permute-done.1.refs_1_, bf16[3,40,128,128]{3,2,1,0:T(8,128)(2,1)} %bitcast.40, ...), custom_call_target="tpu_custom_call" | custom-call | tf_op jit(solution)/shard_map/pallas_call | solution.py:277
  21.0 1.3 %all-to-all-done = bf16[8,128,128]{2,1,0:T(8,128)(2,1)S(1)} async-done(((bf16[8,128,128]{2,1,0:T(8,128)(2,1)}), bf16[8,128,128]{2,1,0:T(8,128)(2,1)S(1)}, u32[]{:S(2)}, u32[]{:S(2)}) %all-to-all-start) | async-done | bytes 262176 | tf_op jit(solution)/shard_map/all_to_all | solution.py:348
  23.0 1.6 %collective-permute-start.7 = (bf16[128,128]{1,0:T(8,128)(2,1)S(1)}, bf16[128,128]{1,0:T(8,128)(2,1)S(1)}, u32[]{:S(2)}, u32[]{:S(2)}) collective-permute-start(bf16[128,128]{1,0:T(8,128)(2,1)S(1)} %fusion.refs_4_.refs_5_.refs_8_), channel_id=1, source_target_pairs={{0,3},{1,2},{2,1},{3,0},{4,7},{5,6},{6,5},{7,4},{8,11},{9,10},{10,... | collective-permute-start | bytes 98312 | tf_op jit(solution)/shard_map/ppermute | solution.py:35
  24.7 1.3 %shard_map.98 = (f32[8,128,128]{2,1,0:T(8,128)S(1)}, bf16[40,128,128]{2,1,0:T(8,128)(2,1)S(1)}) custom-call(s32[8,128]{1,0:T(8,128)S(4)} %get-tuple-element.33.refs_0_, s32[8,128]{1,0:T(8,128)S(4)} %get-tuple-element.40.refs_1_, bf16[3,40,128,128]{3,2,1,0:T(8,128)(2,1)} %bitcast.41, bf16[3,40,128,128]{3,2,1,0:T(8,128)(2,1)} %collective-permute-done.2.refs_3_, ...), custom_call_target="tpu_custom_call" | custom-call | tf_op jit(solution)/shard_map/pallas_call | solution.py:277
  26.0 0.7 %collective-permute-done.5.refs_5_.refs_9_ = bf16[128,128]{1,0:T(8,128)(2,1)S(1)} collective-permute-done((bf16[128,128]{1,0:T(8,128)(2,1)S(1)}, bf16[128,128]{1,0:T(8,128)(2,1)S(1)}, u32[]{:S(2)}, u32[]{:S(2)}) %collective-permute-start.5) | collective-permute-done | bytes 32800 | tf_op jit(solution)/shard_map/ppermute | solution.py:35
  26.7 1.5 %shard_map.99 = bf16[8,64,128]{2,1,0:T(8,128)(2,1)} custom-call(s32[8,128]{1,0:T(8,128)S(4)} %get-tuple-element.33.refs_0_, s32[8,128]{1,0:T(8,128)S(4)} %get-tuple-element.40.refs_1_, bf16[3,40,128,128]{3,2,1,0:T(8,128)(2,1)} %bitcast.42, bf16[3,40,128,128]{3,2,1,0:T(8,128)(2,1)} %collective-permute-done.2.refs_3_, ...), custom_call_target="tpu_custom_call" | custom-call | tf_op jit(solution)/shard_map/pallas_call | solution.py:277
  28.2 5.3 %all-to-all-start.1 = ((bf16[8,64,128]{2,1,0:T(8,128)(2,1)}), bf16[8,64,128]{2,1,0:T(8,128)(2,1)S(1)}, u32[]{:S(2)}, u32[]{:S(2)}) async-start(bf16[8,64,128]{2,1,0:T(8,128)(2,1)} %shard_map.99), calls=%async_computation.1 | async-start | bytes 262144 | tf_op jit(solution)/shard_map/all_to_all | solution.py:348
  33.5 3.3 %shard_map.100 = (f32[8,128,128]{2,1,0:T(8,128)S(1)}, bf16[40,128,128]{2,1,0:T(8,128)(2,1)S(1)}) custom-call(s32[8,128]{1,0:T(8,128)S(4)} %get-tuple-element.33.refs_0_, s32[8,128]{1,0:T(8,128)S(4)} %get-tuple-element.40.refs_1_, bf16[3,40,128,128]{3,2,1,0:T(8,128)(2,1)} %bitcast.43, bf16[3,40,128,128]{3,2,1,0:T(8,128)(2,1)} %collective-permute-done.2.refs_3_, ...), custom_call_target="tpu_custom_call" | custom-call | tf_op jit(solution)/shard_map/pallas_call | solution.py:277
  36.8 1.9 %all-to-all-done.1.received = bf16[8,64,128]{2,1,0:T(8,128)(2,1)S(1)} async-done(((bf16[8,64,128]{2,1,0:T(8,128)(2,1)}), bf16[8,64,128]{2,1,0:T(8,128)(2,1)S(1)}, u32[]{:S(2)}, u32[]{:S(2)}) %all-to-all-start.1) | async-done | bytes 131104 | tf_op jit(solution)/shard_map/all_to_all | solution.py:348
  39.0 1.8 %collective-permute-start.8 = (bf16[64,128]{1,0:T(8,128)(2,1)S(1)}, bf16[64,128]{1,0:T(8,128)(2,1)S(1)}, u32[]{:S(2)}, u32[]{:S(2)}) collective-permute-start(bf16[64,128]{1,0:T(8,128)(2,1)S(1)} %shard_map.101.refs_4_.refs_5_.refs_0_), channel_id=1, source_target_pairs={{0,2},{1,3},{2,0},{3,1},{4,6},{5,7},{6,4},{7,5},{8,10},{9,11},{10,... | collective-permute-start | bytes 49160 | tf_op jit(solution)/shard_map/ppermute | solution.py:35
  40.8 1.6 %shard_map.102 = (f32[8,128,128]{2,1,0:T(8,128)S(1)}, bf16[40,128,128]{2,1,0:T(8,128)(2,1)S(1)}) custom-call(s32[8,128]{1,0:T(8,128)S(4)} %get-tuple-element.33.refs_0_, s32[8,128]{1,0:T(8,128)S(4)} %get-tuple-element.40.refs_1_, bf16[3,40,128,128]{3,2,1,0:T(8,128)(2,1)} %bitcast.44, bf16[3,40,128,128]{3,2,1,0:T(8,128)(2,1)} %collective-permute-done.2.refs_3_, ...), custom_call_target="tpu_custom_call" | custom-call | tf_op jit(solution)/shard_map/pallas_call | solution.py:277
  42.8 0.7 %shard_map.103 = bf16[8,64,128]{2,1,0:T(8,128)(2,1)S(1)} custom-call(s32[8,128]{1,0:T(8,128)S(4)} %get-tuple-element.33.refs_0_, s32[8,128]{1,0:T(8,128)S(4)} %get-tuple-element.40.refs_1_, bf16[3,40,128,128]{3,2,1,0:T(8,128)(2,1)} %bitcast.45, bf16[3,40,128,128]{3,2,1,0:T(8,128)(2,1)} %collective-permute-done.2.refs_3_, ...), custom_call_target="tpu_custom_call" | custom-call | tf_op jit(solution)/shard_map/pallas_call | solution.py:277
  43.5 9.2 %all_to_all.15.received = bf16[8,64,128]{2,1,0:T(8,128)(2,1)S(1)} all-to-all(bf16[8,64,128]{2,1,0:T(8,128)(2,1)S(1)} %shard_map.103), channel_id=1, replica_groups={{16,20,24,28,0,4,8,12},{17,21,25,29,1,5,9,13},{18,22,26,30,2,6,10,14},{..., dimensions={0} | all-to-all | bytes 262144 | tf_op jit(solution)/shard_map/all_to_all | solution.py:348
  53.0 0.6 %maximum_bitcast_fusion = bf16[1,1,1,2,128,128]{5,4,3,2,1,0:T(8,128)(2,1)} fusion(bf16[1,128,128]{2,1,0:T(8,128)(2,1)S(1)} %bitcast.31, bf16[1,128,128]{2,1,0:T(8,128)(2,1)S(1)} %bitcast.32), kind=kLoop, calls=%fused_computation.4 | loop fusion | flops 32768 | bytes 131072 | tf_op jit(solution)/shard_map/broadcast_in_dim | solution.py:417
  53.6 0.6 %collective-permute-done.9.other = bf16[2,64,128]{2,1,0:T(8,128)(2,1)S(1)} collective-permute-done((bf16[2,64,128]{2,1,0:T(8,128)(2,1)S(1)}, bf16[2,64,128]{2,1,0:T(8,128)(2,1)S(1)}, u32[]{:S(2)}, u32[]{:S(2)}) %collective-permute-start.9) | collective-permute-done | bytes 32800 | tf_op jit(solution)/shard_map/ppermute | solution.py:40
  54.2 0.8 %shard_map.105 = bf16[1,1,2,128,128]{4,3,2,1,0:T(8,128)(2,1)} custom-call(bf16[2,64,128]{2,1,0:T(8,128)(2,1)S(1)} %shard_map.104.own, bf16[2,64,128]{2,1,0:T(8,128)(2,1)S(1)} %collective-permute-done.9.other), custom_call_target="tpu_custom_call" | custom-call | tf_op jit(solution)/shard_map/pallas_call | solution.py:327
  (24 shorter events, 2.3 us)
Async XLA Ops:
  1.5 17.3 %collective-permute-start.2 = (bf16[3,40,128,128]{3,2,1,0:T(8,128)(2,1)}, bf16[3,40,128,128]{3,2,1,0:T(8,128)(2,1)}, u32[]{:S(2)}, u32[]{:S(2)}) collective-permute-start(bf16[3,40,128,128]{3,2,1,0:T(8,128)(2,1)} %bitcast.37), channel_id=1, source_target_pairs={{0,1},{1,0},{2,3},{3,2},{4,5},{5,4},{6,7},{7,6},{8,9},{9,8},{10,11... | collective-permute-start | bytes 11796488 | tf_op jit(solution)/shard_map/ppermute | solution.py:40
  2.0 6.0 %collective-permute-start = (bf16[128,128]{1,0:T(8,128)(2,1)S(1)}, bf16[128,128]{1,0:T(8,128)(2,1)S(1)}, u32[]{:S(2)}, u32[]{:S(2)}) collective-permute-start(bf16[128,128]{1,0:T(8,128)(2,1)S(1)} %convolution_convert_fusion.1.refs_2_.refs_4_), channel_id=1, source_target_pairs={{0,2},{1,3},{2,0},{3,1},{4,6},{5,7},{6,4},{7,5},{8,10},{9,11},{10,... | collective-permute-start | bytes 98312 | tf_op jit(solution)/shard_map/ppermute | solution.py:35
  8.8 13.5 %all-to-all-start = ((bf16[8,128,128]{2,1,0:T(8,128)(2,1)}), bf16[8,128,128]{2,1,0:T(8,128)(2,1)S(1)}, u32[]{:S(2)}, u32[]{:S(2)}) async-start(bf16[8,128,128]{2,1,0:T(8,128)(2,1)} %shard_map.96), calls=%async_computation | async-start | bytes 524288 | tf_op jit(solution)/shard_map/all_to_all | solution.py:348
  15.4 6.9 %copy-start.2 = (bf16[1,1,1,2,128,128]{5,4,3,2,1,0:T(8,128)(2,1)S(1)}, bf16[1,1,1,2,128,128]{5,4,3,2,1,0:T(8,128)(2,1)}, u32[]{:S(2)}) copy-start(bf16[1,1,1,2,128,128]{5,4,3,2,1,0:T(8,128)(2,1)} %param.12) | copy-start | bytes 196612
  15.4 6.9 %copy-start.3 = (bf16[1,1,1,2,128,128]{5,4,3,2,1,0:T(8,128)(2,1)S(1)}, bf16[1,1,1,2,128,128]{5,4,3,2,1,0:T(8,128)(2,1)}, u32[]{:S(2)}) copy-start(bf16[1,1,1,2,128,128]{5,4,3,2,1,0:T(8,128)(2,1)} %param.14) | copy-start | bytes 196612
  15.4 1.8 %collective-permute-start.3 = (bf16[128,128]{1,0:T(8,128)(2,1)S(1)}, bf16[128,128]{1,0:T(8,128)(2,1)S(1)}, u32[]{:S(2)}, u32[]{:S(2)}) collective-permute-start(bf16[128,128]{1,0:T(8,128)(2,1)S(1)} %convolution_convert_fusion.1.refs_2_.refs_4_), channel_id=1, source_target_pairs={{0,1},{1,0},{2,3},{3,2},{4,5},{5,4},{6,7},{7,6},{8,9},{9,8},{10,11... | collective-permute-start | bytes 98312 | tf_op jit(solution)/shard_map/ppermute | solution.py:35
  15.5 3.4 %collective-permute-start.4 = (bf16[128,128]{1,0:T(8,128)(2,1)S(1)}, bf16[128,128]{1,0:T(8,128)(2,1)S(1)}, u32[]{:S(2)}, u32[]{:S(2)}) collective-permute-start(bf16[128,128]{1,0:T(8,128)(2,1)S(1)} %convolution_convert_fusion.1.refs_2_.refs_4_), channel_id=1, source_target_pairs={{0,3},{1,2},{2,1},{3,0},{4,7},{5,6},{6,5},{7,4},{8,11},{9,10},{10,... | collective-permute-start | bytes 98312 | tf_op jit(solution)/shard_map/ppermute | solution.py:35
  16.1 1.2 %collective-permute-start.1 = (s32[8,128]{1,0:T(8,128)S(1)}, s32[8,128]{1,0:T(8,128)S(1)}, u32[]{:S(2)}, u32[]{:S(2)}) collective-permute-start(s32[8,128]{1,0:T(8,128)S(1)} %get-tuple-element.37), channel_id=1, source_target_pairs={{0,1},{1,0},{2,3},{3,2},{4,5},{5,4},{6,7},{7,6},{8,9},{9,8},{10,11... | collective-permute-start | bytes 12296 | tf_op jit(solution)/shard_map/ppermute | solution.py:40
  22.5 4.2 %collective-permute-start.5 = (bf16[128,128]{1,0:T(8,128)(2,1)S(1)}, bf16[128,128]{1,0:T(8,128)(2,1)S(1)}, u32[]{:S(2)}, u32[]{:S(2)}) collective-permute-start(bf16[128,128]{1,0:T(8,128)(2,1)S(1)} %fusion.refs_4_.refs_5_.refs_8_), channel_id=1, source_target_pairs={{0,2},{1,3},{2,0},{3,1},{4,6},{5,7},{6,4},{7,5},{8,10},{9,11},{10,... | collective-permute-start | bytes 98312 | tf_op jit(solution)/shard_map/ppermute | solution.py:35
  23.0 3.7 %collective-permute-start.6 = (bf16[128,128]{1,0:T(8,128)(2,1)S(1)}, bf16[128,128]{1,0:T(8,128)(2,1)S(1)}, u32[]{:S(2)}, u32[]{:S(2)}) collective-permute-start(bf16[128,128]{1,0:T(8,128)(2,1)S(1)} %fusion.refs_4_.refs_5_.refs_8_), channel_id=1, source_target_pairs={{0,1},{1,0},{2,3},{3,2},{4,5},{5,4},{6,7},{7,6},{8,9},{9,8},{10,11... | collective-permute-start | bytes 98312 | tf_op jit(solution)/shard_map/ppermute | solution.py:35
  23.0 3.7 %collective-permute-start.7 = (bf16[128,128]{1,0:T(8,128)(2,1)S(1)}, bf16[128,128]{1,0:T(8,128)(2,1)S(1)}, u32[]{:S(2)}, u32[]{:S(2)}) collective-permute-start(bf16[128,128]{1,0:T(8,128)(2,1)S(1)} %fusion.refs_4_.refs_5_.refs_8_), channel_id=1, source_target_pairs={{0,3},{1,2},{2,1},{3,0},{4,7},{5,6},{6,5},{7,4},{8,11},{9,10},{10,... | collective-permute-start | bytes 98312 | tf_op jit(solution)/shard_map/ppermute | solution.py:35
  28.2 10.5 %all-to-all-start.1 = ((bf16[8,64,128]{2,1,0:T(8,128)(2,1)}), bf16[8,64,128]{2,1,0:T(8,128)(2,1)S(1)}, u32[]{:S(2)}, u32[]{:S(2)}) async-start(bf16[8,64,128]{2,1,0:T(8,128)(2,1)} %shard_map.99), calls=%async_computation.1 | async-start | bytes 262144 | tf_op jit(solution)/shard_map/all_to_all | solution.py:348
  33.5 5.2 %copy-start = (bf16[1,1,2,128,128]{4,3,2,1,0:T(8,128)(2,1)S(1)}, bf16[1,1,2,128,128]{4,3,2,1,0:T(8,128)(2,1)}, u32[]{:S(2)}) copy-start(bf16[1,1,2,128,128]{4,3,2,1,0:T(8,128)(2,1)} %param.13) | copy-start | bytes 196612
  33.5 5.2 %copy-start.1 = (bf16[1,1,2,128,128]{4,3,2,1,0:T(8,128)(2,1)S(1)}, bf16[1,1,2,128,128]{4,3,2,1,0:T(8,128)(2,1)}, u32[]{:S(2)}) copy-start(bf16[1,1,2,128,128]{4,3,2,1,0:T(8,128)(2,1)} %param.15) | copy-start | bytes 196612
  39.0 3.8 %collective-permute-start.8 = (bf16[64,128]{1,0:T(8,128)(2,1)S(1)}, bf16[64,128]{1,0:T(8,128)(2,1)S(1)}, u32[]{:S(2)}, u32[]{:S(2)}) collective-permute-start(bf16[64,128]{1,0:T(8,128)(2,1)S(1)} %shard_map.101.refs_4_.refs_5_.refs_0_), channel_id=1, source_target_pairs={{0,2},{1,3},{2,0},{3,1},{4,6},{5,7},{6,4},{7,5},{8,10},{9,11},{10,... | collective-permute-start | bytes 49160 | tf_op jit(solution)/shard_map/ppermute | solution.py:35
  52.9 1.2 %collective-permute-start.9 = (bf16[2,64,128]{2,1,0:T(8,128)(2,1)S(1)}, bf16[2,64,128]{2,1,0:T(8,128)(2,1)S(1)}, u32[]{:S(2)}, u32[]{:S(2)}) collective-permute-start(bf16[2,64,128]{2,1,0:T(8,128)(2,1)S(1)} %shard_map.104.own), channel_id=1, source_target_pairs={{0,1},{1,0},{2,3},{3,2},{4,5},{5,4},{6,7},{7,6},{8,9},{9,8},{10,11... | collective-permute-start | bytes 98312 | tf_op jit(solution)/shard_map/ppermute | solution.py:40

commit v8 on v4

--- a/solution.py
+++ b/solution.py
@@ -7,7 +7,7 @@
 from jax.experimental.pallas import tpu as pltpu
 from jax.sharding import PartitionSpec as P
 
-slot_group = 8
+slot_group = 4
 batch = 4
 field = 10
 field_mask = (1 << field) - 1

time: 54.9 us -> 55.6 us (1.013); the launches traced: 54.1 us -> 55.5 us
  waiting for transfers between devices: 7.22 us -> 8.86 us
    ppermute x7, waiting for transfers between devices: 1.74 us -> 4.28 us  [sibling_values(): found.append(lax.ppermute(value, ('pcol', 'zgrid'), moves))]
    all_to_all x2, starting transfers between devices: 11.5 us -> 13 us  [exchange(): lax.all_to_all(send, 'prow', 0, 0, tiled=True, axis_index_groups=[order])]
    ppermute x7, starting transfers between devices: 7.81 us -> 6.35 us  [sibling_values(): found.append(lax.ppermute(value, ('pcol', 'zgrid'), moves))]
    all_to_all x2, waiting for transfers between devices: 3.83 us -> 2.92 us  [exchange(): lax.all_to_all(send, 'prow', 0, 0, tiled=True, axis_index_groups=[order])]
  transfers between devices with their start and end apart: 12 -> 12, of which waited for: 7 -> 8; matrix products, arithmetic and copies ran while one was open for 1% -> 1% of each run, Pallas kernels for 22% -> 20%
where the time goes in v8:
time: 55.6 us; the launch traced here: 55.5 us
  starting transfers between devices  20 us (36%)
  Pallas kernels  15.4 us (28%)
  blocking collectives  9.02 us (16%)
  waiting for transfers between devices  8.86 us (16%)
  matrix products  0.9 us (2%)
  between operations  0.73 us (1%)
  other arithmetic  0.64 us (1%)
    all_to_all x2, starting transfers between devices, exchange(): lax.all_to_all(send, 'prow', 0, 0, tiled=True, axis_index_groups=[order])  13 us
    pallas_call x7, Pallas kernels, update(): pl.pallas_call(functools.partial(update_kernel, config), out_shape=outs,...  11.6 us
    all_to_all x1, blocking collectives, exchange(): lax.all_to_all(send, 'prow', 0, 0, tiled=True, axis_index_groups=[order])  9.02 us
    ppermute x7, starting transfers between devices, sibling_values(): found.append(lax.ppermute(value, ('pcol', 'zgrid'), moves))  6.35 us
    ppermute x7, waiting for transfers between devices, sibling_values(): found.append(lax.ppermute(value, ('pcol', 'zgrid'), moves))  4.28 us
    all_to_all x2, waiting for transfers between devices, exchange(): lax.all_to_all(send, 'prow', 0, 0, tiled=True, axis_index_groups=[order])  2.92 us
    pallas_call x1, Pallas kernels, make_plan(): pl.pallas_call(functools.partial(plan_kernel, row_count, cols), out_shape...  2 us
    ppermute x3, waiting for transfers between devices, from_other_core(): return lax.ppermute(value, 'zgrid', [(0, 1), (1, 0)])  1.65 us
  transfers between devices with their start and end apart: 12, of which 8 were waited for; matrix products, arithmetic and copies ran while one was open for 1% of the time, Pallas kernels for 20%

profile of v8, /device:TPU:0, one launch (start us, length us, event | category | flops | bytes accessed | tf_op | source)
XLA Modules:
  0.0 55.5 jit_solution(3617965639451189939)
XLA Ops:
  0.6 0.9 %convolution_convert_fusion.refs_2_.refs_4_ = bf16[128,128]{1,0:T(8,128)(2,1)S(1)} fusion(bf16[1,1,1,2,128,128]{5,4,3,2,1,0:T(8,128)(2,1)} %param.12, bf16[1,1,1,2,128,128]{5,4,3,2,1,0:T(8,128)(2,1)} %param.14), kind=kOutput, calls=%fused_computation | convolution fusion | flops 4210688 | bytes 98304 | tf_op jit(solution)/shard_map/dot_general | solution.py:352
  2.0 2.6 %collective-permute-start = (bf16[128,128]{1,0:T(8,128)(2,1)S(1)}, bf16[128,128]{1,0:T(8,128)(2,1)S(1)}, u32[]{:S(2)}, u32[]{:S(2)}) collective-permute-start(bf16[128,128]{1,0:T(8,128)(2,1)S(1)} %convolution_convert_fusion.refs_2_.refs_4_), channel_id=1, source_target_pairs={{0,2},{1,3},{2,0},{3,1},{4,6},{5,7},{6,4},{7,5},{8,10},{9,11},{10,... | collective-permute-start | bytes 98312 | tf_op jit(solution)/shard_map/ppermute | solution.py:35
  4.6 2.0 %shard_map.95 = (s32[8,128]{1,0:T(8,128)S(1)}, s32[8,128]{1,0:T(8,128)S(4)}, bf16[40,128,128]{2,1,0:T(8,128)(2,1)S(1)}) custom-call(s32[3,1,40]{2,1,0:T(1,128)} %bitcast.35, s32[3,1,40]{2,1,0:T(1,128)} %bitcast.36, s32[3]{0:T(128)} %bitcast.37, bf16[3,40,128,128]{3,2,1,0:T(8,128)(2,1)} %bitcast.27), custom_call_target="tpu_custom_call" | custom-call | tf_op jit(solution)/shard_map/pallas_call | solution.py:98
  6.6 0.8 %shard_map.96 = bf16[8,128,128]{2,1,0:T(8,128)(2,1)} custom-call(s32[8,128]{1,0:T(8,128)S(4)} %get-tuple-element.36.refs_0_, bf16[3,40,128,128]{3,2,1,0:T(8,128)(2,1)} %bitcast.28, bf16[128,128]{1,0:T(8,128)(2,1)S(1)} %convolution_convert_fusion.refs_2_.refs_4_, bf16[128,128]{1,0:T(8,128)(2,1)S(1)} %collective-permute-done.refs_3_.refs_5_, ...), custom_call_target="tpu_custom_call" | custom-call | tf_op jit(solution)/shard_map/pallas_call | solution.py:268
  7.4 7.4 %all-to-all-start = ((bf16[8,128,128]{2,1,0:T(8,128)(2,1)}), bf16[8,128,128]{2,1,0:T(8,128)(2,1)S(1)}, u32[]{:S(2)}, u32[]{:S(2)}) async-start(bf16[8,128,128]{2,1,0:T(8,128)(2,1)} %shard_map.96), calls=%async_computation | async-start | bytes 524288 | tf_op jit(solution)/shard_map/all_to_all | solution.py:357
  14.8 1.3 %collective-permute-start.4 = (bf16[128,128]{1,0:T(8,128)(2,1)S(1)}, bf16[128,128]{1,0:T(8,128)(2,1)S(1)}, u32[]{:S(2)}, u32[]{:S(2)}) collective-permute-start(bf16[128,128]{1,0:T(8,128)(2,1)S(1)} %convolution_convert_fusion.refs_2_.refs_4_), channel_id=1, source_target_pairs={{0,3},{1,2},{2,1},{3,0},{4,7},{5,6},{6,5},{7,4},{8,11},{9,10},{10,... | collective-permute-start | bytes 98312 | tf_op jit(solution)/shard_map/ppermute | solution.py:35
  16.3 1.1 %collective-permute-done.1.refs_1_ = s32[8,128]{1,0:T(8,128)S(1)} collective-permute-done((s32[8,128]{1,0:T(8,128)S(1)}, s32[8,128]{1,0:T(8,128)S(1)}, u32[]{:S(2)}, u32[]{:S(2)}) %collective-permute-start.1) | collective-permute-done | bytes 4128 | tf_op jit(solution)/shard_map/ppermute | solution.py:40
  17.4 0.9 %collective-permute-done.4.refs_7_ = bf16[128,128]{1,0:T(8,128)(2,1)S(1)} collective-permute-done((bf16[128,128]{1,0:T(8,128)(2,1)S(1)}, bf16[128,128]{1,0:T(8,128)(2,1)S(1)}, u32[]{:S(2)}, u32[]{:S(2)}) %collective-permute-start.4) | collective-permute-done | bytes 32800 | tf_op jit(solution)/shard_map/ppermute | solution.py:35
  18.2 2.2 %shard_map.97 = (f32[8,128,128]{2,1,0:T(8,128)S(1)}, bf16[40,128,128]{2,1,0:T(8,128)(2,1)S(1)}, s32[8,128]{1,0:T(8,128)S(4)}) custom-call(s32[8,128]{1,0:T(8,128)S(4)} %get-tuple-element.36.refs_0_, s32[8,128]{1,0:T(8,128)S(1)} %collective-permute-done.1.refs_1_, bf16[3,40,128,128]{3,2,1,0:T(8,128)(2,1)} %bitcast.29, ...), custom_call_target="tpu_custom_call" | custom-call | tf_op jit(solution)/shard_map/pallas_call | solution.py:268
  20.4 0.5 all-to-all-done.received
  21.3 2.0 %collective-permute-start.5 = (bf16[64,128]{1,0:T(8,128)(2,1)S(1)}, bf16[64,128]{1,0:T(8,128)(2,1)S(1)}, u32[]{:S(2)}, u32[]{:S(2)}) collective-permute-start(bf16[64,128]{1,0:T(8,128)(2,1)S(1)} %get-tuple-element.55.refs_4_.refs_5_.refs_8_), channel_id=1, source_target_pairs={{0,2},{1,3},{2,0},{3,1},{4,6},{5,7},{6,4},{7,5},{8,10},{9,11},{10,... | collective-permute-start | bytes 49160 | tf_op jit(solution)/shard_map/ppermute | solution.py:35
  23.5 1.3 %shard_map.99 = (f32[8,128,128]{2,1,0:T(8,128)S(1)}, bf16[40,128,128]{2,1,0:T(8,128)(2,1)S(1)}) custom-call(s32[8,128]{1,0:T(8,128)S(4)} %get-tuple-element.36.refs_0_, s32[8,128]{1,0:T(8,128)S(4)} %get-tuple-element.43.refs_1_, bf16[3,40,128,128]{3,2,1,0:T(8,128)(2,1)} %bitcast.30, bf16[3,40,128,128]{3,2,1,0:T(8,128)(2,1)} %collective-permute-done.2.refs_3_, ...), custom_call_target="tpu_custom_call" | custom-call | tf_op jit(solution)/shard_map/pallas_call | solution.py:268
  25.1 1.3 %collective-permute-done.7.refs_7_.refs_11_ = bf16[64,128]{1,0:T(8,128)(2,1)S(1)} collective-permute-done((bf16[64,128]{1,0:T(8,128)(2,1)S(1)}, bf16[64,128]{1,0:T(8,128)(2,1)S(1)}, u32[]{:S(2)}, u32[]{:S(2)}) %collective-permute-start.7) | collective-permute-done | bytes 16416 | tf_op jit(solution)/shard_map/ppermute | solution.py:35
  26.5 1.4 %shard_map.100 = bf16[8,64,128]{2,1,0:T(8,128)(2,1)} custom-call(s32[8,128]{1,0:T(8,128)S(4)} %get-tuple-element.36.refs_0_, s32[8,128]{1,0:T(8,128)S(4)} %get-tuple-element.43.refs_1_, bf16[3,40,128,128]{3,2,1,0:T(8,128)(2,1)} %bitcast.31, bf16[3,40,128,128]{3,2,1,0:T(8,128)(2,1)} %collective-permute-done.2.refs_3_, ...), custom_call_target="tpu_custom_call" | custom-call | tf_op jit(solution)/shard_map/pallas_call | solution.py:268
  27.9 5.6 %all-to-all-start.1 = ((bf16[8,64,128]{2,1,0:T(8,128)(2,1)}), bf16[8,64,128]{2,1,0:T(8,128)(2,1)S(1)}, u32[]{:S(2)}, u32[]{:S(2)}) async-start(bf16[8,64,128]{2,1,0:T(8,128)(2,1)} %shard_map.100), calls=%async_computation.1 | async-start | bytes 262144 | tf_op jit(solution)/shard_map/all_to_all | solution.py:357
  33.5 3.0 %shard_map.101 = (f32[8,128,128]{2,1,0:T(8,128)S(1)}, bf16[40,128,128]{2,1,0:T(8,128)(2,1)S(1)}) custom-call(s32[8,128]{1,0:T(8,128)S(4)} %get-tuple-element.36.refs_0_, s32[8,128]{1,0:T(8,128)S(4)} %get-tuple-element.43.refs_1_, bf16[3,40,128,128]{3,2,1,0:T(8,128)(2,1)} %bitcast.32, bf16[3,40,128,128]{3,2,1,0:T(8,128)(2,1)} %collective-permute-done.2.refs_3_, ...), custom_call_target="tpu_custom_call" | custom-call | tf_op jit(solution)/shard_map/pallas_call | solution.py:268
  36.6 2.4 %all-to-all-done.1.received = bf16[8,64,128]{2,1,0:T(8,128)(2,1)S(1)} async-done(((bf16[8,64,128]{2,1,0:T(8,128)(2,1)}), bf16[8,64,128]{2,1,0:T(8,128)(2,1)S(1)}, u32[]{:S(2)}, u32[]{:S(2)}) %all-to-all-start.1) | async-done | bytes 131104 | tf_op jit(solution)/shard_map/all_to_all | solution.py:357
  39.4 1.7 %shard_map.103 = (f32[8,128,128]{2,1,0:T(8,128)S(1)}, bf16[40,128,128]{2,1,0:T(8,128)(2,1)S(1)}) custom-call(s32[8,128]{1,0:T(8,128)S(4)} %get-tuple-element.36.refs_0_, s32[8,128]{1,0:T(8,128)S(4)} %get-tuple-element.43.refs_1_, bf16[3,40,128,128]{3,2,1,0:T(8,128)(2,1)} %bitcast.33, bf16[3,40,128,128]{3,2,1,0:T(8,128)(2,1)} %collective-permute-done.2.refs_3_, ...), custom_call_target="tpu_custom_call" | custom-call | tf_op jit(solution)/shard_map/pallas_call | solution.py:268
  41.2 1.8 %collective-permute-done.8.refs_5_ = bf16[64,128]{1,0:T(8,128)(2,1)S(1)} collective-permute-done((bf16[64,128]{1,0:T(8,128)(2,1)S(1)}, bf16[64,128]{1,0:T(8,128)(2,1)S(1)}, u32[]{:S(2)}, u32[]{:S(2)}) %collective-permute-start.8) | collective-permute-done | bytes 16416 | tf_op jit(solution)/shard_map/ppermute | solution.py:35
  43.0 1.1 %shard_map.104 = bf16[8,64,128]{2,1,0:T(8,128)(2,1)S(1)} custom-call(s32[8,128]{1,0:T(8,128)S(4)} %get-tuple-element.36.refs_0_, s32[8,128]{1,0:T(8,128)S(4)} %get-tuple-element.43.refs_1_, bf16[3,40,128,128]{3,2,1,0:T(8,128)(2,1)} %bitcast.34, bf16[3,40,128,128]{3,2,1,0:T(8,128)(2,1)} %collective-permute-done.2.refs_3_, ...), custom_call_target="tpu_custom_call" | custom-call | tf_op jit(solution)/shard_map/pallas_call | solution.py:268
  44.2 9.0 %all_to_all.15.received = bf16[8,64,128]{2,1,0:T(8,128)(2,1)S(1)} all-to-all(bf16[8,64,128]{2,1,0:T(8,128)(2,1)S(1)} %shard_map.104), channel_id=1, replica_groups={{16,20,24,28,0,4,8,12},{17,21,25,29,1,5,9,13},{18,22,26,30,2,6,10,14},{..., dimensions={0} | all-to-all | bytes 262144 | tf_op jit(solution)/shard_map/all_to_all | solution.py:357
  53.5 0.6 %maximum_bitcast_fusion = bf16[1,1,1,2,128,128]{5,4,3,2,1,0:T(8,128)(2,1)} fusion(bf16[1,128,128]{2,1,0:T(8,128)(2,1)S(1)} %bitcast.25, bf16[1,128,128]{2,1,0:T(8,128)(2,1)S(1)} %bitcast.18), kind=kLoop, calls=%fused_computation.1 | loop fusion | flops 32768 | bytes 131072 | tf_op jit(solution)/shard_map/broadcast_in_dim | solution.py:426
  54.2 0.6 %collective-permute-done.9.other = bf16[2,64,128]{2,1,0:T(8,128)(2,1)S(1)} collective-permute-done((bf16[2,64,128]{2,1,0:T(8,128)(2,1)S(1)}, bf16[2,64,128]{2,1,0:T(8,128)(2,1)S(1)}, u32[]{:S(2)}, u32[]{:S(2)}) %collective-permute-start.9) | collective-permute-done | bytes 32800 | tf_op jit(solution)/shard_map/ppermute | solution.py:40
  54.7 0.8 %shard_map.106 = bf16[1,1,2,128,128]{4,3,2,1,0:T(8,128)(2,1)} custom-call(bf16[2,64,128]{2,1,0:T(8,128)(2,1)S(1)} %shard_map.105.own, bf16[2,64,128]{2,1,0:T(8,128)(2,1)S(1)} %collective-permute-done.9.other), custom_call_target="tpu_custom_call" | custom-call | tf_op jit(solution)/shard_map/pallas_call | solution.py:342
  (23 shorter events, 2.3 us)
Async XLA Ops:
  1.5 16.7 %collective-permute-start.2 = (bf16[3,40,128,128]{3,2,1,0:T(8,128)(2,1)}, bf16[3,40,128,128]{3,2,1,0:T(8,128)(2,1)}, u32[]{:S(2)}, u32[]{:S(2)}) collective-permute-start(bf16[3,40,128,128]{3,2,1,0:T(8,128)(2,1)} %bitcast.26), channel_id=1, source_target_pairs={{0,1},{1,0},{2,3},{3,2},{4,5},{5,4},{6,7},{7,6},{8,9},{9,8},{10,11... | collective-permute-start | bytes 11796488 | tf_op jit(solution)/shard_map/ppermute | solution.py:40
  2.0 4.6 %collective-permute-start = (bf16[128,128]{1,0:T(8,128)(2,1)S(1)}, bf16[128,128]{1,0:T(8,128)(2,1)S(1)}, u32[]{:S(2)}, u32[]{:S(2)}) collective-permute-start(bf16[128,128]{1,0:T(8,128)(2,1)S(1)} %convolution_convert_fusion.refs_2_.refs_4_), channel_id=1, source_target_pairs={{0,2},{1,3},{2,0},{3,1},{4,6},{5,7},{6,4},{7,5},{8,10},{9,11},{10,... | collective-permute-start | bytes 98312 | tf_op jit(solution)/shard_map/ppermute | solution.py:35
  7.4 13.5 %all-to-all-start = ((bf16[8,128,128]{2,1,0:T(8,128)(2,1)}), bf16[8,128,128]{2,1,0:T(8,128)(2,1)S(1)}, u32[]{:S(2)}, u32[]{:S(2)}) async-start(bf16[8,128,128]{2,1,0:T(8,128)(2,1)} %shard_map.96), calls=%async_computation | async-start | bytes 524288 | tf_op jit(solution)/shard_map/all_to_all | solution.py:357
  14.8 6.1 %copy-start.2 = (bf16[1,1,1,2,128,128]{5,4,3,2,1,0:T(8,128)(2,1)S(1)}, bf16[1,1,1,2,128,128]{5,4,3,2,1,0:T(8,128)(2,1)}, u32[]{:S(2)}) copy-start(bf16[1,1,1,2,128,128]{5,4,3,2,1,0:T(8,128)(2,1)} %param.12) | copy-start | bytes 196612
  14.8 6.1 %copy-start.3 = (bf16[1,1,1,2,128,128]{5,4,3,2,1,0:T(8,128)(2,1)S(1)}, bf16[1,1,1,2,128,128]{5,4,3,2,1,0:T(8,128)(2,1)}, u32[]{:S(2)}) copy-start(bf16[1,1,1,2,128,128]{5,4,3,2,1,0:T(8,128)(2,1)} %param.14) | copy-start | bytes 196612
  14.8 2.5 %collective-permute-start.3 = (bf16[128,128]{1,0:T(8,128)(2,1)S(1)}, bf16[128,128]{1,0:T(8,128)(2,1)S(1)}, u32[]{:S(2)}, u32[]{:S(2)}) collective-permute-start(bf16[128,128]{1,0:T(8,128)(2,1)S(1)} %convolution_convert_fusion.refs_2_.refs_4_), channel_id=1, source_target_pairs={{0,1},{1,0},{2,3},{3,2},{4,5},{5,4},{6,7},{7,6},{8,9},{9,8},{10,11... | collective-permute-start | bytes 98312 | tf_op jit(solution)/shard_map/ppermute | solution.py:35
  14.8 3.4 %collective-permute-start.4 = (bf16[128,128]{1,0:T(8,128)(2,1)S(1)}, bf16[128,128]{1,0:T(8,128)(2,1)S(1)}, u32[]{:S(2)}, u32[]{:S(2)}) collective-permute-start(bf16[128,128]{1,0:T(8,128)(2,1)S(1)} %convolution_convert_fusion.refs_2_.refs_4_), channel_id=1, source_target_pairs={{0,3},{1,2},{2,1},{3,0},{4,7},{5,6},{6,5},{7,4},{8,11},{9,10},{10,... | collective-permute-start | bytes 98312 | tf_op jit(solution)/shard_map/ppermute | solution.py:35
  16.2 1.2 %collective-permute-start.1 = (s32[8,128]{1,0:T(8,128)S(1)}, s32[8,128]{1,0:T(8,128)S(1)}, u32[]{:S(2)}, u32[]{:S(2)}) collective-permute-start(s32[8,128]{1,0:T(8,128)S(1)} %get-tuple-element.40), channel_id=1, source_target_pairs={{0,1},{1,0},{2,3},{3,2},{4,5},{5,4},{6,7},{7,6},{8,9},{9,8},{10,11... | collective-permute-start | bytes 12296 | tf_op jit(solution)/shard_map/ppermute | solution.py:40
  21.3 3.8 %collective-permute-start.5 = (bf16[64,128]{1,0:T(8,128)(2,1)S(1)}, bf16[64,128]{1,0:T(8,128)(2,1)S(1)}, u32[]{:S(2)}, u32[]{:S(2)}) collective-permute-start(bf16[64,128]{1,0:T(8,128)(2,1)S(1)} %get-tuple-element.55.refs_4_.refs_5_.refs_8_), channel_id=1, source_target_pairs={{0,2},{1,3},{2,0},{3,1},{4,6},{5,7},{6,4},{7,5},{8,10},{9,11},{10,... | collective-permute-start | bytes 49160 | tf_op jit(solution)/shard_map/ppermute | solution.py:35
  23.3 1.8 %collective-permute-start.6 = (bf16[64,128]{1,0:T(8,128)(2,1)S(1)}, bf16[64,128]{1,0:T(8,128)(2,1)S(1)}, u32[]{:S(2)}, u32[]{:S(2)}) collective-permute-start(bf16[64,128]{1,0:T(8,128)(2,1)S(1)} %get-tuple-element.49), channel_id=1, source_target_pairs={{0,1},{1,0},{2,3},{3,2},{4,5},{5,4},{6,7},{7,6},{8,9},{9,8},{10,11... | collective-permute-start | bytes 49160 | tf_op jit(solution)/shard_map/ppermute | solution.py:35
  23.3 3.2 %collective-permute-start.7 = (bf16[64,128]{1,0:T(8,128)(2,1)S(1)}, bf16[64,128]{1,0:T(8,128)(2,1)S(1)}, u32[]{:S(2)}, u32[]{:S(2)}) collective-permute-start(bf16[64,128]{1,0:T(8,128)(2,1)S(1)} %get-tuple-element.49), channel_id=1, source_target_pairs={{0,3},{1,2},{2,1},{3,0},{4,7},{5,6},{6,5},{7,4},{8,11},{9,10},{10,... | collective-permute-start | bytes 49160 | tf_op jit(solution)/shard_map/ppermute | solution.py:35
  27.9 11.1 %all-to-all-start.1 = ((bf16[8,64,128]{2,1,0:T(8,128)(2,1)}), bf16[8,64,128]{2,1,0:T(8,128)(2,1)S(1)}, u32[]{:S(2)}, u32[]{:S(2)}) async-start(bf16[8,64,128]{2,1,0:T(8,128)(2,1)} %shard_map.100), calls=%async_computation.1 | async-start | bytes 262144 | tf_op jit(solution)/shard_map/all_to_all | solution.py:357
  33.5 5.4 %copy-start = (bf16[1,1,2,128,128]{4,3,2,1,0:T(8,128)(2,1)S(1)}, bf16[1,1,2,128,128]{4,3,2,1,0:T(8,128)(2,1)}, u32[]{:S(2)}) copy-start(bf16[1,1,2,128,128]{4,3,2,1,0:T(8,128)(2,1)} %param.13) | copy-start | bytes 196612
  33.5 5.4 %copy-start.1 = (bf16[1,1,2,128,128]{4,3,2,1,0:T(8,128)(2,1)S(1)}, bf16[1,1,2,128,128]{4,3,2,1,0:T(8,128)(2,1)}, u32[]{:S(2)}) copy-start(bf16[1,1,2,128,128]{4,3,2,1,0:T(8,128)(2,1)} %param.15) | copy-start | bytes 196612
  39.2 3.8 %collective-permute-start.8 = (bf16[64,128]{1,0:T(8,128)(2,1)S(1)}, bf16[64,128]{1,0:T(8,128)(2,1)S(1)}, u32[]{:S(2)}, u32[]{:S(2)}) collective-permute-start(bf16[64,128]{1,0:T(8,128)(2,1)S(1)} %shard_map.102.refs_4_.refs_5_.refs_0_), channel_id=1, source_target_pairs={{0,2},{1,3},{2,0},{3,1},{4,6},{5,7},{6,4},{7,5},{8,10},{9,11},{10,... | collective-permute-start | bytes 49160 | tf_op jit(solution)/shard_map/ppermute | solution.py:35
  53.5 1.2 %collective-permute-start.9 = (bf16[2,64,128]{2,1,0:T(8,128)(2,1)S(1)}, bf16[2,64,128]{2,1,0:T(8,128)(2,1)S(1)}, u32[]{:S(2)}, u32[]{:S(2)}) collective-permute-start(bf16[2,64,128]{2,1,0:T(8,128)(2,1)S(1)} %shard_map.105.own), channel_id=1, source_target_pairs={{0,1},{1,0},{2,3},{3,2},{4,5},{5,4},{6,7},{7,6},{8,9},{9,8},{10,11... | collective-permute-start | bytes 98312 | tf_op jit(solution)/shard_map/ppermute | solution.py:40

commit v9 on v3

--- a/solution.py
+++ b/solution.py
@@ -8,7 +8,7 @@
 from jax.sharding import PartitionSpec as P
 
 slot_group = 8
-batch = 4
+batch = 8
 field = 10
 field_mask = (1 << field) - 1
 pairs = ((0, 1), (0, 2), (0, 3), (1, 2), (1, 2), (1, 3), (2, 3), (2, 3))

time: 55.5 us -> 54.9 us (0.989)
  Pallas kernels: 15.3 us -> 16.3 us
  starting transfers between devices: 20.3 us -> 19.4 us
    all_to_all x2, starting transfers between devices: 12.1 us -> 11.3 us  [exchange(): lax.all_to_all(send, 'prow', 0, 0, tiled=True, axis_index_groups=[order])]
    pallas_call x7, Pallas kernels: 11.8 us -> 12.4 us  [update(): pl.pallas_call(functools.partial(update_kernel, config), out_shape=outs,...]
  transfers between devices with their start and end apart: 12 -> 12, of which waited for: 8 -> 8; matrix products, arithmetic and copies ran while one was open for 1% -> 1% of each run, Pallas kernels for 21% -> 22%
where the time goes in v9:
time: 54.9 us
  starting transfers between devices  19.4 us (35%)
  Pallas kernels  16.3 us (30%)
  blocking collectives  9.05 us (16%)
  waiting for transfers between devices  7.64 us (14%)
  matrix products  1.03 us (2%)
  between operations  0.75 us (1%)
  other arithmetic  0.68 us (1%)
    pallas_call x7, Pallas kernels, update(): pl.pallas_call(functools.partial(update_kernel, config), out_shape=outs,...  12.4 us
    all_to_all x2, starting transfers between devices, exchange(): lax.all_to_all(send, 'prow', 0, 0, tiled=True, axis_index_groups=[order])  11.3 us
    all_to_all x1, blocking collectives, exchange(): lax.all_to_all(send, 'prow', 0, 0, tiled=True, axis_index_groups=[order])  9.05 us
    ppermute x7, starting transfers between devices, sibling_values(): found.append(lax.ppermute(value, ('pcol', 'zgrid'), moves))  7.54 us
    all_to_all x2, waiting for transfers between devices, exchange(): lax.all_to_all(send, 'prow', 0, 0, tiled=True, axis_index_groups=[order])  3.82 us
    pallas_call x1, Pallas kernels, make_plan(): pl.pallas_call(functools.partial(plan_kernel, row_count, cols), out_shape...  2.54 us
    ppermute x7, waiting for transfers between devices, sibling_values(): found.append(lax.ppermute(value, ('pcol', 'zgrid'), moves))  2.17 us
    ppermute x3, waiting for transfers between devices, from_other_core(): return lax.ppermute(value, 'zgrid', [(0, 1), (1, 0)])  1.65 us
  transfers between devices with their start and end apart: 12, of which 8 were waited for; matrix products, arithmetic and copies ran while one was open for 1% of the time, Pallas kernels for 22%

profile of v9, /device:TPU:0, one launch (start us, length us, event | category | flops | bytes accessed | tf_op | source)
XLA Modules:
  0.0 54.9 jit_solution(6068487743761107192)
XLA Ops:
  0.6 0.9 %convolution_convert_fusion.1.refs_2_.refs_4_ = bf16[128,128]{1,0:T(8,128)(2,1)S(1)} fusion(bf16[1,1,1,2,128,128]{5,4,3,2,1,0:T(8,128)(2,1)} %param.12, bf16[1,1,1,2,128,128]{5,4,3,2,1,0:T(8,128)(2,1)} %param.14), kind=kOutput, calls=%fused_computation.1 | convolution fusion | flops 4210688 | bytes 98304 | tf_op jit(solution)/shard_map/dot_general | solution.py:329
  2.0 2.6 %collective-permute-start = (bf16[128,128]{1,0:T(8,128)(2,1)S(1)}, bf16[128,128]{1,0:T(8,128)(2,1)S(1)}, u32[]{:S(2)}, u32[]{:S(2)}) collective-permute-start(bf16[128,128]{1,0:T(8,128)(2,1)S(1)} %convolution_convert_fusion.1.refs_2_.refs_4_), channel_id=1, source_target_pairs={{0,2},{1,3},{2,0},{3,1},{4,6},{5,7},{6,4},{7,5},{8,10},{9,11},{10,... | collective-permute-start | bytes 98312 | tf_op jit(solution)/shard_map/ppermute | solution.py:35
  4.6 2.5 %shard_map.95 = (s32[8,128]{1,0:T(8,128)S(1)}, s32[8,128]{1,0:T(8,128)S(4)}, bf16[40,128,128]{2,1,0:T(8,128)(2,1)S(1)}) custom-call(s32[3,1,40]{2,1,0:T(1,128)} %bitcast.46, s32[3,1,40]{2,1,0:T(1,128)} %bitcast.47, s32[3]{0:T(128)} %bitcast.48, bf16[3,40,128,128]{3,2,1,0:T(8,128)(2,1)} %bitcast.38), custom_call_target="tpu_custom_call" | custom-call | tf_op jit(solution)/shard_map/pallas_call | solution.py:98
  7.2 1.0 %shard_map.96 = bf16[8,128,128]{2,1,0:T(8,128)(2,1)} custom-call(s32[8,128]{1,0:T(8,128)S(4)} %get-tuple-element.33.refs_0_, bf16[3,40,128,128]{3,2,1,0:T(8,128)(2,1)} %bitcast.39, bf16[128,128]{1,0:T(8,128)(2,1)S(1)} %convolution_convert_fusion.1.refs_2_.refs_4_, bf16[128,128]{1,0:T(8,128)(2,1)S(1)} %collective-permute-done.refs_3_.refs_5_, ...), custom_call_target="tpu_custom_call" | custom-call | tf_op jit(solution)/shard_map/pallas_call | solution.py:269
  8.2 6.2 %all-to-all-start = ((bf16[8,128,128]{2,1,0:T(8,128)(2,1)}), bf16[8,128,128]{2,1,0:T(8,128)(2,1)S(1)}, u32[]{:S(2)}, u32[]{:S(2)}) async-start(bf16[8,128,128]{2,1,0:T(8,128)(2,1)} %shard_map.96), calls=%async_computation | async-start | bytes 524288 | tf_op jit(solution)/shard_map/all_to_all | solution.py:340
  14.4 1.6 %collective-permute-start.4 = (bf16[128,128]{1,0:T(8,128)(2,1)S(1)}, bf16[128,128]{1,0:T(8,128)(2,1)S(1)}, u32[]{:S(2)}, u32[]{:S(2)}) collective-permute-start(bf16[128,128]{1,0:T(8,128)(2,1)S(1)} %convolution_convert_fusion.1.refs_2_.refs_4_), channel_id=1, source_target_pairs={{0,3},{1,2},{2,1},{3,0},{4,7},{5,6},{6,5},{7,4},{8,11},{9,10},{10,... | collective-permute-start | bytes 98312 | tf_op jit(solution)/shard_map/ppermute | solution.py:35
  16.1 1.1 %collective-permute-done.1.refs_1_ = s32[8,128]{1,0:T(8,128)S(1)} collective-permute-done((s32[8,128]{1,0:T(8,128)S(1)}, s32[8,128]{1,0:T(8,128)S(1)}, u32[]{:S(2)}, u32[]{:S(2)}) %collective-permute-start.1) | collective-permute-done | bytes 4128 | tf_op jit(solution)/shard_map/ppermute | solution.py:40
  17.2 0.6 %collective-permute-done.4.refs_7_ = bf16[128,128]{1,0:T(8,128)(2,1)S(1)} collective-permute-done((bf16[128,128]{1,0:T(8,128)(2,1)S(1)}, bf16[128,128]{1,0:T(8,128)(2,1)S(1)}, u32[]{:S(2)}, u32[]{:S(2)}) %collective-permute-start.4) | collective-permute-done | bytes 32800 | tf_op jit(solution)/shard_map/ppermute | solution.py:35
  17.8 2.1 %shard_map.97 = (f32[8,128,128]{2,1,0:T(8,128)S(1)}, bf16[40,128,128]{2,1,0:T(8,128)(2,1)S(1)}, s32[8,128]{1,0:T(8,128)S(4)}) custom-call(s32[8,128]{1,0:T(8,128)S(4)} %get-tuple-element.33.refs_0_, s32[8,128]{1,0:T(8,128)S(1)} %collective-permute-done.1.refs_1_, bf16[3,40,128,128]{3,2,1,0:T(8,128)(2,1)} %bitcast.40, ...), custom_call_target="tpu_custom_call" | custom-call | tf_op jit(solution)/shard_map/pallas_call | solution.py:269
  20.0 1.5 %all-to-all-done = bf16[8,128,128]{2,1,0:T(8,128)(2,1)S(1)} async-done(((bf16[8,128,128]{2,1,0:T(8,128)(2,1)}), bf16[8,128,128]{2,1,0:T(8,128)(2,1)S(1)}, u32[]{:S(2)}, u32[]{:S(2)}) %all-to-all-start) | async-done | bytes 262176 | tf_op jit(solution)/shard_map/all_to_all | solution.py:340
  21.7 0.9 %collective-permute-start.5 = (bf16[128,128]{1,0:T(8,128)(2,1)S(1)}, bf16[128,128]{1,0:T(8,128)(2,1)S(1)}, u32[]{:S(2)}, u32[]{:S(2)}) collective-permute-start(bf16[128,128]{1,0:T(8,128)(2,1)S(1)} %fusion.refs_4_.refs_5_.refs_8_), channel_id=1, source_target_pairs={{0,2},{1,3},{2,0},{3,1},{4,6},{5,7},{6,4},{7,5},{8,10},{9,11},{10,... | collective-permute-start | bytes 98312 | tf_op jit(solution)/shard_map/ppermute | solution.py:35
  22.6 1.2 %collective-permute-start.7 = (bf16[128,128]{1,0:T(8,128)(2,1)S(1)}, bf16[128,128]{1,0:T(8,128)(2,1)S(1)}, u32[]{:S(2)}, u32[]{:S(2)}) collective-permute-start(bf16[128,128]{1,0:T(8,128)(2,1)S(1)} %fusion.refs_4_.refs_5_.refs_8_), channel_id=1, source_target_pairs={{0,3},{1,2},{2,1},{3,0},{4,7},{5,6},{6,5},{7,4},{8,11},{9,10},{10,... | collective-permute-start | bytes 98312 | tf_op jit(solution)/shard_map/ppermute | solution.py:35
  23.9 1.3 %shard_map.98 = (f32[8,128,128]{2,1,0:T(8,128)S(1)}, bf16[40,128,128]{2,1,0:T(8,128)(2,1)S(1)}) custom-call(s32[8,128]{1,0:T(8,128)S(4)} %get-tuple-element.33.refs_0_, s32[8,128]{1,0:T(8,128)S(4)} %get-tuple-element.40.refs_1_, bf16[3,40,128,128]{3,2,1,0:T(8,128)(2,1)} %bitcast.41, bf16[3,40,128,128]{3,2,1,0:T(8,128)(2,1)} %collective-permute-done.2.refs_3_, ...), custom_call_target="tpu_custom_call" | custom-call | tf_op jit(solution)/shard_map/pallas_call | solution.py:269
  26.0 1.9 %shard_map.99 = bf16[8,64,128]{2,1,0:T(8,128)(2,1)} custom-call(s32[8,128]{1,0:T(8,128)S(4)} %get-tuple-element.33.refs_0_, s32[8,128]{1,0:T(8,128)S(4)} %get-tuple-element.40.refs_1_, bf16[3,40,128,128]{3,2,1,0:T(8,128)(2,1)} %bitcast.42, bf16[3,40,128,128]{3,2,1,0:T(8,128)(2,1)} %collective-permute-done.2.refs_3_, ...), custom_call_target="tpu_custom_call" | custom-call | tf_op jit(solution)/shard_map/pallas_call | solution.py:269
  27.9 5.1 %all-to-all-start.1 = ((bf16[8,64,128]{2,1,0:T(8,128)(2,1)}), bf16[8,64,128]{2,1,0:T(8,128)(2,1)S(1)}, u32[]{:S(2)}, u32[]{:S(2)}) async-start(bf16[8,64,128]{2,1,0:T(8,128)(2,1)} %shard_map.99), calls=%async_computation.1 | async-start | bytes 262144 | tf_op jit(solution)/shard_map/all_to_all | solution.py:340
  33.0 3.3 %shard_map.100 = (f32[8,128,128]{2,1,0:T(8,128)S(1)}, bf16[40,128,128]{2,1,0:T(8,128)(2,1)S(1)}) custom-call(s32[8,128]{1,0:T(8,128)S(4)} %get-tuple-element.33.refs_0_, s32[8,128]{1,0:T(8,128)S(4)} %get-tuple-element.40.refs_1_, bf16[3,40,128,128]{3,2,1,0:T(8,128)(2,1)} %bitcast.43, bf16[3,40,128,128]{3,2,1,0:T(8,128)(2,1)} %collective-permute-done.2.refs_3_, ...), custom_call_target="tpu_custom_call" | custom-call | tf_op jit(solution)/shard_map/pallas_call | solution.py:269
  36.2 2.3 %all-to-all-done.1.received = bf16[8,64,128]{2,1,0:T(8,128)(2,1)S(1)} async-done(((bf16[8,64,128]{2,1,0:T(8,128)(2,1)}), bf16[8,64,128]{2,1,0:T(8,128)(2,1)S(1)}, u32[]{:S(2)}, u32[]{:S(2)}) %all-to-all-start.1) | async-done | bytes 131104 | tf_op jit(solution)/shard_map/all_to_all | solution.py:340
  38.8 1.2 %collective-permute-start.8 = (bf16[64,128]{1,0:T(8,128)(2,1)S(1)}, bf16[64,128]{1,0:T(8,128)(2,1)S(1)}, u32[]{:S(2)}, u32[]{:S(2)}) collective-permute-start(bf16[64,128]{1,0:T(8,128)(2,1)S(1)} %shard_map.101.refs_4_.refs_5_.refs_0_), channel_id=1, source_target_pairs={{0,2},{1,3},{2,0},{3,1},{4,6},{5,7},{6,4},{7,5},{8,10},{9,11},{10,... | collective-permute-start | bytes 49160 | tf_op jit(solution)/shard_map/ppermute | solution.py:35
  40.0 1.8 %shard_map.102 = (f32[8,128,128]{2,1,0:T(8,128)S(1)}, bf16[40,128,128]{2,1,0:T(8,128)(2,1)S(1)}) custom-call(s32[8,128]{1,0:T(8,128)S(4)} %get-tuple-element.33.refs_0_, s32[8,128]{1,0:T(8,128)S(4)} %get-tuple-element.40.refs_1_, bf16[3,40,128,128]{3,2,1,0:T(8,128)(2,1)} %bitcast.44, bf16[3,40,128,128]{3,2,1,0:T(8,128)(2,1)} %collective-permute-done.2.refs_3_, ...), custom_call_target="tpu_custom_call" | custom-call | tf_op jit(solution)/shard_map/pallas_call | solution.py:269
  41.8 0.8 %collective-permute-done.8.refs_5_ = bf16[64,128]{1,0:T(8,128)(2,1)S(1)} collective-permute-done((bf16[64,128]{1,0:T(8,128)(2,1)S(1)}, bf16[64,128]{1,0:T(8,128)(2,1)S(1)}, u32[]{:S(2)}, u32[]{:S(2)}) %collective-permute-start.8) | collective-permute-done | bytes 16416 | tf_op jit(solution)/shard_map/ppermute | solution.py:35
  42.6 0.9 %shard_map.103 = bf16[8,64,128]{2,1,0:T(8,128)(2,1)S(1)} custom-call(s32[8,128]{1,0:T(8,128)S(4)} %get-tuple-element.33.refs_0_, s32[8,128]{1,0:T(8,128)S(4)} %get-tuple-element.40.refs_1_, bf16[3,40,128,128]{3,2,1,0:T(8,128)(2,1)} %bitcast.45, bf16[3,40,128,128]{3,2,1,0:T(8,128)(2,1)} %collective-permute-done.2.refs_3_, ...), custom_call_target="tpu_custom_call" | custom-call | tf_op jit(solution)/shard_map/pallas_call | solution.py:269
  43.5 9.0 %all_to_all.15.received = bf16[8,64,128]{2,1,0:T(8,128)(2,1)S(1)} all-to-all(bf16[8,64,128]{2,1,0:T(8,128)(2,1)S(1)} %shard_map.103), channel_id=1, replica_groups={{16,20,24,28,0,4,8,12},{17,21,25,29,1,5,9,13},{18,22,26,30,2,6,10,14},{..., dimensions={0} | all-to-all | bytes 262144 | tf_op jit(solution)/shard_map/all_to_all | solution.py:340
  52.9 0.6 %maximum_bitcast_fusion = bf16[1,1,1,2,128,128]{5,4,3,2,1,0:T(8,128)(2,1)} fusion(bf16[1,128,128]{2,1,0:T(8,128)(2,1)S(1)} %bitcast.31, bf16[1,128,128]{2,1,0:T(8,128)(2,1)S(1)} %bitcast.32), kind=kLoop, calls=%fused_computation.4 | loop fusion | flops 32768 | bytes 131072 | tf_op jit(solution)/shard_map/broadcast_in_dim | solution.py:409
  54.1 0.8 %shard_map.105 = bf16[1,1,2,128,128]{4,3,2,1,0:T(8,128)(2,1)} custom-call(bf16[2,64,128]{2,1,0:T(8,128)(2,1)S(1)} %shard_map.104.own, bf16[2,64,128]{2,1,0:T(8,128)(2,1)S(1)} %collective-permute-done.9.other), custom_call_target="tpu_custom_call" | custom-call | tf_op jit(solution)/shard_map/pallas_call | solution.py:319
  (24 shorter events, 2.7 us)
Async XLA Ops:
  1.5 16.3 %collective-permute-start.2 = (bf16[3,40,128,128]{3,2,1,0:T(8,128)(2,1)}, bf16[3,40,128,128]{3,2,1,0:T(8,128)(2,1)}, u32[]{:S(2)}, u32[]{:S(2)}) collective-permute-start(bf16[3,40,128,128]{3,2,1,0:T(8,128)(2,1)} %bitcast.37), channel_id=1, source_target_pairs={{0,1},{1,0},{2,3},{3,2},{4,5},{5,4},{6,7},{7,6},{8,9},{9,8},{10,11... | collective-permute-start | bytes 11796488 | tf_op jit(solution)/shard_map/ppermute | solution.py:40
  2.0 5.2 %collective-permute-start = (bf16[128,128]{1,0:T(8,128)(2,1)S(1)}, bf16[128,128]{1,0:T(8,128)(2,1)S(1)}, u32[]{:S(2)}, u32[]{:S(2)}) collective-permute-start(bf16[128,128]{1,0:T(8,128)(2,1)S(1)} %convolution_convert_fusion.1.refs_2_.refs_4_), channel_id=1, source_target_pairs={{0,2},{1,3},{2,0},{3,1},{4,6},{5,7},{6,4},{7,5},{8,10},{9,11},{10,... | collective-permute-start | bytes 98312 | tf_op jit(solution)/shard_map/ppermute | solution.py:35
  8.2 13.3 %all-to-all-start = ((bf16[8,128,128]{2,1,0:T(8,128)(2,1)}), bf16[8,128,128]{2,1,0:T(8,128)(2,1)S(1)}, u32[]{:S(2)}, u32[]{:S(2)}) async-start(bf16[8,128,128]{2,1,0:T(8,128)(2,1)} %shard_map.96), calls=%async_computation | async-start | bytes 524288 | tf_op jit(solution)/shard_map/all_to_all | solution.py:340
  14.4 7.1 %copy-start.2 = (bf16[1,1,1,2,128,128]{5,4,3,2,1,0:T(8,128)(2,1)S(1)}, bf16[1,1,1,2,128,128]{5,4,3,2,1,0:T(8,128)(2,1)}, u32[]{:S(2)}) copy-start(bf16[1,1,1,2,128,128]{5,4,3,2,1,0:T(8,128)(2,1)} %param.12) | copy-start | bytes 196612
  14.4 7.2 %copy-start.3 = (bf16[1,1,1,2,128,128]{5,4,3,2,1,0:T(8,128)(2,1)S(1)}, bf16[1,1,1,2,128,128]{5,4,3,2,1,0:T(8,128)(2,1)}, u32[]{:S(2)}) copy-start(bf16[1,1,1,2,128,128]{5,4,3,2,1,0:T(8,128)(2,1)} %param.14) | copy-start | bytes 196612
  14.4 2.8 %collective-permute-start.3 = (bf16[128,128]{1,0:T(8,128)(2,1)S(1)}, bf16[128,128]{1,0:T(8,128)(2,1)S(1)}, u32[]{:S(2)}, u32[]{:S(2)}) collective-permute-start(bf16[128,128]{1,0:T(8,128)(2,1)S(1)} %convolution_convert_fusion.1.refs_2_.refs_4_), channel_id=1, source_target_pairs={{0,1},{1,0},{2,3},{3,2},{4,5},{5,4},{6,7},{7,6},{8,9},{9,8},{10,11... | collective-permute-start | bytes 98312 | tf_op jit(solution)/shard_map/ppermute | solution.py:35
  14.4 3.4 %collective-permute-start.4 = (bf16[128,128]{1,0:T(8,128)(2,1)S(1)}, bf16[128,128]{1,0:T(8,128)(2,1)S(1)}, u32[]{:S(2)}, u32[]{:S(2)}) collective-permute-start(bf16[128,128]{1,0:T(8,128)(2,1)S(1)} %convolution_convert_fusion.1.refs_2_.refs_4_), channel_id=1, source_target_pairs={{0,3},{1,2},{2,1},{3,0},{4,7},{5,6},{6,5},{7,4},{8,11},{9,10},{10,... | collective-permute-start | bytes 98312 | tf_op jit(solution)/shard_map/ppermute | solution.py:35
  16.0 1.2 %collective-permute-start.1 = (s32[8,128]{1,0:T(8,128)S(1)}, s32[8,128]{1,0:T(8,128)S(1)}, u32[]{:S(2)}, u32[]{:S(2)}) collective-permute-start(s32[8,128]{1,0:T(8,128)S(1)} %get-tuple-element.37), channel_id=1, source_target_pairs={{0,1},{1,0},{2,3},{3,2},{4,5},{5,4},{6,7},{7,6},{8,9},{9,8},{10,11... | collective-permute-start | bytes 12296 | tf_op jit(solution)/shard_map/ppermute | solution.py:40
  21.7 3.9 %collective-permute-start.5 = (bf16[128,128]{1,0:T(8,128)(2,1)S(1)}, bf16[128,128]{1,0:T(8,128)(2,1)S(1)}, u32[]{:S(2)}, u32[]{:S(2)}) collective-permute-start(bf16[128,128]{1,0:T(8,128)(2,1)S(1)} %fusion.refs_4_.refs_5_.refs_8_), channel_id=1, source_target_pairs={{0,2},{1,3},{2,0},{3,1},{4,6},{5,7},{6,4},{7,5},{8,10},{9,11},{10,... | collective-permute-start | bytes 98312 | tf_op jit(solution)/shard_map/ppermute | solution.py:35
  22.6 3.0 %collective-permute-start.6 = (bf16[128,128]{1,0:T(8,128)(2,1)S(1)}, bf16[128,128]{1,0:T(8,128)(2,1)S(1)}, u32[]{:S(2)}, u32[]{:S(2)}) collective-permute-start(bf16[128,128]{1,0:T(8,128)(2,1)S(1)} %fusion.refs_4_.refs_5_.refs_8_), channel_id=1, source_target_pairs={{0,1},{1,0},{2,3},{3,2},{4,5},{5,4},{6,7},{7,6},{8,9},{9,8},{10,11... | collective-permute-start | bytes 98312 | tf_op jit(solution)/shard_map/ppermute | solution.py:35
  22.6 3.4 %collective-permute-start.7 = (bf16[128,128]{1,0:T(8,128)(2,1)S(1)}, bf16[128,128]{1,0:T(8,128)(2,1)S(1)}, u32[]{:S(2)}, u32[]{:S(2)}) collective-permute-start(bf16[128,128]{1,0:T(8,128)(2,1)S(1)} %fusion.refs_4_.refs_5_.refs_8_), channel_id=1, source_target_pairs={{0,3},{1,2},{2,1},{3,0},{4,7},{5,6},{6,5},{7,4},{8,11},{9,10},{10,... | collective-permute-start | bytes 98312 | tf_op jit(solution)/shard_map/ppermute | solution.py:35
  27.9 10.6 %all-to-all-start.1 = ((bf16[8,64,128]{2,1,0:T(8,128)(2,1)}), bf16[8,64,128]{2,1,0:T(8,128)(2,1)S(1)}, u32[]{:S(2)}, u32[]{:S(2)}) async-start(bf16[8,64,128]{2,1,0:T(8,128)(2,1)} %shard_map.99), calls=%async_computation.1 | async-start | bytes 262144 | tf_op jit(solution)/shard_map/all_to_all | solution.py:340
  33.0 5.6 %copy-start = (bf16[1,1,2,128,128]{4,3,2,1,0:T(8,128)(2,1)S(1)}, bf16[1,1,2,128,128]{4,3,2,1,0:T(8,128)(2,1)}, u32[]{:S(2)}) copy-start(bf16[1,1,2,128,128]{4,3,2,1,0:T(8,128)(2,1)} %param.13) | copy-start | bytes 196612
  33.0 5.6 %copy-start.1 = (bf16[1,1,2,128,128]{4,3,2,1,0:T(8,128)(2,1)S(1)}, bf16[1,1,2,128,128]{4,3,2,1,0:T(8,128)(2,1)}, u32[]{:S(2)}) copy-start(bf16[1,1,2,128,128]{4,3,2,1,0:T(8,128)(2,1)} %param.15) | copy-start | bytes 196612
  38.8 3.8 %collective-permute-start.8 = (bf16[64,128]{1,0:T(8,128)(2,1)S(1)}, bf16[64,128]{1,0:T(8,128)(2,1)S(1)}, u32[]{:S(2)}, u32[]{:S(2)}) collective-permute-start(bf16[64,128]{1,0:T(8,128)(2,1)S(1)} %shard_map.101.refs_4_.refs_5_.refs_0_), channel_id=1, source_target_pairs={{0,2},{1,3},{2,0},{3,1},{4,6},{5,7},{6,4},{7,5},{8,10},{9,11},{10,... | collective-permute-start | bytes 49160 | tf_op jit(solution)/shard_map/ppermute | solution.py:35
  52.8 1.2 %collective-permute-start.9 = (bf16[2,64,128]{2,1,0:T(8,128)(2,1)S(1)}, bf16[2,64,128]{2,1,0:T(8,128)(2,1)S(1)}, u32[]{:S(2)}, u32[]{:S(2)}) collective-permute-start(bf16[2,64,128]{2,1,0:T(8,128)(2,1)S(1)} %shard_map.104.own), channel_id=1, source_target_pairs={{0,1},{1,0},{2,3},{3,2},{4,5},{5,4},{6,7},{7,6},{8,9},{9,8},{10,11... | collective-permute-start | bytes 98312 | tf_op jit(solution)/shard_map/ppermute | solution.py:40
